TPU v7x, 32 devices: a whole 2x2x4 slice. The times are simulated.
32 devices in a mesh: region: 8 (over z, core), group: 4 (over y, x).
Axes of the slice: x: 2, y: 2, z: 4, core: 2. Of those that a mesh axis runs over, the one named last changes fastest.
Arguments:
- object_slab: float32 [4096, 2, 2048], P('region', None, 'group'), may hold values from -6 to 6
- probe: float32 [4, 2, 256, 256], replicated, may hold values from -6 to 6
- diffraction: float32 [128, 256, 256], P(('region', 'group')), may hold values from 0.25 to 16
- positions: int32 [128, 2], P(('region', 'group')), may hold values from 0 to 3840, as said below
- slot_counts: int32 [4, 8], P('group', 'region'), may hold values from 1 to 4, 20 in all within a row
Outputs:
- new_object: float32 [4096, 2, 2048], P('region', None, 'group')
- new_probe: float32 [4, 2, 256, 256], replicated
Inputs may be any that keep to these rules, and one draw needn't show every extreme that they name: `positions`: A slot of region index r has its row in r * 512 to min(r * 512 + 511, 3840); columns lie in 0 to 256; rows 0 and 3840 and columns 0 and 256 are each taken by some slot.
All inputs are finite; a program needn't handle non-finite values. No bound on the sum of `slot_counts` on one device may be relied on, other than what follows from the above.
Results may differ from a plain program's by a relative error of at most 0.0003.
Values sent between devices are 32-bit elements; how exact they have to be, the bound alone decides.
No kernel may reach another device: no remote copies, remote signals or barrier semaphores. Data moves between devices by JAX's collectives and lax.ppermute only.
A program may use at most 128 MiB of HBM per device.

v0:
```python
import math

import jax
import jax.numpy as jnp
from jax import lax
from jax.sharding import PartitionSpec as P

highest = lax.Precision.HIGHEST


def shifted(block, axis, distance):
    devices = range(lax.axis_size(axis))
    route = [(i - distance, i) for i in devices if i - distance in devices]
    return lax.ppermute(block, axis, route)


def tables(side):
    index = jnp.arange(side, dtype=jnp.int32)
    prod = index[:, None] * index[None, :] % side
    angle = prod.astype(jnp.float32) * (2.0 * math.pi / side)
    scale = 1.0 / math.sqrt(side)
    return (jnp.cos(angle) * scale, -jnp.sin(angle) * scale)


def transform(real_part, imag_part, cos_tab, sin_tab):
    left_r = jnp.einsum("jk,mkl->mjl", cos_tab, real_part, precision=highest) - jnp.einsum(
        "jk,mkl->mjl", sin_tab, imag_part, precision=highest
    )
    left_i = jnp.einsum("jk,mkl->mjl", cos_tab, imag_part, precision=highest) + jnp.einsum(
        "jk,mkl->mjl", sin_tab, real_part, precision=highest
    )
    out_r = jnp.einsum("mjk,kl->mjl", left_r, cos_tab, precision=highest) - jnp.einsum(
        "mjk,kl->mjl", left_i, sin_tab, precision=highest
    )
    out_i = jnp.einsum("mjk,kl->mjl", left_r, sin_tab, precision=highest) + jnp.einsum(
        "mjk,kl->mjl", left_i, cos_tab, precision=highest
    )
    return (out_r, out_i)


def on_device(object_slab, probe, diffraction, positions, slot_counts):
    side = probe.shape[2]
    slots = diffraction.shape[0]
    tile_rows = object_slab.shape[0]
    active_count = slot_counts[0, 0]
    cos_tab, sin_tab = tables(side)
    base = lax.axis_index("region") * tile_rows
    local_rows = positions[:, 0] - base
    shard_columns = positions[:, 1]
    obj = object_slab
    prb = probe
    peak = jnp.max(jnp.sum(prb[:, 0] * prb[:, 0] + prb[:, 1] * prb[:, 1], axis=0))
    below = shifted(obj, "region", -1)
    extended = jnp.concatenate([obj, below], axis=0)

    def cut(row, col):
        return lax.dynamic_slice(extended, (row, jnp.int32(0), col), (side, 2, side))

    windows = jax.vmap(cut)(local_rows, shard_columns)
    probe_r = prb[:, 0]
    probe_i = prb[:, 1]

    def single_position(position_entry, carry):
        wgrads, pgrad, cover = carry
        live = (position_entry < active_count).astype(jnp.float32)
        win = lax.dynamic_index_in_dim(windows, position_entry, 0, keepdims=False)
        observed_intensity = lax.dynamic_index_in_dim(
            diffraction, position_entry, 0, keepdims=False
        )
        win_r = win[:, 0, :]
        win_i = win[:, 1, :]
        exit_r = probe_r * win_r[None] - probe_i * win_i[None]
        exit_i = probe_r * win_i[None] + probe_i * win_r[None]
        far_r, far_i = transform(exit_r, exit_i, cos_tab, sin_tab)
        model_intensity = jnp.sum(far_r * far_r + far_i * far_i, axis=0)
        update_ratio = 1.0 - jnp.sqrt(observed_intensity) / jnp.sqrt(
            jnp.maximum(model_intensity, 1.0)
        )
        chi_r, chi_i = transform(
            far_r * update_ratio[None], far_i * update_ratio[None], cos_tab, -sin_tab
        )
        chi_r = chi_r * live
        chi_i = chi_i * live
        go_r = jnp.sum(probe_r * chi_r + probe_i * chi_i, axis=0)
        go_i = jnp.sum(probe_r * chi_i - probe_i * chi_r, axis=0)
        grad_win = jnp.stack([go_r, go_i], axis=1)
        wgrads = lax.dynamic_update_index_in_dim(wgrads, grad_win, position_entry, 0)
        gp = jnp.stack(
            [win_r[None] * chi_r + win_i[None] * chi_i, win_r[None] * chi_i - win_i[None] * chi_r],
            axis=1,
        )
        return (wgrads, pgrad + gp, cover + live * (win_r * win_r + win_i * win_i))

    start_carry = (
        jnp.zeros((slots, side, 2, side), jnp.float32),
        jnp.zeros(prb.shape, jnp.float32),
        jnp.zeros((side, side), jnp.float32),
    )
    wgrads, pgrad, cover = lax.fori_loop(0, slots, single_position, start_carry)
    pgrad, cover = lax.psum((pgrad, cover), ("region", "group"))

    def put(position_entry, scratch_array):
        row = local_rows[position_entry]
        col = shard_columns[position_entry]
        current = lax.dynamic_slice(scratch_array, (row, jnp.int32(0), col), (side, 2, side))
        return lax.dynamic_update_slice(
            scratch_array, current + wgrads[position_entry], (row, jnp.int32(0), col)
        )

    scratch_array = lax.fori_loop(0, slots, put, jnp.zeros(extended.shape, jnp.float32))
    tile_grad = scratch_array[:tile_rows]
    spill = scratch_array[tile_rows:]
    arrived = shifted(spill, "region", 1)
    tile_grad = tile_grad + arrived
    obj = obj - tile_grad / peak
    prb = prb - pgrad / (cover + 1e-06)[None, None]
    return (obj, prb)


def solution(mesh):
    placed = (
        P("region", None, "group"),
        P(),
        P(("region", "group"), None, None),
        P(("region", "group"), None),
        P("group", "region"),
    )
    return jax.shard_map(
        on_device,
        mesh=mesh,
        in_specs=placed,
        out_specs=(P("region", None, "group"), P()),
        check_vma=False,
    )
```

profile of v0, /device:TPU:0, one launch (start us, length us, event | category | flops | bytes accessed | tf_op | source)
XLA Modules:
  0.0 683.6 jit_solution(3246817226725037544)
XLA Ops:
  13.6 5.3 pad_maximum_fusion
  20.8 17.1 %while.35 = (s32[]{:T(128)}, f32[1024,2,512]{2,1,0:T(2,128)}, s32[4,3]{1,0:T(4,128)S(1)}, f32[4,256,2,256]{3,2,1,0:T(2,128)}, s32[]{:T(128)}) while((s32[]{:T(128)}, f32[1024,2,512]{2,1,0:T(2,128)}, s32[4,3]{1,0:T(4,128)S(1)}, f32[4,256,2,256]{3,2,1,0:T(2,128)}, s32[]{:T(128)}) %tuple.99), condition=%wide.while_cond, body=%wide.while_body.sunk | while | flops 2 | bytes 1050217 | solution.py:57
  21.4 3.7 bitcast_dynamic-update-slice_fusion.2
  25.6 3.7 bitcast_dynamic-update-slice_fusion.2
  29.9 3.7 bitcast_dynamic-update-slice_fusion.2
  34.2 3.7 bitcast_dynamic-update-slice_fusion.2
  39.8 249.9 %while.36 = (s32[]{:T(128)}, f32[4,256,2,256]{3,2,1,0:T(2,128)}, f32[4,2,256,256]{3,2,0,1:T(8,128)}, f32[256,256]{1,0:T(8,128)}, f32[4,256,2,256]{3,2,1,0:T(2,12...) while((s32[]{:T(128)}, f32[4,256,2,256]{3,2,1,0:T(2,128)}, ...), condition=%wide.region_4.5_spmd.clone.clone, body=%wide.region_0.4_spmd.clone.clone.sunk | while | flops 12915048448 | bytes 82838280 | solution.py:99
  41.4 2.7 fusion.223
  44.1 2.7 fusion.224
  46.8 2.7 fusion.220
  49.6 2.7 fusion.221
  52.3 3.2 fusion.222
  60.9 2.7 add_reduce_fusion.4
  64.6 2.8 fusion.230
  67.5 3.7 fusion.231
  77.5 3.7 fusion.229
  81.8 4.6 fusion.232
  89.1 5.4 add_bitcast_fusion.2
  94.5 3.2 maximum_add_fusion.2
  101.8 2.7 fusion.223
  104.5 2.7 fusion.224
  107.2 2.7 fusion.220
  110.0 2.7 fusion.221
  112.7 2.8 fusion.222
  120.9 2.7 add_reduce_fusion.4
  124.7 2.9 fusion.230
  127.5 3.7 fusion.231
  137.6 3.7 fusion.229
  141.9 4.8 fusion.232
  149.4 5.4 add_bitcast_fusion.2
  154.7 3.9 maximum_add_fusion.2
  163.4 2.7 fusion.223
  166.2 2.7 fusion.224
  168.9 2.7 fusion.220
  171.6 2.7 fusion.221
  174.4 2.9 fusion.222
  182.6 2.7 add_reduce_fusion.4
  186.4 3.1 fusion.230
  189.5 3.7 fusion.231
  199.5 3.7 fusion.229
  203.8 4.5 fusion.232
  211.1 5.4 add_bitcast_fusion.2
  216.4 3.9 maximum_add_fusion.2
  225.2 2.7 fusion.223
  227.9 2.7 fusion.224
  230.6 2.7 fusion.220
  233.4 2.7 fusion.221
  236.1 3.1 fusion.222
  248.3 2.8 fusion.230
  251.1 3.7 fusion.231
  261.2 3.7 fusion.229
  265.5 4.6 fusion.232
  272.8 5.4 add_bitcast_fusion.2
  278.1 3.9 maximum_add_fusion.2
  289.7 3.0 broadcast_in_dim.30
  292.7 207.1 %while.34 = (s32[]{:T(128)}, f32[1024,2,512]{2,1,0:T(2,128)}, s32[4]{0:T(128)S(1)}, s32[4]{0:T(128)S(1)}, f32[4,256,2,256]{3,2,1,0:T(2,128)}, /*index=5*/s32[]{:T(128)}, s32[]{:T(128)}, s32[]{:T(128)}, s32[]{:T(128)}) while((s32[]{:T(128)}, f32[1024,2,512]{2,1,0:T(2,128)}, s32[4]{0:T(128)S(1)}, s32[4]{0:T(128)S(1)}, ...), condition=%wide.region_6.7_spmd, body=%wide.region_5.6_spmd.sunk | while | flops 131080 | bytes 2621641 | solution.py:110
  299.5 45.0 %dynamic_update_slice.21 = f32[1024,2,512]{2,1,0:T(2,128)} dynamic-update-slice(f32[1024,2,512]{2,1,0:T(2,128)} %get-tuple-element.735, f32[256,2,256]{2,1,0:T(2,128)S(1)} %bitcast_add_fusion.2, s32[]{:T(128)S(6)} %select_n.175, s32[]{:T(128)} %constant.116.clone.1..sunk, s32[]{:T(128)S(6)} %select_n.176) | dynamic-update-slice | bytes 1048580 | tf_op jit(solution)/shard_map/while/body/eval_jaxpr/dynamic_update_slice | solution.py:106
  351.3 45.0 %dynamic_update_slice.21 = f32[1024,2,512]{2,1,0:T(2,128)} dynamic-update-slice(f32[1024,2,512]{2,1,0:T(2,128)} %get-tuple-element.735, f32[256,2,256]{2,1,0:T(2,128)S(1)} %bitcast_add_fusion.2, s32[]{:T(128)S(6)} %select_n.175, s32[]{:T(128)} %constant.116.clone.1..sunk, s32[]{:T(128)S(6)} %select_n.176) | dynamic-update-slice | bytes 1048580 | tf_op jit(solution)/shard_map/while/body/eval_jaxpr/dynamic_update_slice | solution.py:106
  403.1 45.0 %dynamic_update_slice.21 = f32[1024,2,512]{2,1,0:T(2,128)} dynamic-update-slice(f32[1024,2,512]{2,1,0:T(2,128)} %get-tuple-element.735, f32[256,2,256]{2,1,0:T(2,128)S(1)} %bitcast_add_fusion.2, s32[]{:T(128)S(6)} %select_n.175, s32[]{:T(128)} %constant.116.clone.1..sunk, s32[]{:T(128)S(6)} %select_n.176) | dynamic-update-slice | bytes 1048580 | tf_op jit(solution)/shard_map/while/body/eval_jaxpr/dynamic_update_slice | solution.py:106
  454.8 45.0 %dynamic_update_slice.21 = f32[1024,2,512]{2,1,0:T(2,128)} dynamic-update-slice(f32[1024,2,512]{2,1,0:T(2,128)} %get-tuple-element.735, f32[256,2,256]{2,1,0:T(2,128)S(1)} %bitcast_add_fusion.2, s32[]{:T(128)S(6)} %select_n.175, s32[]{:T(128)} %constant.116.clone.1..sunk, s32[]{:T(128)S(6)} %select_n.176) | dynamic-update-slice | bytes 1048580 | tf_op jit(solution)/shard_map/while/body/eval_jaxpr/dynamic_update_slice | solution.py:106
  499.8 3.8 slice.43
  510.2 156.2 %all-reduce.3.cloned.1.call-done = (f32[4,2,256,256]{3,2,1,0:T(8,128)}, f32[256,256]{1,0:T(8,128)}) async-done(((f32[4,2,256,256]{3,2,1,0:T(8,128)}, f32[256,256]{1,0:T(8,128)}), (f32[4,2,256,256]{3,2,1,0:T(8,128)}, f32[256,256]{1,0:T(8,128)})) %all-reduce.3.cloned.1.call-update) | async-done | bytes 2359312 | tf_op jit(solution)/shard_map/psum | solution.py:100
  667.4 3.4 divide_subtract_fusion.1
  671.6 4.9 divide_subtract_fusion
  (137 shorter events, 115.4 us)
Async XLA Ops:
  7.2 659.2 %all-reduce.3.cloned.1.call-start = ((), (), s32[]{:S(2)}) async-start(), calls=%async_computation | async-start | bytes 4718592 | tf_op jit(solution)/shard_map/psum | solution.py:100
  7.2 6.4 collective-permute-start
  9.7 3.9 copy-start.7
  76.5 1.0 copy-start.1
  81.8 4.6 copy-start.2
  81.8 7.3 %copy-start = (f32[4,256,256]{1,2,0:T(8,128)S(1)}, f32[4,256,256]{1,2,0:T(8,128)}, u32[]{:S(2)}) copy-start(f32[4,256,256]{1,2,0:T(8,128)} %fusion.231) | copy-start | bytes 3145732 | tf_op jit(solution)/shard_map/while
  94.5 3.2 copy-start.5
  136.6 1.0 copy-start.1
  141.9 4.8 copy-start.2
  141.9 7.5 %copy-start = (f32[4,256,256]{1,2,0:T(8,128)S(1)}, f32[4,256,256]{1,2,0:T(8,128)}, u32[]{:S(2)}) copy-start(f32[4,256,256]{1,2,0:T(8,128)} %fusion.231) | copy-start | bytes 3145732 | tf_op jit(solution)/shard_map/while
  154.7 3.9 copy-start.5
  198.5 1.0 copy-start.1
  203.8 4.6 copy-start.2
  203.8 7.2 %copy-start = (f32[4,256,256]{1,2,0:T(8,128)S(1)}, f32[4,256,256]{1,2,0:T(8,128)}, u32[]{:S(2)}) copy-start(f32[4,256,256]{1,2,0:T(8,128)} %fusion.231) | copy-start | bytes 3145732 | tf_op jit(solution)/shard_map/while
  216.4 3.9 copy-start.5
  260.1 1.0 copy-start.1
  265.5 4.6 copy-start.2
  265.5 7.3 %copy-start = (f32[4,256,256]{1,2,0:T(8,128)S(1)}, f32[4,256,256]{1,2,0:T(8,128)}, u32[]{:S(2)}) copy-start(f32[4,256,256]{1,2,0:T(8,128)} %fusion.231) | copy-start | bytes 3145732 | tf_op jit(solution)/shard_map/while
  278.1 3.9 copy-start.5
  499.8 6.4 copy-start.3
  503.6 167.2 %collective-permute-start.1 = (f32[512,2,512]{2,1,0:T(2,128)}, f32[512,2,512]{2,1,0:T(2,128)}, u32[]{:S(2)}, u32[]{:S(2)}) collective-permute-start(f32[512,2,512]{2,1,0:T(2,128)} %slice.43), channel_id=1, source_target_pairs={{0,4},{4,8},{8,12},{12,16},{16,20},{20,24},{24,28},{1,5},{5,9},{9,... | collective-permute-start | bytes 6291464 | tf_op jit(solution)/shard_map/ppermute | solution.py:14
  507.8 1.6 copy-start.6
  667.4 3.4 copy-start.4
  667.4 4.2 copy-start.8
Sparse Core Ops, SparseCore 0:
  507.9 158.4 all-reduce.2
where the time goes:
time: 689 us; the launch traced here: 684 us
  local copies, waits for them, and re-layouts  230 us (33%)
  matrix products  201 us (29%)
  waiting for transfers between devices  158 us (23%)
  other arithmetic  53.2 us (8%)
  loops' own time  23.3 us (3%)
  between operations  14.3 us (2%)
    dynamic_update_slice x4, local copies, waits for them, and re-layouts, put(): lax.dynamic_update_slice(scratch_array, current + wgrads[position_entry],...  180 us
    psum x1, waiting for transfers between devices, on_device(): pgrad, cover = lax.psum((pgrad, cover), ('region', 'group'))  156 us
    dot_general x8, matrix products, transform(): jnp.einsum('mjk,kl->mjl', left_i, sin_tab, precision=highest)  32.1 us
    dot_general x8, matrix products, transform(): jnp.einsum('mjk,kl->mjl', left_i, cos_tab, precision=highest)  29.2 us
    dot_general x8, matrix products, transform(): jnp.einsum('jk,mkl->mjl', sin_tab, real_part, precision=highest)  25.5 us
    dot_general x8, matrix products, transform(): jnp.einsum('mjk,kl->mjl', left_r, sin_tab, precision=highest)  25.3 us
    dot_general x8, matrix products, transform(): jnp.einsum('mjk,kl->mjl', left_r, cos_tab, precision=highest)  22.6 us
    dot_general x8, matrix products, transform(): jnp.einsum('jk,mkl->mjl', cos_tab, imag_part, precision=highest)  22.5 us
  transfers between devices with their start and end apart: 3, of which 2 were waited for; matrix products, arithmetic and copies ran while one was open for 1% of the time, Pallas kernels for 0%

commit v1 on v0

v1 whole, which is shorter than its diff:
```python
import functools
import math

import jax
import jax.numpy as jnp
import numpy as np
from jax import lax
from jax.experimental import pallas as pl
from jax.experimental.pallas import tpu as pltpu
from jax.sharding import PartitionSpec as P

LANES = 128
SUBLANES = 8
EPSILON = 1e-06


def shifted(block, axis, distance):
    devices = range(lax.axis_size(axis))
    route = [(i - distance, i) for i in devices if i - distance in devices]
    return lax.ppermute(block, axis, route)


def packed(block):
    rows, parts, columns = block.shape
    cut = block.reshape(rows, parts, columns // LANES, LANES).transpose(0, 2, 1, 3)
    return cut.reshape(rows * parts * columns // LANES, LANES)


def unpacked(block, shape):
    rows, parts, columns = shape
    cut = block.reshape(rows, columns // LANES, parts, LANES).transpose(0, 2, 1, 3)
    return cut.reshape(rows, parts, columns)


def tables(side):
    half = side // 2
    n, q = np.arange(half)[:, None], np.arange(half)[None, :]
    made = []
    for odd in range(2):
        angle = 2.0 * math.pi * ((n * (2 * q + odd)) % side) / side
        re, im = np.cos(angle) / math.sqrt(side), -np.sin(angle) / math.sqrt(side)
        made.append(np.block([[re, im], [-im, re]]))
    exact = np.stack([made[0], made[1], made[0].T, made[1].T]).astype(np.float32)
    high = exact.astype(jnp.bfloat16)
    low = (exact - high.astype(np.float32)).astype(jnp.bfloat16)
    return np.stack([high, low])


def parity_order(side):
    half = side // 2
    order = np.concatenate([np.arange(0, side, 2), np.arange(1, side, 2)])
    move = np.zeros((side, side), np.float32)
    move[order, np.arange(side)] = 1.0
    return np.stack([move, move.T]).astype(jnp.bfloat16)


def split(x):
    high = x.astype(jnp.bfloat16)
    low = (x - high.astype(jnp.float32)).astype(jnp.bfloat16)
    return high, low


def dot(a, b):
    return jnp.dot(a, b, preferred_element_type=jnp.float32)


def by_lanes(x, table_ref, index):
    high, low = split(x)
    t_high, t_low = table_ref[0, index], table_ref[1, index]
    return dot(
        jnp.concatenate([high, low, high], axis=1),
        jnp.concatenate([t_high, t_high, t_low], axis=0),
    )


def by_rows(x, table_ref, index):
    high, low = split(x)
    t_high, t_low = table_ref[0, index], table_ref[1, index]
    return dot(
        jnp.concatenate([t_high, t_high, t_low], axis=1),
        jnp.concatenate([high, low, high], axis=0),
    )


def moved(x, product):
    first, _ = split(x)
    rest = x - first.astype(jnp.float32)
    return product([first, *split(rest)])


def step_kernel(
    place_ref,
    count_ref,
    core_ref,
    object_hbm,
    halo_hbm,
    probe_ref,
    diffraction_ref,
    table_ref,
    order_ref,
    object_out,
    spill_out,
    mine_out,
    theirs_out,
    extended,
    gradient,
    sums,
    window,
    power,
    far,
    back,
    semaphores,
):
    modes, _, side, _ = probe_ref.shape
    half = side // 2
    tile_rows = object_hbm.shape[0]
    halo_rows = halo_hbm.shape[0]
    per_row = object_out.shape[0] // (object_out.shape[0] // SUBLANES)
    chunks = sums.shape[0]
    copies = [
        pltpu.make_async_copy(object_hbm, extended.at[pl.ds(0, tile_rows)], semaphores.at[0]),
        pltpu.make_async_copy(halo_hbm, extended.at[pl.ds(tile_rows, halo_rows)], semaphores.at[1]),
    ]
    for copy in copies:
        copy.start()
    gradient[...] = jnp.zeros_like(gradient)
    sums[...] = jnp.zeros_like(sums)
    total = jnp.zeros((side, side), jnp.float32)
    for mode in range(modes):
        total = total + probe_ref[mode, 0] * probe_ref[mode, 0] + probe_ref[mode, 1] * probe_ref[mode, 1]
    power[...] = total
    scale = 1.0 / jnp.max(total)
    for copy in copies:
        copy.wait()
    lane = lax.broadcasted_iota(jnp.int32, (side, LANES), 1)
    blocks = side // LANES

    def slot(index, carry):
        row = place_ref[index, 0]
        column = place_ref[index, 1]
        first = column // LANES
        shift = column - first * LANES
        back_shift = lax.rem(LANES - shift, LANES)
        last = per_row // 2 - 1

        def rows_of(block, part):
            at = row * per_row + jnp.minimum(first + block, last) * 2 + part
            return pl.ds(at, side, stride=per_row)

        for part in range(2):
            rolled = [
                pltpu.roll(extended[rows_of(block, part), :], back_shift, 1)
                for block in range(blocks + 1)
            ]
            for block in range(blocks):
                window[part, :, pl.ds(block * LANES, LANES)] = jnp.where(
                    lane < LANES - shift, rolled[block], rolled[block + 1]
                )

        def forward(mode, carry):
            w_r, w_i = window[0], window[1]
            p_r, p_i = probe_ref[mode, 0], probe_ref[mode, 1]
            e_r = p_r * w_r - p_i * w_i
            e_i = p_r * w_i + p_i * w_r
            plus = jnp.concatenate([e_r[:, :half] + e_r[:, half:], e_i[:, :half] + e_i[:, half:]], axis=1)
            minus = jnp.concatenate([e_r[:, :half] - e_r[:, half:], e_i[:, :half] - e_i[:, half:]], axis=1)
            even = by_lanes(plus, table_ref, 0)
            odd = by_lanes(minus, table_ref, 1)
            real = jnp.concatenate([even[:, :half], odd[:, :half]], axis=1)
            imag = jnp.concatenate([even[:, half:], odd[:, half:]], axis=1)
            plus = jnp.concatenate([real[:half] + real[half:], imag[:half] + imag[half:]], axis=0)
            minus = jnp.concatenate([real[:half] - real[half:], imag[:half] - imag[half:]], axis=0)
            far[mode, 0] = by_rows(plus, table_ref, 2)
            far[mode, 1] = by_rows(minus, table_ref, 3)
            return carry

        lax.fori_loop(0, modes, forward, 0)

        move = order_ref[0]
        measured = moved(diffraction_ref[index], lambda terms: dot(
            jnp.concatenate([order_ref[1]] * 3, axis=1), jnp.concatenate(terms, axis=0)
        ))
        measured = moved(measured, lambda terms: dot(
            jnp.concatenate(terms, axis=1), jnp.concatenate([move] * 3, axis=0)
        ))
        for odd in range(2):
            seen = measured[odd * half : (odd + 1) * half]
            intensity = jnp.zeros((half, side), jnp.float32)
            for mode in range(modes):
                re, im = far[mode, odd, pl.ds(0, half), :], far[mode, odd, pl.ds(half, half), :]
                intensity = intensity + re * re + im * im
            ratio = seen * lax.rsqrt(seen * jnp.maximum(intensity, 1.0))
            for mode in range(modes):
                far[mode, odd, pl.ds(0, half), :] = far[mode, odd, pl.ds(0, half), :] * ratio
                far[mode, odd, pl.ds(half, half), :] = far[mode, odd, pl.ds(half, half), :] * ratio

        back[0] = power[...] * window[0]
        back[1] = power[...] * window[1]

        def backward(mode, carry):
            even = by_rows(far[mode, 0], table_ref, 0)
            odd = by_rows(far[mode, 1], table_ref, 1)
            plus, minus = even + odd, even - odd
            real = jnp.concatenate([plus[:half], minus[:half]], axis=0)
            imag = jnp.concatenate([plus[half:], minus[half:]], axis=0)
            even = by_lanes(jnp.concatenate([real[:, :half], imag[:, :half]], axis=1), table_ref, 2)
            odd = by_lanes(jnp.concatenate([real[:, half:], imag[:, half:]], axis=1), table_ref, 3)
            plus, minus = even + odd, even - odd
            c_r = jnp.concatenate([plus[:, :half], minus[:, :half]], axis=1)
            c_i = jnp.concatenate([plus[:, half:], minus[:, half:]], axis=1)
            p_r, p_i = probe_ref[mode, 0], probe_ref[mode, 1]
            back[0] = back[0] - (p_r * c_r + p_i * c_i)
            back[1] = back[1] - (p_r * c_i - p_i * c_r)
            w_r, w_i = window[0], window[1]
            by_chunk = (chunks, SUBLANES, side)
            sums[:, 2 * mode] += (w_r * c_r + w_i * c_i).reshape(by_chunk)
            sums[:, 2 * mode + 1] += (w_r * c_i - w_i * c_r).reshape(by_chunk)
            return carry

        lax.fori_loop(0, modes, backward, 0)
        w_r, w_i = window[0], window[1]
        sums[:, 2 * modes] += (w_r * w_r + w_i * w_i).reshape(chunks, SUBLANES, side)

        for part in range(2):
            rolled = [
                pltpu.roll(back[part, :, pl.ds(block * LANES, LANES)], shift, 1) for block in range(blocks)
            ]
            zero = jnp.zeros((side, LANES), jnp.float32)
            for block in range(blocks + 1):
                here = rolled[block] if block < blocks else zero
                before = rolled[block - 1] if block else zero
                at = rows_of(block, part)
                gradient[at, :] = gradient[at, :] + jnp.where(lane >= shift, here, before)
        return carry

    lax.fori_loop(0, count_ref[0, 0], slot, 0)
    object_out[...] = extended[pl.ds(0, tile_rows), :] - gradient[pl.ds(0, tile_rows), :] * scale
    spill_out[...] = gradient[pl.ds(tile_rows, halo_rows), :] * scale
    share = chunks // 2
    core = core_ref[0, 0]
    mine_out[...] = sums[pl.ds(core * share, share)]
    theirs_out[...] = sums[pl.ds((1 - core) * share, share)]


def gradient_step(place, count, core, tile, halo, probe, diffraction):
    modes, parts, side, _ = probe.shape
    planes = parts * modes + 1
    chunks = side // SUBLANES
    f32 = jnp.float32
    smem = pl.BlockSpec(memory_space=pltpu.SMEM)
    vmem = pl.BlockSpec(memory_space=pltpu.VMEM)
    anywhere = pl.BlockSpec(memory_space=pl.ANY)
    share = jax.ShapeDtypeStruct((chunks // 2, planes, SUBLANES, side), f32)
    products = 3 * 16 * modes * diffraction.shape[0] * side**3
    return pl.pallas_call(
        step_kernel,
        out_shape=(
            jax.ShapeDtypeStruct(tile.shape, f32),
            jax.ShapeDtypeStruct(halo.shape, f32),
            share,
            share,
        ),
        in_specs=[smem, smem, smem, anywhere, anywhere, vmem, vmem, vmem, vmem],
        out_specs=(vmem, vmem, vmem, vmem),
        scratch_shapes=[
            pltpu.VMEM((tile.shape[0] + halo.shape[0], LANES), f32),
            pltpu.VMEM((tile.shape[0] + halo.shape[0], LANES), f32),
            pltpu.VMEM((chunks, planes, SUBLANES, side), f32),
            pltpu.VMEM((2, side, side), f32),
            pltpu.VMEM((side, side), f32),
            pltpu.VMEM((modes, 2, side, side), f32),
            pltpu.VMEM((2, side, side), f32),
            pltpu.SemaphoreType.DMA((2,)),
        ],
        compiler_params=pltpu.CompilerParams(vmem_limit_bytes=48 * 1024 * 1024),
        cost_estimate=pl.CostEstimate(flops=2 * products, bytes_accessed=16 << 20, transcendentals=0),
        name="gradient_step",
    )(place, count, core, tile, halo, probe, diffraction, jnp.asarray(tables(side)), jnp.asarray(parity_order(side)))


def on_device(object_slab, probe, diffraction, positions, slot_counts):
    modes, parts, side, _ = probe.shape
    tile_rows, _, columns = object_slab.shape
    regions, groups = lax.axis_size("region"), lax.axis_size("group")
    region, group = lax.axis_index("region"), lax.axis_index("group")
    core, layer = region % 2, region // 2
    layers = regions // 2
    per_row = parts * columns // LANES
    assert per_row == SUBLANES
    tile = packed(object_slab)
    halo = shifted(tile[: side * per_row], "region", -1)
    place = positions - jnp.stack([region * tile_rows, jnp.zeros_like(region)])[None, :].astype(jnp.int32)
    core_entry = core.astype(jnp.int32).reshape(1, 1)
    new_tile, spill, mine, theirs = gradient_step(place, slot_counts, core_entry, tile, halo, probe, diffraction)

    partner = [(i, i ^ 1) for i in range(regions)]
    arrived = shifted(spill, "region", 1)
    mine = mine + lax.ppermute(theirs, "region", partner)
    same_core = [[2 * i + c for i in range(layers)] for c in range(2)]
    planes = parts * modes + 1
    mine = lax.all_to_all(mine, "group", 0, 0, tiled=True)
    mine = jnp.sum(mine.reshape(groups, -1, planes, SUBLANES, side), axis=0)
    rows = mine.shape[0] * SUBLANES // layers
    mine = mine.reshape(-1, planes, SUBLANES // min(rows, SUBLANES), min(rows, SUBLANES), side)
    mine = mine.transpose(0, 2, 1, 3, 4).reshape(layers, planes, rows, side)
    mine = lax.all_to_all(mine, "region", 0, 0, axis_index_groups=same_core, tiled=True)
    mine = jnp.sum(mine.reshape(layers, planes, rows, side), axis=0)
    start = core * (side // 2) + group * (rows * layers) + layer * rows
    old = lax.dynamic_slice(probe.reshape(planes - 1, side, side), (0, start, 0), (planes - 1, rows, side))
    fresh = (EPSILON * old + mine[:-1]) / (mine[-1:] + EPSILON)
    fresh = lax.all_gather(fresh, "region", axis_index_groups=same_core)
    fresh = lax.all_gather(fresh, "group")
    other = lax.ppermute(fresh, "region", partner)
    whole = jnp.where(core == 0, jnp.stack([fresh, other]), jnp.stack([other, fresh]))
    new_probe = whole.transpose(3, 0, 1, 2, 4, 5).reshape(probe.shape)

    overlap = spill.shape[0]
    new_tile = lax.dynamic_update_slice(new_tile, new_tile[:overlap] - arrived, (0, 0))
    return (unpacked(new_tile, object_slab.shape), new_probe)


def solution(mesh):
    placed = (
        P("region", None, "group"),
        P(),
        P(("region", "group"), None, None),
        P(("region", "group"), None),
        P("group", "region"),
    )
    return jax.shard_map(
        on_device,
        mesh=mesh,
        in_specs=placed,
        out_specs=(P("region", None, "group"), P()),
        check_vma=False,
    )
```

time: 689 us -> 154 us (0.22)
  local copies, waits for them, and re-layouts: 230 us -> 4.65 us
  matrix products: 201 us -> 0 us
  waiting for transfers between devices: 158 us -> 38.8 us
  blocking collectives: 0 us -> 56.6 us
  other arithmetic: 53.2 us -> 6.19 us
  loops' own time: 23.3 us -> 0 us
  Pallas kernels: 0 us -> 20.8 us
  starting transfers between devices: 3.94 us -> 11.7 us
    dot_general x64 -> x0, matrix products: 201 us -> none  [the longest x8 32.1 us: transform(): jnp.einsum('mjk,kl->mjl', left_i, sin_tab, precision=highest)]
    dynamic_update_slice x4 -> x0, local copies, waits for them, and re-layouts: 180 us -> none  [put(): lax.dynamic_update_slice(scratch_array, current + wgrads[position_entry],...]
    psum x1 -> x0, waiting for transfers between devices: 156 us -> none  [on_device(): pgrad, cover = lax.psum((pgrad, cover), ('region', 'group'))]
    all_to_all x0 -> x1, blocking collectives: none -> 42 us  [on_device(): mine = lax.all_to_all(mine, 'group', 0, 0, tiled=True)]
    add x13 -> x1, other arithmetic: 29.2 us -> 0.15 us  [on_device(): mine = mine + lax.ppermute(theirs, 'region', partner)]
    all_gather x0 -> x1, waiting for transfers between devices: none -> 24.5 us  [on_device(): fresh = lax.all_gather(fresh, 'group')]
    another operation x3 -> x0, loops' own time: 23.3 us -> none  [the longest x1 14.6 us: on_device(): lax.fori_loop(0, slots, put, jnp.zeros(extended.shape, jnp.float32))]
    pallas_call x0 -> x1, Pallas kernels: none -> 20.8 us  [gradient_step(): pl.pallas_call(step_kernel, out_shape=(jax.ShapeDtypeStruct(tile.shape, f...]
  transfers between devices with their start and end apart: 3 -> 6, of which waited for: 2 -> 5; matrix products, arithmetic and copies ran while one was open for 1% -> 2% of each run, Pallas kernels for 0% -> 0%
where the time goes in v1:
time: 154 us; the launch traced here: 153 us
  blocking collectives  56.6 us (37%)
  waiting for transfers between devices  38.8 us (25%)
  Pallas kernels  20.8 us (14%)
  between operations  14.8 us (10%)
  starting transfers between devices  11.7 us (8%)
  other arithmetic  6.19 us (4%)
  local copies, waits for them, and re-layouts  4.65 us (3%)
    all_to_all x1, blocking collectives, on_device(): mine = lax.all_to_all(mine, 'group', 0, 0, tiled=True)  42 us
    all_gather x1, waiting for transfers between devices, on_device(): fresh = lax.all_gather(fresh, 'group')  24.5 us
    pallas_call x1, Pallas kernels, gradient_step(): pl.pallas_call(step_kernel, out_shape=(jax.ShapeDtypeStruct(tile.shape, f...  20.8 us
    all_gather x1, blocking collectives, on_device(): fresh = lax.all_gather(fresh, 'region', axis_index_groups=same_core)  14.5 us
    all_to_all x1, waiting for transfers between devices, on_device(): lax.all_to_all(mine, 'region', 0, 0, axis_index_groups=same_core, tiled=T...  8.62 us
    ppermute x1, starting transfers between devices, on_device(): mine = mine + lax.ppermute(theirs, 'region', partner)  5.23 us
    all_to_all x1, starting transfers between devices, on_device(): lax.all_to_all(mine, 'region', 0, 0, axis_index_groups=same_core, tiled=T...  3.8 us
  transfers between devices with their start and end apart: 6, of which 5 were waited for; matrix products, arithmetic and copies ran while one was open for 2% of the time, Pallas kernels for 0%

profile of v1, /device:TPU:0, one launch (start us, length us, event | category | flops | bytes accessed | tf_op | source)
XLA Modules:
  0.0 153.5 jit_solution(632038610403356972)
XLA Ops:
  7.2 0.0 copy-start.2
  7.2 0.0 copy-start.4
  7.2 0.0 copy-start
  7.2 1.7 %slice.20 = f32[256,4,2,128]{3,2,1,0:T(2,128)S(1)} slice(f32[512,4,2,128]{3,2,1,0:T(2,128)} %bitcast.31), slice={[0:256], [0:4], [0:2], [0:128]} | slice | bytes 2097152 | tf_op jit(solution)/shard_map/slice | solution.py:291
  8.9 1.3 collective-permute-start
  10.2 0.0 copy-done.4
  10.2 0.1 copy.23
  11.0 0.1 pad_add_fusion
  11.0 2.4 %collective-permute-done.halo_hbm = f32[2048,128]{1,0:T(8,128)S(1)} collective-permute-done((f32[2048,128]{1,0:T(8,128)S(1)}, f32[2048,128]{1,0:T(8,128)S(1)}, u32[]{:S(2)}, u32[]{:S(2)}) %collective-permute-start) | collective-permute-done | bytes 1048608 | tf_op jit(solution)/shard_map/ppermute | solution.py:20
  13.4 0.0 copy-done.2
  13.4 0.0 copy-done
  13.4 0.0 copy-start.1
  13.4 1.2 copy-done.1
  14.7 20.8 %gradient_step.1 = (f32[4096,128]{1,0:T(8,128)}, f32[2048,128]{1,0:T(8,128)S(1)}, f32[16,9,8,256]{3,2,1,0:T(8,128)S(1)}, f32[16,9,8,256]{3,2,1,0:T(8,128)}) custom-call(s32[4,2]{1,0:T(4,128)S(1)} %broadcast_subtract_fusion.place_ref, s32[1,1]{1,0:T(1,128)S(6)} %copy.28.count_ref, s32[1,1]{1,0:T(1,128)} %bitcast.1.core_ref, f32[4096,128]{1,0:T(8,128)} %bitcast.32, ...), custom_call_target="tpu_custom_call" | custom-call | flops 25769803776 | bytes 16777216 | tf_op jit(solution)/shard_map/gradient_step/pallas_call | solution.py:255
  35.5 5.2 %collective-permute-start.2 = (f32[16,9,8,256]{3,2,1,0:T(8,128)}, f32[16,9,8,256]{3,2,1,0:T(8,128)S(1)}, u32[]{:S(2)}, u32[]{:S(2)}) collective-permute-start(f32[16,9,8,256]{3,2,1,0:T(8,128)} %get-tuple-element.9), channel_id=1, source_target_pairs={{0,4},{4,0},{8,12},{12,8},{16,20},{20,16},{24,28},{28,24},{1,5},{5... | collective-permute-start | bytes 3538952 | tf_op jit(solution)/shard_map/ppermute | solution.py:298
  40.7 2.7 %collective-permute-done.2 = f32[16,9,8,256]{3,2,1,0:T(8,128)S(1)} collective-permute-done((f32[16,9,8,256]{3,2,1,0:T(8,128)}, f32[16,9,8,256]{3,2,1,0:T(8,128)S(1)}, u32[]{:S(2)}, u32[]{:S(2)}) %collective-permute-start.2) | collective-permute-done | bytes 1179680 | tf_op jit(solution)/shard_map/ppermute | solution.py:298
  43.4 0.2 add.30
  43.5 42.0 %all_to_all.10 = f32[16,9,8,256]{3,2,1,0:T(8,128)S(1)} all-to-all(f32[16,9,8,256]{3,2,1,0:T(8,128)S(1)} %add.30), channel_id=1, replica_groups=mesh['region'=8,'group'=4] {'group'}, dimensions={0} | all-to-all | bytes 2359296 | tf_op jit(solution)/shard_map/all_to_all | solution.py:301
  85.6 0.8 reduce_sum.18
  86.4 3.8 %all-to-all-start.1 = ((f32[4,9,8,256]{3,2,1,0:T(8,128)}), f32[4,9,8,256]{3,2,1,0:T(8,128)S(1)}, u32[]{:S(2)}, u32[]{:S(2)}) async-start(f32[4,9,8,256]{3,2,1,0:T(8,128)} %reduce_sum.18), calls=%async_computation.1 | async-start | bytes 589824 | tf_op jit(solution)/shard_map/all_to_all | solution.py:306
  90.2 0.0 all-gather.4.cloned.1.call-start
  90.2 8.6 %all-to-all-done.1 = f32[4,9,8,256]{3,2,1,0:T(8,128)S(1)} async-done(((f32[4,9,8,256]{3,2,1,0:T(8,128)}), f32[4,9,8,256]{3,2,1,0:T(8,128)S(1)}, u32[]{:S(2)}, u32[]{:S(2)}) %all-to-all-start.1) | async-done | bytes 294944 | tf_op jit(solution)/shard_map/all_to_all | solution.py:306
  98.8 0.9 fusion.1
  99.7 14.5 %all-gather = f32[32,8,256]{2,1,0:T(8,128)} all-gather(f32[8,8,256]{2,1,0:T(8,128)S(1)} %fusion.1), channel_id=2, replica_groups={{0,8,16,24},{4,12,20,28},{1,9,17,25},{5,13,21,29},{2,10,18,26},{6,14,22..., dimensions={0}, use_global_device_ids=true | all-gather | bytes 327680 | tf_op jit(solution)/shard_map/all_gather | solution.py:311
  114.2 0.0 all-gather.4.cloned.1.call-update
  114.3 1.4 collective-permute-start.1
  115.6 24.5 %all-gather.4.cloned.1.call-done = f32[16,8,8,256]{3,2,1,0:T(8,128)} async-done(((f32[4,8,8,256]{3,2,1,0:T(8,128)}), f32[16,8,8,256]{3,2,1,0:T(8,128)}) %all-gather.4.cloned.1.call-update) | async-done | bytes 1048592 | tf_op jit(solution)/shard_map/all_gather | solution.py:312
  140.1 0.0 copy-start.3
  140.1 0.0 collective-permute-start.3
  140.1 0.0 collective-permute-done.1
  140.1 2.4 %subtract_dynamic-update-slice_fusion = f32[4096,128]{1,0:T(8,128)} fusion(f32[4096,128]{1,0:T(8,128)} %get-tuple-element.6, f32[2048,128]{1,0:T(8,128)S(1)} %collective-permute-done.1), kind=kLoop, calls=%fused_computation.2 | loop fusion | flops 262144 | bytes 3145728 | tf_op jit(solution)/shard_map/dynamic_update_slice | solution.py:318
  142.5 0.6 collective-permute-done.3
  143.1 0.0 copy-done.3
  143.1 1.9 %fusion = f32[8,2,4,4,8,256]{5,4,0,3,2,1:T(8,128)S(1)} fusion(f32[1,4,4,8,8,256]{5,4,3,2,1,0:T(8,128)} %bitcast.16, f32[1,4,4,8,8,256]{5,4,3,2,1,0:T(8,128)S(1)} %bitcast.27, pred[]{:T(512)S(6)} %eq.5), kind=kLoop, calls=%fused_computation.1 | loop fusion | flops 1572864 | bytes 4194305 | tf_op jit(solution)/shard_map/transpose | solution.py:315
  145.0 1.6 %copy.26 = f32[8,2,4,4,8,256]{5,4,3,2,1,0:T(8,128)} copy(f32[8,2,4,4,8,256]{5,4,0,3,2,1:T(8,128)S(1)} %fusion) | data formatting | bytes 4194304 | tf_op jit(solution)/shard_map/transpose | solution.py:315
  (3 shorter events, 0.0 us)
Async XLA Ops:
  7.2 6.3 %copy-start.2 = (bf16[2,256,256]{2,1,0:T(8,128)(2,1)S(1)}, bf16[2,256,256]{2,1,0:T(8,128)(2,1)}, u32[]{:S(2)}) copy-start(bf16[2,256,256]{2,1,0:T(8,128)(2,1)} %constant.56.clone.order_ref) | copy-start | bytes 786436
  7.2 3.0 %copy-start.4 = (s32[4,2]{0,1:T(2,128)S(1)}, s32[4,2]{0,1:T(2,128)}, u32[]{:S(2)}) copy-start(s32[4,2]{0,1:T(2,128)} %param.10) | copy-start | bytes 100
  7.2 6.3 %copy-start = (f32[4,256,256]{2,1,0:T(8,128)S(1)}, f32[4,256,256]{2,1,0:T(8,128)}, u32[]{:S(2)}) copy-start(f32[4,256,256]{2,1,0:T(8,128)} %diffraction_ref.1) | copy-start | bytes 3145732
  8.9 4.6 %collective-permute-start = (f32[2048,128]{1,0:T(8,128)S(1)}, f32[2048,128]{1,0:T(8,128)S(1)}, u32[]{:S(2)}, u32[]{:S(2)}) collective-permute-start(f32[2048,128]{1,0:T(8,128)S(1)} %bitcast.29), channel_id=1, source_target_pairs={{4,0},{8,4},{12,8},{16,12},{20,16},{24,20},{28,24},{5,1},{9,5},{13... | collective-permute-start | bytes 3145736 | tf_op jit(solution)/shard_map/ppermute | solution.py:20
  13.4 1.2 copy-start.1
  35.5 7.9 %collective-permute-start.2 = (f32[16,9,8,256]{3,2,1,0:T(8,128)}, f32[16,9,8,256]{3,2,1,0:T(8,128)S(1)}, u32[]{:S(2)}, u32[]{:S(2)}) collective-permute-start(f32[16,9,8,256]{3,2,1,0:T(8,128)} %get-tuple-element.9), channel_id=1, source_target_pairs={{0,4},{4,0},{8,12},{12,8},{16,20},{20,16},{24,28},{28,24},{1,5},{5... | collective-permute-start | bytes 3538952 | tf_op jit(solution)/shard_map/ppermute | solution.py:298
  86.4 12.4 %all-to-all-start.1 = ((f32[4,9,8,256]{3,2,1,0:T(8,128)}), f32[4,9,8,256]{3,2,1,0:T(8,128)S(1)}, u32[]{:S(2)}, u32[]{:S(2)}) async-start(f32[4,9,8,256]{3,2,1,0:T(8,128)} %reduce_sum.18), calls=%async_computation.1 | async-start | bytes 589824 | tf_op jit(solution)/shard_map/all_to_all | solution.py:306
  90.2 49.9 %all-gather.4.cloned.1.call-start = ((), (), s32[]{:S(2)}) async-start(), calls=%async_computation.2 | async-start | bytes 1310720 | tf_op jit(solution)/shard_map/all_gather | solution.py:312
  114.3 25.8 %collective-permute-start.1 = (f32[2048,128]{1,0:T(8,128)S(1)}, f32[2048,128]{1,0:T(8,128)S(1)}, u32[]{:S(2)}, u32[]{:S(2)}) collective-permute-start(f32[2048,128]{1,0:T(8,128)S(1)} %get-tuple-element.7), channel_id=1, source_target_pairs={{0,4},{4,8},{8,12},{12,16},{16,20},{20,24},{24,28},{1,5},{5,9},{9,... | collective-permute-start | bytes 3145736 | tf_op jit(solution)/shard_map/ppermute | solution.py:20
  140.1 3.0 %copy-start.3 = (f32[16,8,8,256]{3,2,1,0:T(8,128)S(1)}, f32[16,8,8,256]{3,2,1,0:T(8,128)}, u32[]{:S(2)}) copy-start(f32[16,8,8,256]{3,2,1,0:T(8,128)} %all-gather.4.cloned.1.call-done) | copy-start | bytes 3145732
  140.1 3.0 %collective-permute-start.3 = (f32[4,4,8,8,256]{4,3,2,1,0:T(8,128)}, f32[4,4,8,8,256]{4,3,2,1,0:T(8,128)}, u32[]{:S(2)}, u32[]{:S(2)}) collective-permute-start(f32[4,4,8,8,256]{4,3,2,1,0:T(8,128)} %bitcast.26), channel_id=1, source_target_pairs={{0,4},{4,0},{8,12},{12,8},{16,20},{20,16},{24,28},{28,24},{1,5},{5... | collective-permute-start | bytes 3145736 | tf_op jit(solution)/shard_map/ppermute | solution.py:313
Sparse Core Ops, SparseCore 0:
  114.4 25.6 all-gather.3

commit v2 on v1

--- a/solution.py
+++ b/solution.py
@@ -91,7 +91,7 @@
 def step_kernel(
     place_ref,
     count_ref,
-    core_ref,
+    here_ref,
     object_hbm,
     halo_hbm,
     probe_ref,
@@ -101,7 +101,8 @@
     object_out,
     spill_out,
     mine_out,
-    theirs_out,
+    near_out,
+    far_out,
     extended,
     gradient,
     sums,
@@ -157,7 +158,7 @@
                     lane < LANES - shift, rolled[block], rolled[block + 1]
                 )
 
-        def forward(mode, carry):
+        for mode in range(modes):
             w_r, w_i = window[0], window[1]
             p_r, p_i = probe_ref[mode, 0], probe_ref[mode, 1]
             e_r = p_r * w_r - p_i * w_i
@@ -172,9 +173,6 @@
             minus = jnp.concatenate([real[:half] - real[half:], imag[:half] - imag[half:]], axis=0)
             far[mode, 0] = by_rows(plus, table_ref, 2)
             far[mode, 1] = by_rows(minus, table_ref, 3)
-            return carry
-
-        lax.fori_loop(0, modes, forward, 0)
 
         move = order_ref[0]
         measured = moved(diffraction_ref[index], lambda terms: dot(
@@ -197,7 +195,7 @@
         back[0] = power[...] * window[0]
         back[1] = power[...] * window[1]
 
-        def backward(mode, carry):
+        for mode in range(modes):
             even = by_rows(far[mode, 0], table_ref, 0)
             odd = by_rows(far[mode, 1], table_ref, 1)
             plus, minus = even + odd, even - odd
@@ -215,9 +213,6 @@
             by_chunk = (chunks, SUBLANES, side)
             sums[:, 2 * mode] += (w_r * c_r + w_i * c_i).reshape(by_chunk)
             sums[:, 2 * mode + 1] += (w_r * c_i - w_i * c_r).reshape(by_chunk)
-            return carry
-
-        lax.fori_loop(0, modes, backward, 0)
         w_r, w_i = window[0], window[1]
         sums[:, 2 * modes] += (w_r * w_r + w_i * w_i).reshape(chunks, SUBLANES, side)
 
@@ -236,13 +231,19 @@
     lax.fori_loop(0, count_ref[0, 0], slot, 0)
     object_out[...] = extended[pl.ds(0, tile_rows), :] - gradient[pl.ds(0, tile_rows), :] * scale
     spill_out[...] = gradient[pl.ds(tile_rows, halo_rows), :] * scale
-    share = chunks // 2
-    core = core_ref[0, 0]
-    mine_out[...] = sums[pl.ds(core * share, share)]
-    theirs_out[...] = sums[pl.ds((1 - core) * share, share)]
-
-
-def gradient_step(place, count, core, tile, halo, probe, diffraction):
+    core, group, layer = here_ref[0, 0], here_ref[0, 1], here_ref[0, 2]
+    groups, layers = mine_out.shape[0], mine_out.shape[1]
+    for hop in range(groups):
+        for step in range(layers):
+            at = (group ^ hop) * layers + lax.rem(layer + step, layers)
+            mine_out[hop, step] = sums[core * (chunks // 2) + at]
+            if hop < groups - 1:
+                near_out[hop, step] = sums[(1 - core) * (chunks // 2) + at]
+            else:
+                far_out[step] = sums[(1 - core) * (chunks // 2) + at]
+
+
+def gradient_step(place, count, here, tile, halo, probe, diffraction, groups, layers):
     modes, parts, side, _ = probe.shape
     planes = parts * modes + 1
     chunks = side // SUBLANES
@@ -250,22 +251,23 @@
     smem = pl.BlockSpec(memory_space=pltpu.SMEM)
     vmem = pl.BlockSpec(memory_space=pltpu.VMEM)
     anywhere = pl.BlockSpec(memory_space=pl.ANY)
-    share = jax.ShapeDtypeStruct((chunks // 2, planes, SUBLANES, side), f32)
+    chunk = (planes, SUBLANES, side)
     products = 3 * 16 * modes * diffraction.shape[0] * side**3
     return pl.pallas_call(
         step_kernel,
         out_shape=(
             jax.ShapeDtypeStruct(tile.shape, f32),
             jax.ShapeDtypeStruct(halo.shape, f32),
-            share,
-            share,
+            jax.ShapeDtypeStruct((groups, layers, *chunk), f32),
+            jax.ShapeDtypeStruct((groups - 1, layers, *chunk), f32),
+            jax.ShapeDtypeStruct((layers, *chunk), f32),
         ),
         in_specs=[smem, smem, smem, anywhere, anywhere, vmem, vmem, vmem, vmem],
-        out_specs=(vmem, vmem, vmem, vmem),
+        out_specs=(vmem, vmem, vmem, vmem, vmem),
         scratch_shapes=[
             pltpu.VMEM((tile.shape[0] + halo.shape[0], LANES), f32),
             pltpu.VMEM((tile.shape[0] + halo.shape[0], LANES), f32),
-            pltpu.VMEM((chunks, planes, SUBLANES, side), f32),
+            pltpu.VMEM((chunks, *chunk), f32),
             pltpu.VMEM((2, side, side), f32),
             pltpu.VMEM((side, side), f32),
             pltpu.VMEM((modes, 2, side, side), f32),
@@ -275,7 +277,82 @@
         compiler_params=pltpu.CompilerParams(vmem_limit_bytes=48 * 1024 * 1024),
         cost_estimate=pl.CostEstimate(flops=2 * products, bytes_accessed=16 << 20, transcendentals=0),
         name="gradient_step",
-    )(place, count, core, tile, halo, probe, diffraction, jnp.asarray(tables(side)), jnp.asarray(parity_order(side)))
+    )(place, count, here, tile, halo, probe, diffraction, jnp.asarray(tables(side)), jnp.asarray(parity_order(side)))
+
+
+def place_kernel(layers, pieces, here_ref, *refs):
+    *sources, out = refs
+    core, group, layer = here_ref[0, 0], here_ref[0, 1], here_ref[0, 2]
+    for source, (flip, hop, first) in zip(sources, pieces):
+        for j in range(source.shape[0]):
+            from_layer = lax.rem(layer + layers - (first + j), layers)
+            at = (core ^ flip) * (out.shape[1] // 2) + (group ^ hop) * layers + from_layer
+            out[:, at] = source[j]
+
+
+def put_in_place(here, layers, pieces, arrays, planes, side):
+    vmem = pl.BlockSpec(memory_space=pltpu.VMEM)
+    return pl.pallas_call(
+        functools.partial(place_kernel, layers, pieces),
+        out_shape=jax.ShapeDtypeStruct((planes, side // SUBLANES, SUBLANES, side), jnp.float32),
+        in_specs=[pl.BlockSpec(memory_space=pltpu.SMEM)] + [vmem] * len(arrays),
+        out_specs=vmem,
+        compiler_params=pltpu.CompilerParams(vmem_limit_bytes=24 * 1024 * 1024),
+        cost_estimate=pl.CostEstimate(flops=0, bytes_accessed=4 << 20, transcendentals=0),
+        name="put_in_place",
+    )(here, *arrays)
+
+
+def across(block, hop):
+    return lax.ppermute(block, "group", [(i, i ^ hop) for i in range(lax.axis_size("group"))])
+
+
+def from_partner(block):
+    return lax.ppermute(block, "region", [(i, i ^ 1) for i in range(lax.axis_size("region"))])
+
+
+def up_layers(block, step):
+    regions = lax.axis_size("region")
+    return lax.ppermute(block, "region", [(i, (i + 2 * step) % regions) for i in range(regions)])
+
+
+def probe_by_shards(probe, mine, near, far, here, layers, arrived):
+    modes, parts, side, _ = probe.shape
+    planes = modes * parts
+    half = layers // 2
+    near, other_far = lax.optimization_barrier((near, from_partner(far)))
+    other_near = from_partner(near)
+    far_sum = mine[3] + other_far
+    by_x, by_y = across(far_sum[:half], 1), across(far_sum[half:], 2)
+    near_sum = mine[:3] + other_near
+    to_x = near_sum[1].at[half:].add(by_y)
+    to_y = near_sum[2].at[:half].add(by_x)
+    summed = near_sum[0] + across(to_x, 1) + across(to_y, 2)
+    summed, arrived = lax.optimization_barrier((summed, arrived))
+    total = summed[0]
+    for step in range(1, layers):
+        total = total + up_layers(summed[step], step)
+    core, group, layer = here[0, 0], here[0, 1], here[0, 2]
+    start = core * (side // 2) + (group * layers + layer) * SUBLANES
+    old = lax.dynamic_slice(probe.reshape(planes, side, side), (0, start, 0), (planes, SUBLANES, side))
+    fresh = (EPSILON * old + total[:-1]) / (total[-1:] + EPSILON)
+    own = jnp.stack([fresh] + [up_layers(fresh, step) for step in range(1, layers)])
+    x, y = across(own, 1), across(own, 2)
+    arrays = [own, x, y, across(x[:half], 2), across(y[half:], 1)]
+    pieces = [(0, 0), (1, 0), (2, 0), (3, 0), (3, half)]
+    arrays = arrays + [from_partner(array) for array in arrays]
+    pieces = tuple((flip, hop, first) for flip in range(2) for hop, first in pieces)
+    return put_in_place(here, layers, pieces, arrays, planes, side).reshape(probe.shape), arrived
+
+
+def probe_from_whole(probe, mine, near, far):
+    side = probe.shape[2]
+    own = mine.reshape(-1, *mine.shape[2:])
+    rest = jnp.concatenate([near.reshape(-1, *near.shape[2:]), far])
+    whole = lax.psum(jnp.concatenate([own, rest]), ("region", "group"))
+    whole = whole.transpose(1, 0, 2, 3).reshape(-1, side, side)
+    old = probe.reshape(-1, side, side)
+    return ((EPSILON * old + whole[:-1]) / (whole[-1:] + EPSILON)).reshape(probe.shape)
 
 
 def on_device(object_slab, probe, diffraction, positions, slot_counts):
@@ -283,37 +360,26 @@
     tile_rows, _, columns = object_slab.shape
     regions, groups = lax.axis_size("region"), lax.axis_size("group")
     region, group = lax.axis_index("region"), lax.axis_index("group")
-    core, layer = region % 2, region // 2
-    layers = regions // 2
     per_row = parts * columns // LANES
     assert per_row == SUBLANES
+    layers = regions // 2
+    sharded = groups == 4 and 2 * groups * layers * SUBLANES == side
     tile = packed(object_slab)
     halo = shifted(tile[: side * per_row], "region", -1)
     place = positions - jnp.stack([region * tile_rows, jnp.zeros_like(region)])[None, :].astype(jnp.int32)
-    core_entry = core.astype(jnp.int32).reshape(1, 1)
-    new_tile, spill, mine, theirs = gradient_step(place, slot_counts, core_entry, tile, halo, probe, diffraction)
-
-    partner = [(i, i ^ 1) for i in range(regions)]
+    if sharded:
+        here = jnp.stack([region % 2, group, region // 2]).astype(jnp.int32).reshape(1, 3)
+    else:
+        here = jnp.zeros((1, 3), jnp.int32)
+        groups, layers = 4, side // SUBLANES // 8
+    new_tile, spill, mine, near, far = gradient_step(
+        place, slot_counts, here, tile, halo, probe, diffraction, groups, layers
+    )
     arrived = shifted(spill, "region", 1)
-    mine = mine + lax.ppermute(theirs, "region", partner)
-    same_core = [[2 * i + c for i in range(layers)] for c in range(2)]
-    planes = parts * modes + 1
-    mine = lax.all_to_all(mine, "group", 0, 0, tiled=True)
-    mine = jnp.sum(mine.reshape(groups, -1, planes, SUBLANES, side), axis=0)
-    rows = mine.shape[0] * SUBLANES // layers
-    mine = mine.reshape(-1, planes, SUBLANES // min(rows, SUBLANES), min(rows, SUBLANES), side)
-    mine = mine.transpose(0, 2, 1, 3, 4).reshape(layers, planes, rows, side)
-    mine = lax.all_to_all(mine, "region", 0, 0, axis_index_groups=same_core, tiled=True)
-    mine = jnp.sum(mine.reshape(layers, planes, rows, side), axis=0)
-    start = core * (side // 2) + group * (rows * layers) + layer * rows
-    old = lax.dynamic_slice(probe.reshape(planes - 1, side, side), (0, start, 0), (planes - 1, rows, side))
-    fresh = (EPSILON * old + mine[:-1]) / (mine[-1:] + EPSILON)
-    fresh = lax.all_gather(fresh, "region", axis_index_groups=same_core)
-    fresh = lax.all_gather(fresh, "group")
-    other = lax.ppermute(fresh, "region", partner)
-    whole = jnp.where(core == 0, jnp.stack([fresh, other]), jnp.stack([other, fresh]))
-    new_probe = whole.transpose(3, 0, 1, 2, 4, 5).reshape(probe.shape)
-
+    if sharded:
+        new_probe, arrived = probe_by_shards(probe, mine, near, far, here, layers, arrived)
+    else:
+        new_probe = probe_from_whole(probe, mine, near, far)
     overlap = spill.shape[0]
     new_tile = lax.dynamic_update_slice(new_tile, new_tile[:overlap] - arrived, (0, 0))
     return (unpacked(new_tile, object_slab.shape), new_probe)

time: 154 us -> 111 us (0.72)
  blocking collectives: 56.6 us -> 0 us
  starting transfers between devices: 11.7 us -> 45.7 us
  between operations: 14.8 us -> 3.46 us
  waiting for transfers between devices: 38.8 us -> 32.5 us
    all_to_all x1 -> x0, blocking collectives: 42 us -> none  [on_device(): mine = lax.all_to_all(mine, 'group', 0, 0, tiled=True)]
    ppermute x2 -> x21, starting transfers between devices: 5.23 us -> 42.4 us  [the longest x8 23 us: across(): lax.ppermute(block, 'group', [(i, i ^ hop) for i in range(lax.axis_size('...]
    ppermute x2 -> x21, waiting for transfers between devices: 3.29 us -> 30 us  [the longest x8 18.9 us: across(): lax.ppermute(block, 'group', [(i, i ^ hop) for i in range(lax.axis_size('...]
    all_gather x1 -> x0, waiting for transfers between devices: 24.5 us -> none  [on_device(): fresh = lax.all_gather(fresh, 'group')]
    all_gather x1 -> x0, blocking collectives: 14.5 us -> none  [on_device(): fresh = lax.all_gather(fresh, 'region', axis_index_groups=same_core)]
    all_to_all x1 -> x0, waiting for transfers between devices: 8.62 us -> none  [on_device(): lax.all_to_all(mine, 'region', 0, 0, axis_index_groups=same_core, tiled=T...]
    all_to_all x1 -> x0, starting transfers between devices: 3.8 us -> none  [on_device(): lax.all_to_all(mine, 'region', 0, 0, axis_index_groups=same_core, tiled=T...]
    add x1 -> x4, other arithmetic: 0.15 us -> 3.38 us  [the longest x1 1.34 us: probe_by_shards(): near_sum = mine[:3] + other_near]
  transfers between devices with their start and end apart: 6 -> 23, of which waited for: 5 -> 14; matrix products, arithmetic and copies ran while one was open for 2% -> 3% of each run, Pallas kernels for 0% -> 0%
where the time goes in v2:
time: 111 us
  starting transfers between devices  45.7 us (41%)
  waiting for transfers between devices  32.5 us (29%)
  Pallas kernels  20 us (18%)
  local copies, waits for them, and re-layouts  5.16 us (5%)
  other arithmetic  4.67 us (4%)
  between operations  3.46 us (3%)
    ppermute x8, starting transfers between devices, across(): lax.ppermute(block, 'group', [(i, i ^ hop) for i in range(lax.axis_size('...  23 us
    ppermute x8, waiting for transfers between devices, across(): lax.ppermute(block, 'group', [(i, i ^ hop) for i in range(lax.axis_size('...  18.9 us
    pallas_call x1, Pallas kernels, gradient_step(): pl.pallas_call(step_kernel, out_shape=(jax.ShapeDtypeStruct(tile.shape, f...  17.9 us
    ppermute x7, starting transfers between devices, from_partner(): lax.ppermute(block, 'region', [(i, i ^ 1) for i in range(lax.axis_size('r...  13.9 us
    ppermute x6, waiting for transfers between devices, up_layers(): lax.ppermute(block, 'region', [(i, (i + 2 * step) % regions) for i in ran...  8.73 us
    ppermute x6, starting transfers between devices, up_layers(): lax.ppermute(block, 'region', [(i, (i + 2 * step) % regions) for i in ran...  5.42 us
    ppermute x2, starting transfers between devices, shifted(): return lax.ppermute(block, axis, route)  3.38 us
    slice x1, local copies, waits for them, and re-layouts, on_device(): halo = shifted(tile[:side * per_row], 'region', -1)  2.7 us
  transfers between devices with their start and end apart: 23, of which 14 were waited for; matrix products, arithmetic and copies ran while one was open for 3% of the time, Pallas kernels for 0%

profile of v2, /device:TPU:0, one launch (start us, length us, event | category | flops | bytes accessed | tf_op | source)
XLA Modules:
  0.0 111.5 jit_solution(14994456250249979403)
XLA Ops:
  0.6 0.0 copy-start.1
  0.7 2.7 %slice.146 = f32[256,4,2,128]{3,2,1,0:T(2,128)} slice(f32[512,4,2,128]{3,2,1,0:T(2,128)} %bitcast.64), slice={[0:256], [0:4], [0:2], [0:128]} | slice | bytes 2097152 | tf_op jit(solution)/shard_map/slice | solution.py:368
  3.4 1.3 %collective-permute-start = (f32[2048,128]{1,0:T(8,128)}, f32[2048,128]{1,0:T(8,128)S(1)}, u32[]{:S(2)}, u32[]{:S(2)}) collective-permute-start(f32[2048,128]{1,0:T(8,128)} %bitcast.9), channel_id=1, source_target_pairs={{4,0},{8,4},{12,8},{16,12},{20,16},{24,20},{28,24},{5,1},{9,5},{13... | collective-permute-start | bytes 3145736 | tf_op jit(solution)/shard_map/ppermute | solution.py:20
  4.7 0.1 copy.9
  5.4 0.1 pad_add_fusion
  5.5 0.1 add_bitcast_fusion.here_ref
  5.6 2.5 %collective-permute-done.halo_hbm = f32[2048,128]{1,0:T(8,128)S(1)} collective-permute-done((f32[2048,128]{1,0:T(8,128)}, f32[2048,128]{1,0:T(8,128)S(1)}, u32[]{:S(2)}, u32[]{:S(2)}) %collective-permute-start) | collective-permute-done | bytes 1048608 | tf_op jit(solution)/shard_map/ppermute | solution.py:20
  8.1 0.0 copy-done
  8.1 0.9 copy-done.2
  9.1 17.9 %gradient_step.1 = (f32[4096,128]{1,0:T(8,128)}, f32[2048,128]{1,0:T(8,128)S(1)}, f32[4,4,9,8,256]{4,3,2,1,0:T(8,128)}, f32[3,4,9,8,256]{4,3,2,1,0:T(8,128)S(1)}, f32[4,9,8,256]{3,2,1,0:T(8,128)S(1)}) custom-call(s32[4,2]{1,0:T(4,128)S(1)} %broadcast_subtract_fusion.place_ref, s32[1,1]{1,0:T(1,128)S(6)} %copy.15.count_ref, ...), custom_call_target="tpu_custom_call" | custom-call | flops 25769803776 | bytes 16777216 | tf_op jit(solution)/shard_map/gradient_step/pallas_call | solution.py:256
  27.0 13.0 %collective-permute-start.1 = (f32[4,9,8,256]{3,2,1,0:T(8,128)S(1)}, f32[4,9,8,256]{3,2,1,0:T(8,128)S(1)}, u32[]{:S(2)}, u32[]{:S(2)}) collective-permute-start(f32[4,9,8,256]{3,2,1,0:T(8,128)S(1)} %get-tuple-element.38), channel_id=1, source_target_pairs={{0,4},{4,0},{8,12},{12,8},{16,20},{20,16},{24,28},{28,24},{1,5},{5... | collective-permute-start | bytes 884744 | tf_op jit(solution)/shard_map/ppermute | solution.py:311
  40.1 1.2 %collective-permute-done.1 = f32[4,9,8,256]{3,2,1,0:T(8,128)S(1)} collective-permute-done((f32[4,9,8,256]{3,2,1,0:T(8,128)S(1)}, f32[4,9,8,256]{3,2,1,0:T(8,128)S(1)}, u32[]{:S(2)}, u32[]{:S(2)}) %collective-permute-start.1) | collective-permute-done | bytes 294944 | tf_op jit(solution)/shard_map/ppermute | solution.py:311
  41.3 0.4 collective-permute-start.2
  41.7 2.1 %collective-permute-start.7 = (f32[2048,128]{1,0:T(8,128)S(1)}, f32[2048,128]{1,0:T(8,128)S(1)}, u32[]{:S(2)}, u32[]{:S(2)}) collective-permute-start(f32[2048,128]{1,0:T(8,128)S(1)} %get-tuple-element.41), channel_id=1, source_target_pairs={{0,4},{4,8},{8,12},{12,16},{16,20},{20,24},{24,28},{1,5},{5,9},{9,... | collective-permute-start | bytes 3145736 | tf_op jit(solution)/shard_map/ppermute | solution.py:20
  43.8 1.0 bitcast_add_fusion
  44.8 1.6 %collective-permute-start.3 = (f32[2,9,8,256]{3,2,1,0:T(8,128)S(1)}, f32[2,9,8,256]{3,2,1,0:T(8,128)S(1)}, u32[]{:S(2)}, u32[]{:S(2)}) collective-permute-start(f32[2,9,8,256]{3,2,1,0:T(8,128)S(1)} %get-tuple-element.51), channel_id=1, source_target_pairs={{0,2},{1,3},{2,0},{3,1},{4,6},{5,7},{6,4},{7,5},{8,10},{9,11},{10,... | collective-permute-start | bytes 442376 | tf_op jit(solution)/shard_map/ppermute | solution.py:307
  46.3 12.8 %collective-permute-start.5 = (f32[2,9,8,256]{3,2,1,0:T(8,128)S(1)}, f32[2,9,8,256]{3,2,1,0:T(8,128)S(1)}, u32[]{:S(2)}, u32[]{:S(2)}) collective-permute-start(f32[2,9,8,256]{3,2,1,0:T(8,128)S(1)} %get-tuple-element.52), channel_id=1, source_target_pairs={{0,1},{1,0},{2,3},{3,2},{4,5},{5,4},{6,7},{7,6},{8,9},{9,8},{10,11... | collective-permute-start | bytes 442376 | tf_op jit(solution)/shard_map/ppermute | solution.py:307
  59.2 0.0 collective-permute-done.2
  59.2 1.3 %slice_add_fusion = f32[3,4,9,8,256]{4,3,2,1,0:T(8,128)S(1)} fusion(f32[3,4,9,8,256]{4,3,2,1,0:T(8,128)S(1)} %collective-permute-done.2, f32[4,4,9,8,256]{4,3,2,1,0:T(8,128)} %get-tuple-element.36), kind=kLoop, calls=%fused_computation.1 | loop fusion | flops 221184 | bytes 2654208 | tf_op jit(solution)/shard_map/add | solution.py:327
  60.6 0.0 collective-permute-done.3
  60.6 2.4 %collective-permute-done.5 = f32[2,9,8,256]{3,2,1,0:T(8,128)S(1)} collective-permute-done((f32[2,9,8,256]{3,2,1,0:T(8,128)S(1)}, f32[2,9,8,256]{3,2,1,0:T(8,128)S(1)}, u32[]{:S(2)}, u32[]{:S(2)}) %collective-permute-start.5) | collective-permute-done | bytes 147488 | tf_op jit(solution)/shard_map/ppermute | solution.py:307
  63.0 2.2 %collective-permute-start.6 = (f32[4,9,8,256]{3,2,1,0:T(8,128)S(1)}, f32[4,9,8,256]{3,2,1,0:T(8,128)S(1)}, u32[]{:S(2)}, u32[]{:S(2)}) collective-permute-start(f32[4,9,8,256]{3,2,1,0:T(8,128)S(1)} %get-tuple-element.45), channel_id=1, source_target_pairs={{0,2},{1,3},{2,0},{3,1},{4,6},{5,7},{6,4},{7,5},{8,10},{9,11},{10,... | collective-permute-start | bytes 884744 | tf_op jit(solution)/shard_map/ppermute | solution.py:307
  65.3 2.5 %collective-permute-start.4 = (f32[4,9,8,256]{3,2,1,0:T(8,128)S(1)}, f32[4,9,8,256]{3,2,1,0:T(8,128)S(1)}, u32[]{:S(2)}, u32[]{:S(2)}) collective-permute-start(f32[4,9,8,256]{3,2,1,0:T(8,128)S(1)} %get-tuple-element.44), channel_id=1, source_target_pairs={{0,1},{1,0},{2,3},{3,2},{4,5},{5,4},{6,7},{7,6},{8,9},{9,8},{10,11... | collective-permute-start | bytes 884744 | tf_op jit(solution)/shard_map/ppermute | solution.py:307
  67.7 5.1 %collective-permute-done.6 = f32[4,9,8,256]{3,2,1,0:T(8,128)S(1)} collective-permute-done((f32[4,9,8,256]{3,2,1,0:T(8,128)S(1)}, f32[4,9,8,256]{3,2,1,0:T(8,128)S(1)}, u32[]{:S(2)}, u32[]{:S(2)}) %collective-permute-start.6) | collective-permute-done | bytes 294944 | tf_op jit(solution)/shard_map/ppermute | solution.py:307
  72.9 1.9 %collective-permute-done.4 = f32[4,9,8,256]{3,2,1,0:T(8,128)S(1)} collective-permute-done((f32[4,9,8,256]{3,2,1,0:T(8,128)S(1)}, f32[4,9,8,256]{3,2,1,0:T(8,128)S(1)}, u32[]{:S(2)}, u32[]{:S(2)}) %collective-permute-start.4) | collective-permute-done | bytes 294944 | tf_op jit(solution)/shard_map/ppermute | solution.py:307
  74.7 0.1 fusion.1
  74.8 0.0 collective-permute-done.7
  74.8 0.7 slice_bitcast_fusion.7
  75.5 0.0 collective-permute-start.10
  75.5 1.0 collective-permute-start.9
  76.5 1.0 collective-permute-start.8
  77.5 0.7 fusion.11
  80.1 0.3 collective-permute-done.10
  80.4 3.4 %collective-permute-done.9 = f32[9,8,256]{2,1,0:T(8,128)} collective-permute-done((f32[9,8,256]{2,1,0:T(8,128)}, f32[9,8,256]{2,1,0:T(8,128)}, u32[]{:S(2)}, u32[]{:S(2)}) %collective-permute-start.9) | collective-permute-done | bytes 73760 | tf_op jit(solution)/shard_map/ppermute | solution.py:316
  83.9 0.0 collective-permute-done.8
  83.9 1.0 fusion.7
  84.9 0.9 fusion.8
  85.7 1.3 %collective-permute-start.13 = (f32[8,8,256]{2,1,0:T(8,128)S(1)}, f32[8,8,256]{2,1,0:T(8,128)S(1)}, u32[]{:S(2)}, u32[]{:S(2)}) collective-permute-start(f32[8,8,256]{2,1,0:T(8,128)S(1)} %fusion.8), channel_id=1, source_target_pairs={{0,24},{4,28},{8,0},{12,4},{16,8},{20,12},{24,16},{28,20},{1,25},{... | collective-permute-start | bytes 196616 | tf_op jit(solution)/shard_map/ppermute | solution.py:316
  87.1 0.1 collective-permute-start.12
  87.2 1.9 %collective-permute-start.11 = (f32[8,8,256]{2,1,0:T(8,128)S(1)}, f32[8,8,256]{2,1,0:T(8,128)S(1)}, u32[]{:S(2)}, u32[]{:S(2)}) collective-permute-start(f32[8,8,256]{2,1,0:T(8,128)S(1)} %fusion.8), channel_id=1, source_target_pairs={{0,8},{4,12},{8,16},{12,20},{16,24},{20,28},{24,0},{28,4},{1,9},{5... | collective-permute-start | bytes 196616 | tf_op jit(solution)/shard_map/ppermute | solution.py:316
  89.1 1.3 %collective-permute-done.13 = f32[8,8,256]{2,1,0:T(8,128)S(1)} collective-permute-done((f32[8,8,256]{2,1,0:T(8,128)S(1)}, f32[8,8,256]{2,1,0:T(8,128)S(1)}, u32[]{:S(2)}, u32[]{:S(2)}) %collective-permute-start.13) | collective-permute-done | bytes 65568 | tf_op jit(solution)/shard_map/ppermute | solution.py:316
  90.4 3.7 %collective-permute-done.12 = f32[8,8,256]{2,1,0:T(8,128)S(1)} collective-permute-done((f32[8,8,256]{2,1,0:T(8,128)S(1)}, f32[8,8,256]{2,1,0:T(8,128)S(1)}, u32[]{:S(2)}, u32[]{:S(2)}) %collective-permute-start.12) | collective-permute-done | bytes 65568 | tf_op jit(solution)/shard_map/ppermute | solution.py:316
  94.1 0.0 collective-permute-done.11
  94.1 1.2 %collective-permute-start.14 = (f32[4,8,8,256]{3,2,1,0:T(8,128)S(1)}, f32[4,8,8,256]{3,2,1,0:T(8,128)S(1)}, u32[]{:S(2)}, u32[]{:S(2)}) collective-permute-start(f32[4,8,8,256]{3,2,1,0:T(8,128)S(1)} %pad_maximum_fusion.refs_0_), channel_id=1, source_target_pairs={{0,1},{1,0},{2,3},{3,2},{4,5},{5,4},{6,7},{7,6},{8,9},{9,8},{10,11... | collective-permute-start | bytes 786440 | tf_op jit(solution)/shard_map/ppermute | solution.py:307
  95.3 1.0 collective-permute-start.15
  96.3 4.3 %collective-permute-done.14.refs_1_ = f32[4,8,8,256]{3,2,1,0:T(8,128)S(1)} collective-permute-done((f32[4,8,8,256]{3,2,1,0:T(8,128)S(1)}, f32[4,8,8,256]{3,2,1,0:T(8,128)S(1)}, u32[]{:S(2)}, u32[]{:S(2)}) %collective-permute-start.14) | collective-permute-done | bytes 262176 | tf_op jit(solution)/shard_map/ppermute | solution.py:307
  100.6 0.8 collective-permute-start.16
  101.4 1.7 %collective-permute-done.15.refs_2_ = f32[4,8,8,256]{3,2,1,0:T(8,128)S(1)} collective-permute-done((f32[4,8,8,256]{3,2,1,0:T(8,128)S(1)}, f32[4,8,8,256]{3,2,1,0:T(8,128)S(1)}, u32[]{:S(2)}, u32[]{:S(2)}) %collective-permute-start.15) | collective-permute-done | bytes 262176 | tf_op jit(solution)/shard_map/ppermute | solution.py:307
  103.1 1.0 collective-permute-start.17
  104.1 0.0 collective-permute-start.18
  104.1 0.5 collective-permute-start.19
  104.6 0.0 collective-permute-start.20
  104.6 1.0 collective-permute-done.16.refs_3_
  105.6 0.0 collective-permute-start.21
  105.6 2.5 %collective-permute-done.17.refs_4_ = f32[2,8,8,256]{3,2,1,0:T(8,128)S(1)} collective-permute-done((f32[2,8,8,256]{3,2,1,0:T(8,128)S(1)}, f32[2,8,8,256]{3,2,1,0:T(8,128)S(1)}, u32[]{:S(2)}, u32[]{:S(2)}) %collective-permute-start.17) | collective-permute-done | bytes 131104 | tf_op jit(solution)/shard_map/ppermute | solution.py:307
  108.1 0.0 collective-permute-start.22
  108.1 0.2 subtract_dynamic-update-slice_fusion
  108.4 0.0 copy-start.4
  108.4 0.0 collective-permute-done.18.refs_5_
  108.4 0.0 collective-permute-done.19.refs_6_
  108.4 0.0 collective-permute-done.20.refs_7_
  108.4 0.0 collective-permute-done.21.refs_8_
  108.4 1.1 collective-permute-done.22.refs_9_
  109.5 2.0 %put_in_place.1 = f32[8,32,8,256]{3,2,1,0:T(8,128)} custom-call(s32[1,3]{1,0:T(1,128)S(1)} %add_bitcast_fusion.here_ref, f32[4,8,8,256]{3,2,1,0:T(8,128)S(1)} %pad_maximum_fusion.refs_0_, f32[4,8,8,256]{3,2,1,0:T(8,128)S(1)} %collective-permute-done.14.refs_1_, f32[4,8,8,256]{3,2,1,0:T(8,128)S(1)} %collective-permute-done.15.refs_2_, ...), custom_call_target="tpu_custom_call" | custom-call | bytes 4194304 | tf_op jit(solution)/shard_map/put_in_place/pallas_call | solution.py:295
  (16 shorter events, 0.2 us)
Async XLA Ops:
  0.6 7.5 %copy-start.1 = (bf16[2,4,256,256]{3,2,1,0:T(8,128)(2,1)S(1)}, bf16[2,4,256,256]{3,2,1,0:T(8,128)(2,1)}, u32[]{:S(2)}) copy-start(bf16[2,4,256,256]{3,2,1,0:T(8,128)(2,1)} %constant.110.clone.table_ref) | copy-start | bytes 3145732
  0.6 4.0 %copy-start.5 = (s32[4,2]{0,1:T(2,128)S(1)}, s32[4,2]{0,1:T(2,128)}, u32[]{:S(2)}) copy-start(s32[4,2]{0,1:T(2,128)} %param.14) | copy-start | bytes 100
  0.7 7.5 %copy-start = (f32[4,256,256]{2,1,0:T(8,128)S(1)}, f32[4,256,256]{2,1,0:T(8,128)}, u32[]{:S(2)}) copy-start(f32[4,256,256]{2,1,0:T(8,128)} %diffraction_ref.1) | copy-start | bytes 3145732
  3.4 4.8 %collective-permute-start = (f32[2048,128]{1,0:T(8,128)}, f32[2048,128]{1,0:T(8,128)S(1)}, u32[]{:S(2)}, u32[]{:S(2)}) collective-permute-start(f32[2048,128]{1,0:T(8,128)} %bitcast.9), channel_id=1, source_target_pairs={{4,0},{8,4},{12,8},{16,12},{20,16},{24,20},{28,24},{5,1},{9,5},{13... | collective-permute-start | bytes 3145736 | tf_op jit(solution)/shard_map/ppermute | solution.py:20
  8.1 1.0 copy-start.2
  27.0 14.3 %collective-permute-start.1 = (f32[4,9,8,256]{3,2,1,0:T(8,128)S(1)}, f32[4,9,8,256]{3,2,1,0:T(8,128)S(1)}, u32[]{:S(2)}, u32[]{:S(2)}) collective-permute-start(f32[4,9,8,256]{3,2,1,0:T(8,128)S(1)} %get-tuple-element.38), channel_id=1, source_target_pairs={{0,4},{4,0},{8,12},{12,8},{16,20},{20,16},{24,28},{28,24},{1,5},{5... | collective-permute-start | bytes 884744 | tf_op jit(solution)/shard_map/ppermute | solution.py:311
  41.3 17.9 %collective-permute-start.2 = (f32[3,4,9,8,256]{4,3,2,1,0:T(8,128)S(1)}, f32[3,4,9,8,256]{4,3,2,1,0:T(8,128)S(1)}, u32[]{:S(2)}, u32[]{:S(2)}) collective-permute-start(f32[3,4,9,8,256]{4,3,2,1,0:T(8,128)S(1)} %get-tuple-element.39), channel_id=1, source_target_pairs={{0,4},{4,0},{8,12},{12,8},{16,20},{20,16},{24,28},{28,24},{1,5},{5... | collective-permute-start | bytes 2654216 | tf_op jit(solution)/shard_map/ppermute | solution.py:311
  41.7 33.1 %collective-permute-start.7 = (f32[2048,128]{1,0:T(8,128)S(1)}, f32[2048,128]{1,0:T(8,128)S(1)}, u32[]{:S(2)}, u32[]{:S(2)}) collective-permute-start(f32[2048,128]{1,0:T(8,128)S(1)} %get-tuple-element.41), channel_id=1, source_target_pairs={{0,4},{4,8},{8,12},{12,16},{16,20},{20,24},{24,28},{1,5},{5,9},{9,... | collective-permute-start | bytes 3145736 | tf_op jit(solution)/shard_map/ppermute | solution.py:20
  44.8 15.8 %collective-permute-start.3 = (f32[2,9,8,256]{3,2,1,0:T(8,128)S(1)}, f32[2,9,8,256]{3,2,1,0:T(8,128)S(1)}, u32[]{:S(2)}, u32[]{:S(2)}) collective-permute-start(f32[2,9,8,256]{3,2,1,0:T(8,128)S(1)} %get-tuple-element.51), channel_id=1, source_target_pairs={{0,2},{1,3},{2,0},{3,1},{4,6},{5,7},{6,4},{7,5},{8,10},{9,11},{10,... | collective-permute-start | bytes 442376 | tf_op jit(solution)/shard_map/ppermute | solution.py:307
  46.3 16.6 %collective-permute-start.5 = (f32[2,9,8,256]{3,2,1,0:T(8,128)S(1)}, f32[2,9,8,256]{3,2,1,0:T(8,128)S(1)}, u32[]{:S(2)}, u32[]{:S(2)}) collective-permute-start(f32[2,9,8,256]{3,2,1,0:T(8,128)S(1)} %get-tuple-element.52), channel_id=1, source_target_pairs={{0,1},{1,0},{2,3},{3,2},{4,5},{5,4},{6,7},{7,6},{8,9},{9,8},{10,11... | collective-permute-start | bytes 442376 | tf_op jit(solution)/shard_map/ppermute | solution.py:307
  63.0 45.1 %copy-start.3 = (f32[4096,128]{1,0:T(8,128)S(1)}, f32[4096,128]{1,0:T(8,128)}, u32[]{:S(2)}) copy-start(f32[4096,128]{1,0:T(8,128)} %get-tuple-element.35) | copy-start | bytes 6291460
  63.0 9.8 %collective-permute-start.6 = (f32[4,9,8,256]{3,2,1,0:T(8,128)S(1)}, f32[4,9,8,256]{3,2,1,0:T(8,128)S(1)}, u32[]{:S(2)}, u32[]{:S(2)}) collective-permute-start(f32[4,9,8,256]{3,2,1,0:T(8,128)S(1)} %get-tuple-element.45), channel_id=1, source_target_pairs={{0,2},{1,3},{2,0},{3,1},{4,6},{5,7},{6,4},{7,5},{8,10},{9,11},{10,... | collective-permute-start | bytes 884744 | tf_op jit(solution)/shard_map/ppermute | solution.py:307
  65.3 9.5 %collective-permute-start.4 = (f32[4,9,8,256]{3,2,1,0:T(8,128)S(1)}, f32[4,9,8,256]{3,2,1,0:T(8,128)S(1)}, u32[]{:S(2)}, u32[]{:S(2)}) collective-permute-start(f32[4,9,8,256]{3,2,1,0:T(8,128)S(1)} %get-tuple-element.44), channel_id=1, source_target_pairs={{0,1},{1,0},{2,3},{3,2},{4,5},{5,4},{6,7},{7,6},{8,9},{9,8},{10,11... | collective-permute-start | bytes 884744 | tf_op jit(solution)/shard_map/ppermute | solution.py:307
  75.5 5.0 %collective-permute-start.10 = (f32[9,8,256]{2,1,0:T(8,128)}, f32[9,8,256]{2,1,0:T(8,128)}, u32[]{:S(2)}, u32[]{:S(2)}) collective-permute-start(f32[9,8,256]{2,1,0:T(8,128)} %get-tuple-element.49), channel_id=1, source_target_pairs={{0,24},{4,28},{8,0},{12,4},{16,8},{20,12},{24,16},{28,20},{1,25},{... | collective-permute-start | bytes 221192 | tf_op jit(solution)/shard_map/ppermute | solution.py:316
  75.5 8.4 %collective-permute-start.9 = (f32[9,8,256]{2,1,0:T(8,128)}, f32[9,8,256]{2,1,0:T(8,128)}, u32[]{:S(2)}, u32[]{:S(2)}) collective-permute-start(f32[9,8,256]{2,1,0:T(8,128)} %get-tuple-element.50), channel_id=1, source_target_pairs={{0,16},{4,20},{8,24},{12,28},{16,0},{20,4},{24,8},{28,12},{1,17},{... | collective-permute-start | bytes 221192 | tf_op jit(solution)/shard_map/ppermute | solution.py:316
  76.5 7.4 %collective-permute-start.8 = (f32[9,8,256]{2,1,0:T(8,128)S(1)}, f32[9,8,256]{2,1,0:T(8,128)}, u32[]{:S(2)}, u32[]{:S(2)}) collective-permute-start(f32[9,8,256]{2,1,0:T(8,128)S(1)} %get-tuple-element.48), channel_id=1, source_target_pairs={{0,8},{4,12},{8,16},{12,20},{16,24},{20,28},{24,0},{28,4},{1,9},{5... | collective-permute-start | bytes 221192 | tf_op jit(solution)/shard_map/ppermute | solution.py:316
  85.7 4.7 %collective-permute-start.13 = (f32[8,8,256]{2,1,0:T(8,128)S(1)}, f32[8,8,256]{2,1,0:T(8,128)S(1)}, u32[]{:S(2)}, u32[]{:S(2)}) collective-permute-start(f32[8,8,256]{2,1,0:T(8,128)S(1)} %fusion.8), channel_id=1, source_target_pairs={{0,24},{4,28},{8,0},{12,4},{16,8},{20,12},{24,16},{28,20},{1,25},{... | collective-permute-start | bytes 196616 | tf_op jit(solution)/shard_map/ppermute | solution.py:316
  87.1 7.0 %collective-permute-start.12 = (f32[8,8,256]{2,1,0:T(8,128)S(1)}, f32[8,8,256]{2,1,0:T(8,128)S(1)}, u32[]{:S(2)}, u32[]{:S(2)}) collective-permute-start(f32[8,8,256]{2,1,0:T(8,128)S(1)} %fusion.8), channel_id=1, source_target_pairs={{0,16},{4,20},{8,24},{12,28},{16,0},{20,4},{24,8},{28,12},{1,17},{... | collective-permute-start | bytes 196616 | tf_op jit(solution)/shard_map/ppermute | solution.py:316
  87.2 6.9 %collective-permute-start.11 = (f32[8,8,256]{2,1,0:T(8,128)S(1)}, f32[8,8,256]{2,1,0:T(8,128)S(1)}, u32[]{:S(2)}, u32[]{:S(2)}) collective-permute-start(f32[8,8,256]{2,1,0:T(8,128)S(1)} %fusion.8), channel_id=1, source_target_pairs={{0,8},{4,12},{8,16},{12,20},{16,24},{20,28},{24,0},{28,4},{1,9},{5... | collective-permute-start | bytes 196616 | tf_op jit(solution)/shard_map/ppermute | solution.py:316
  94.1 6.4 %collective-permute-start.14 = (f32[4,8,8,256]{3,2,1,0:T(8,128)S(1)}, f32[4,8,8,256]{3,2,1,0:T(8,128)S(1)}, u32[]{:S(2)}, u32[]{:S(2)}) collective-permute-start(f32[4,8,8,256]{3,2,1,0:T(8,128)S(1)} %pad_maximum_fusion.refs_0_), channel_id=1, source_target_pairs={{0,1},{1,0},{2,3},{3,2},{4,5},{5,4},{6,7},{7,6},{8,9},{9,8},{10,11... | collective-permute-start | bytes 786440 | tf_op jit(solution)/shard_map/ppermute | solution.py:307
  95.3 7.8 %collective-permute-start.15 = (f32[4,8,8,256]{3,2,1,0:T(8,128)S(1)}, f32[4,8,8,256]{3,2,1,0:T(8,128)S(1)}, u32[]{:S(2)}, u32[]{:S(2)}) collective-permute-start(f32[4,8,8,256]{3,2,1,0:T(8,128)S(1)} %pad_maximum_fusion.refs_0_), channel_id=1, source_target_pairs={{0,2},{1,3},{2,0},{3,1},{4,6},{5,7},{6,4},{7,5},{8,10},{9,11},{10,... | collective-permute-start | bytes 786440 | tf_op jit(solution)/shard_map/ppermute | solution.py:307
  100.6 5.0 %collective-permute-start.16 = (f32[2,8,8,256]{3,2,1,0:T(8,128)S(1)}, f32[2,8,8,256]{3,2,1,0:T(8,128)S(1)}, u32[]{:S(2)}, u32[]{:S(2)}) collective-permute-start(f32[2,8,8,256]{3,2,1,0:T(8,128)S(1)} %slice.156), channel_id=1, source_target_pairs={{0,2},{1,3},{2,0},{3,1},{4,6},{5,7},{6,4},{7,5},{8,10},{9,11},{10,... | collective-permute-start | bytes 393224 | tf_op jit(solution)/shard_map/ppermute | solution.py:307
  103.1 5.0 %collective-permute-start.17 = (f32[2,8,8,256]{3,2,1,0:T(8,128)S(1)}, f32[2,8,8,256]{3,2,1,0:T(8,128)S(1)}, u32[]{:S(2)}, u32[]{:S(2)}) collective-permute-start(f32[2,8,8,256]{3,2,1,0:T(8,128)S(1)} %slice.157), channel_id=1, source_target_pairs={{0,1},{1,0},{2,3},{3,2},{4,5},{5,4},{6,7},{7,6},{8,9},{9,8},{10,11... | collective-permute-start | bytes 393224 | tf_op jit(solution)/shard_map/ppermute | solution.py:307
  104.1 4.3 %collective-permute-start.18 = (f32[4,8,8,256]{3,2,1,0:T(8,128)S(1)}, f32[4,8,8,256]{3,2,1,0:T(8,128)S(1)}, u32[]{:S(2)}, u32[]{:S(2)}) collective-permute-start(f32[4,8,8,256]{3,2,1,0:T(8,128)S(1)} %pad_maximum_fusion.refs_0_), channel_id=1, source_target_pairs={{0,4},{4,0},{8,12},{12,8},{16,20},{20,16},{24,28},{28,24},{1,5},{5... | collective-permute-start | bytes 786440 | tf_op jit(solution)/shard_map/ppermute | solution.py:311
  104.1 4.3 %collective-permute-start.19 = (f32[4,8,8,256]{3,2,1,0:T(8,128)S(1)}, f32[4,8,8,256]{3,2,1,0:T(8,128)S(1)}, u32[]{:S(2)}, u32[]{:S(2)}) collective-permute-start(f32[4,8,8,256]{3,2,1,0:T(8,128)S(1)} %collective-permute-done.14.refs_1_), channel_id=1, source_target_pairs={{0,4},{4,0},{8,12},{12,8},{16,20},{20,16},{24,28},{28,24},{1,5},{5... | collective-permute-start | bytes 786440 | tf_op jit(solution)/shard_map/ppermute | solution.py:311
  104.6 3.8 %collective-permute-start.20 = (f32[4,8,8,256]{3,2,1,0:T(8,128)S(1)}, f32[4,8,8,256]{3,2,1,0:T(8,128)S(1)}, u32[]{:S(2)}, u32[]{:S(2)}) collective-permute-start(f32[4,8,8,256]{3,2,1,0:T(8,128)S(1)} %collective-permute-done.15.refs_2_), channel_id=1, source_target_pairs={{0,4},{4,0},{8,12},{12,8},{16,20},{20,16},{24,28},{28,24},{1,5},{5... | collective-permute-start | bytes 786440 | tf_op jit(solution)/shard_map/ppermute | solution.py:311
  105.6 2.8 %collective-permute-start.21 = (f32[2,8,8,256]{3,2,1,0:T(8,128)S(1)}, f32[2,8,8,256]{3,2,1,0:T(8,128)S(1)}, u32[]{:S(2)}, u32[]{:S(2)}) collective-permute-start(f32[2,8,8,256]{3,2,1,0:T(8,128)S(1)} %collective-permute-done.16.refs_3_), channel_id=1, source_target_pairs={{0,4},{4,0},{8,12},{12,8},{16,20},{20,16},{24,28},{28,24},{1,5},{5... | collective-permute-start | bytes 393224 | tf_op jit(solution)/shard_map/ppermute | solution.py:311
  108.1 1.3 %collective-permute-start.22 = (f32[2,8,8,256]{3,2,1,0:T(8,128)S(1)}, f32[2,8,8,256]{3,2,1,0:T(8,128)S(1)}, u32[]{:S(2)}, u32[]{:S(2)}) collective-permute-start(f32[2,8,8,256]{3,2,1,0:T(8,128)S(1)} %collective-permute-done.17.refs_4_), channel_id=1, source_target_pairs={{0,4},{4,0},{8,12},{12,8},{16,20},{20,16},{24,28},{28,24},{1,5},{5... | collective-permute-start | bytes 393224 | tf_op jit(solution)/shard_map/ppermute | solution.py:311
  108.4 3.1 %copy-start.4 = (f32[4096,128]{1,0:T(8,128)}, f32[4096,128]{1,0:T(8,128)S(1)}, u32[]{:S(2)}) copy-start(f32[4096,128]{1,0:T(8,128)S(1)} %subtract_dynamic-update-slice_fusion) | copy-start | bytes 6291460

commit v3 on v2

--- a/solution.py
+++ b/solution.py
@@ -11,6 +11,7 @@
 
 LANES = 128
 SUBLANES = 8
+ROWS = 32
 EPSILON = 1e-06
 
 
@@ -64,22 +65,24 @@
     return jnp.dot(a, b, preferred_element_type=jnp.float32)
 
 
-def by_lanes(x, table_ref, index):
-    high, low = split(x)
-    t_high, t_low = table_ref[0, index], table_ref[1, index]
-    return dot(
-        jnp.concatenate([high, low, high], axis=1),
-        jnp.concatenate([t_high, t_high, t_low], axis=0),
-    )
-
-
-def by_rows(x, table_ref, index):
-    high, low = split(x)
-    t_high, t_low = table_ref[0, index], table_ref[1, index]
-    return dot(
-        jnp.concatenate([t_high, t_high, t_low], axis=1),
-        jnp.concatenate([high, low, high], axis=0),
-    )
+def transform(terms, rows, table_ref, table, out):
+    side = out.shape[2]
+    for half in range(2):
+        high = terms[half, rows, pl.ds(0, side)]
+        low = terms[half, rows, pl.ds(side, side)]
+        t_high, t_low = table_ref[0, table + half], table_ref[1, table + half]
+        out[half, rows, :] = dot(
+            jnp.concatenate([high, low, high], axis=1),
+            jnp.concatenate([t_high, t_high, t_low], axis=0),
+        )
+
+
+def keep(terms, half, start, real, imag):
+    rows = pl.ds(start, real.shape[0])
+    side = 2 * real.shape[1]
+    high, low = split(jnp.concatenate([real, imag], axis=1))
+    terms[half, rows, pl.ds(0, side)] = high
+    terms[half, rows, pl.ds(side, side)] = low
 
 
 def moved(x, product):
@@ -103,12 +106,15 @@
     mine_out,
     near_out,
     far_out,
+    old_out,
     extended,
     gradient,
     sums,
     window,
     power,
-    far,
+    measured,
+    terms,
+    result,
     back,
     semaphores,
 ):
@@ -116,7 +122,7 @@
     half = side // 2
     tile_rows = object_hbm.shape[0]
     halo_rows = halo_hbm.shape[0]
-    per_row = object_out.shape[0] // (object_out.shape[0] // SUBLANES)
+    per_row = SUBLANES
     chunks = sums.shape[0]
     copies = [
         pltpu.make_async_copy(object_hbm, extended.at[pl.ds(0, tile_rows)], semaphores.at[0]),
@@ -135,6 +141,12 @@
         copy.wait()
     lane = lax.broadcasted_iota(jnp.int32, (side, LANES), 1)
     blocks = side // LANES
+    left, right = pl.ds(0, half), pl.ds(half, half)
+    pieces = [pl.ds(start, ROWS) for start in range(0, side, ROWS)]
+    streams = [range(start, min(start + 2, modes)) for start in range(0, modes, 2)]
+
+    def rows_of(stream):
+        return pl.ds(stream[0] * side, len(stream) * side)
 
     def slot(index, carry):
         row = place_ref[index, 0]
@@ -144,77 +156,101 @@
         back_shift = lax.rem(LANES - shift, LANES)
         last = per_row // 2 - 1
 
-        def rows_of(block, part):
+        def strided(block, part):
             at = row * per_row + jnp.minimum(first + block, last) * 2 + part
             return pl.ds(at, side, stride=per_row)
 
         for part in range(2):
             rolled = [
-                pltpu.roll(extended[rows_of(block, part), :], back_shift, 1)
-                for block in range(blocks + 1)
+                pltpu.roll(extended[strided(block, part), :], back_shift, 1) for block in range(blocks + 1)
             ]
             for block in range(blocks):
                 window[part, :, pl.ds(block * LANES, LANES)] = jnp.where(
                     lane < LANES - shift, rolled[block], rolled[block + 1]
                 )
-
-        for mode in range(modes):
-            w_r, w_i = window[0], window[1]
-            p_r, p_i = probe_ref[mode, 0], probe_ref[mode, 1]
-            e_r = p_r * w_r - p_i * w_i
-            e_i = p_r * w_i + p_i * w_r
-            plus = jnp.concatenate([e_r[:, :half] + e_r[:, half:], e_i[:, :half] + e_i[:, half:]], axis=1)
-            minus = jnp.concatenate([e_r[:, :half] - e_r[:, half:], e_i[:, :half] - e_i[:, half:]], axis=1)
-            even = by_lanes(plus, table_ref, 0)
-            odd = by_lanes(minus, table_ref, 1)
-            real = jnp.concatenate([even[:, :half], odd[:, :half]], axis=1)
-            imag = jnp.concatenate([even[:, half:], odd[:, half:]], axis=1)
-            plus = jnp.concatenate([real[:half] + real[half:], imag[:half] + imag[half:]], axis=0)
-            minus = jnp.concatenate([real[:half] - real[half:], imag[:half] - imag[half:]], axis=0)
-            far[mode, 0] = by_rows(plus, table_ref, 2)
-            far[mode, 1] = by_rows(minus, table_ref, 3)
-
         move = order_ref[0]
-        measured = moved(diffraction_ref[index], lambda terms: dot(
-            jnp.concatenate([order_ref[1]] * 3, axis=1), jnp.concatenate(terms, axis=0)
+        seen = moved(diffraction_ref[index], lambda bits: dot(
+            jnp.concatenate([order_ref[1]] * 3, axis=1), jnp.concatenate(bits, axis=0)
         ))
-        measured = moved(measured, lambda terms: dot(
-            jnp.concatenate(terms, axis=1), jnp.concatenate([move] * 3, axis=0)
+        seen = moved(seen, lambda bits: dot(
+            jnp.concatenate(bits, axis=1), jnp.concatenate([move] * 3, axis=0)
         ))
+        measured[...] = seen.T
+
+        for stream in streams:
+            for mode in stream:
+                for rows in pieces:
+                    w = [window[part, rows, side_] for part in range(2) for side_ in (left, right)]
+                    p = [probe_ref[mode, part, rows, side_] for part in range(2) for side_ in (left, right)]
+                    real = [p[k] * w[k] - p[2 + k] * w[2 + k] for k in range(2)]
+                    imag = [p[k] * w[2 + k] + p[2 + k] * w[k] for k in range(2)]
+                    start = mode * side + rows.start
+                    keep(terms, 0, start, real[0] + real[1], imag[0] + imag[1])
+                    keep(terms, 1, start, real[0] - real[1], imag[0] - imag[1])
+            transform(terms, rows_of(stream), table_ref, 0, result)
+        for stream in streams:
+            for mode in stream:
+                for odd in range(2):
+                    top, bottom = pl.ds(mode * side, half), pl.ds(mode * side + half, half)
+                    a = [result[odd, top, side_] for side_ in (left, right)]
+                    b = [result[odd, bottom, side_] for side_ in (left, right)]
+                    start = mode * side + odd * half
+                    keep(terms, 0, start, (a[0] + b[0]).T, (a[1] + b[1]).T)
+                    keep(terms, 1, start, (a[0] - b[0]).T, (a[1] - b[1]).T)
+            transform(terms, rows_of(stream), table_ref, 0, result)
         for odd in range(2):
-            seen = measured[odd * half : (odd + 1) * half]
-            intensity = jnp.zeros((half, side), jnp.float32)
-            for mode in range(modes):
-                re, im = far[mode, odd, pl.ds(0, half), :], far[mode, odd, pl.ds(half, half), :]
-                intensity = intensity + re * re + im * im
-            ratio = seen * lax.rsqrt(seen * jnp.maximum(intensity, 1.0))
-            for mode in range(modes):
-                far[mode, odd, pl.ds(0, half), :] = far[mode, odd, pl.ds(0, half), :] * ratio
-                far[mode, odd, pl.ds(half, half), :] = far[mode, odd, pl.ds(half, half), :] * ratio
-
-        back[0] = power[...] * window[0]
-        back[1] = power[...] * window[1]
-
-        for mode in range(modes):
-            even = by_rows(far[mode, 0], table_ref, 0)
-            odd = by_rows(far[mode, 1], table_ref, 1)
-            plus, minus = even + odd, even - odd
-            real = jnp.concatenate([plus[:half], minus[:half]], axis=0)
-            imag = jnp.concatenate([plus[half:], minus[half:]], axis=0)
-            even = by_lanes(jnp.concatenate([real[:, :half], imag[:, :half]], axis=1), table_ref, 2)
-            odd = by_lanes(jnp.concatenate([real[:, half:], imag[:, half:]], axis=1), table_ref, 3)
-            plus, minus = even + odd, even - odd
-            c_r = jnp.concatenate([plus[:, :half], minus[:, :half]], axis=1)
-            c_i = jnp.concatenate([plus[:, half:], minus[:, half:]], axis=1)
-            p_r, p_i = probe_ref[mode, 0], probe_ref[mode, 1]
-            back[0] = back[0] - (p_r * c_r + p_i * c_i)
-            back[1] = back[1] - (p_r * c_i - p_i * c_r)
-            w_r, w_i = window[0], window[1]
-            by_chunk = (chunks, SUBLANES, side)
-            sums[:, 2 * mode] += (w_r * c_r + w_i * c_i).reshape(by_chunk)
-            sums[:, 2 * mode + 1] += (w_r * c_i - w_i * c_r).reshape(by_chunk)
-        w_r, w_i = window[0], window[1]
-        sums[:, 2 * modes] += (w_r * w_r + w_i * w_i).reshape(chunks, SUBLANES, side)
+            for rows in pieces:
+                far = [
+                    [result[odd, pl.ds(mode * side + rows.start, ROWS), side_] for side_ in (left, right)]
+                    for mode in range(modes)
+                ]
+                intensity = jnp.zeros((ROWS, half), jnp.float32)
+                for real, imag in far:
+                    intensity = intensity + real * real + imag * imag
+                amount = measured[rows, pl.ds(odd * half, half)]
+                ratio = amount * lax.rsqrt(amount * jnp.maximum(intensity, 1.0))
+                for mode, (real, imag) in enumerate(far):
+                    keep(terms, odd, mode * side + rows.start, real * ratio, imag * ratio)
+        for stream in streams:
+            transform(terms, rows_of(stream), table_ref, 2, result)
+        for stream in streams:
+            for mode in stream:
+                for odd in range(2):
+                    rows = pl.ds(mode * side + odd * half, half)
+                    a = [result[0, rows, side_] for side_ in (left, right)]
+                    b = [result[1, rows, side_] for side_ in (left, right)]
+                    start = mode * side
+                    keep(terms, odd, start, (a[0] + b[0]).T, (a[1] + b[1]).T)
+                    keep(terms, odd, start + half, (a[0] - b[0]).T, (a[1] - b[1]).T)
+            transform(terms, rows_of(stream), table_ref, 2, result)
+        for number, stream in enumerate(streams):
+            for rows in pieces:
+                chunk = pl.ds(rows.start // SUBLANES, ROWS // SUBLANES)
+                by_chunk = (ROWS // SUBLANES, SUBLANES, half)
+                for lower, side_ in enumerate((left, right)):
+                    w_r, w_i = window[0, rows, side_], window[1, rows, side_]
+                    if number:
+                        g_r, g_i = back[0, rows, side_], back[1, rows, side_]
+                    else:
+                        strength = power[rows, side_]
+                        g_r, g_i = strength * w_r, strength * w_i
+                    for mode in stream:
+                        at = pl.ds(mode * side + rows.start, ROWS)
+                        if lower:
+                            c_r = result[0, at, left] - result[1, at, left]
+                            c_i = result[0, at, right] - result[1, at, right]
+                        else:
+                            c_r = result[0, at, left] + result[1, at, left]
+                            c_i = result[0, at, right] + result[1, at, right]
+                        p_r, p_i = probe_ref[mode, 0, rows, side_], probe_ref[mode, 1, rows, side_]
+                        g_r = g_r - (p_r * c_r + p_i * c_i)
+                        g_i = g_i - (p_r * c_i - p_i * c_r)
+                        sums[chunk, 2 * mode, :, side_] += (w_r * c_r + w_i * c_i).reshape(by_chunk)
+                        sums[chunk, 2 * mode + 1, :, side_] += (w_r * c_i - w_i * c_r).reshape(by_chunk)
+                    back[0, rows, side_] = g_r
+                    back[1, rows, side_] = g_i
+                    if not number:
+                        sums[chunk, 2 * modes, :, side_] += (w_r * w_r + w_i * w_i).reshape(by_chunk)
 
         for part in range(2):
             rolled = [
@@ -224,7 +260,7 @@
             for block in range(blocks + 1):
                 here = rolled[block] if block < blocks else zero
                 before = rolled[block - 1] if block else zero
-                at = rows_of(block, part)
+                at = strided(block, part)
                 gradient[at, :] = gradient[at, :] + jnp.where(lane >= shift, here, before)
         return carry
 
@@ -241,6 +277,10 @@
                 near_out[hop, step] = sums[(1 - core) * (chunks // 2) + at]
             else:
                 far_out[step] = sums[(1 - core) * (chunks // 2) + at]
+    start = pl.multiple_of(((core * groups + group) * layers + layer) * SUBLANES, SUBLANES)
+    for mode in range(modes):
+        for part in range(2):
+            old_out[2 * mode + part] = probe_ref[mode, part, pl.ds(start, SUBLANES), :]
 
 
 def gradient_step(place, count, here, tile, halo, probe, diffraction, groups, layers):
@@ -261,23 +301,57 @@
             jax.ShapeDtypeStruct((groups, layers, *chunk), f32),
             jax.ShapeDtypeStruct((groups - 1, layers, *chunk), f32),
             jax.ShapeDtypeStruct((layers, *chunk), f32),
+            jax.ShapeDtypeStruct((planes - 1, SUBLANES, side), f32),
         ),
-        in_specs=[smem, smem, smem, anywhere, anywhere, vmem, vmem, vmem, vmem],
-        out_specs=(vmem, vmem, vmem, vmem, vmem),
+        in_specs=[smem, smem, smem, pl.BlockSpec(memory_space=pltpu.HBM), anywhere, vmem, vmem, vmem, vmem],
+        out_specs=(vmem,) * 6,
         scratch_shapes=[
             pltpu.VMEM((tile.shape[0] + halo.shape[0], LANES), f32),
             pltpu.VMEM((tile.shape[0] + halo.shape[0], LANES), f32),
             pltpu.VMEM((chunks, *chunk), f32),
             pltpu.VMEM((2, side, side), f32),
             pltpu.VMEM((side, side), f32),
-            pltpu.VMEM((modes, 2, side, side), f32),
+            pltpu.VMEM((side, side), f32),
+            pltpu.VMEM((2, modes * side, 2 * side), jnp.bfloat16),
+            pltpu.VMEM((2, modes * side, side), f32),
             pltpu.VMEM((2, side, side), f32),
             pltpu.SemaphoreType.DMA((2,)),
         ],
-        compiler_params=pltpu.CompilerParams(vmem_limit_bytes=48 * 1024 * 1024),
+        compiler_params=pltpu.CompilerParams(vmem_limit_bytes=30 * 1024 * 1024),
         cost_estimate=pl.CostEstimate(flops=2 * products, bytes_accessed=16 << 20, transcendentals=0),
         name="gradient_step",
     )(place, count, here, tile, halo, probe, diffraction, jnp.asarray(tables(side)), jnp.asarray(parity_order(side)))
+
+
+def first_rows(tile, rows):
+    def kernel(tile_ref, out_ref, semaphore):
+        copy = pltpu.make_async_copy(tile_ref.at[pl.ds(0, rows)], out_ref, semaphore)
+        copy.start()
+        copy.wait()
+
+    return pl.pallas_call(
+        kernel,
+        out_shape=jax.ShapeDtypeStruct((rows, LANES), jnp.float32),
+        in_specs=[pl.BlockSpec(memory_space=pltpu.HBM)],
+        out_specs=pl.BlockSpec(memory_space=pl.ANY),
+        scratch_shapes=[pltpu.SemaphoreType.DMA],
+        compiler_params=pltpu.CompilerParams(vmem_limit_bytes=62 * 1024 * 1024),
+        name="first_rows",
+    )(tile)
+
+
+def divide_kernel(old_ref, *refs):
+    *parts, out_ref = refs
+    total = parts[0][...]
+    for part in parts[1:]:
+        total = total + part[...]
+    out_ref[...] = (EPSILON * old_ref[...] + total[:-1]) / (total[-1:] + EPSILON)
+
+
+def divided(old, parts):
+    return pl.pallas_call(
+        divide_kernel, out_shape=jax.ShapeDtypeStruct(old.shape, jnp.float32), name="divided"
+    )(old, *parts)
 
 
 def place_kernel(layers, pieces, here_ref, *refs):
@@ -316,7 +390,7 @@
     return lax.ppermute(block, "region", [(i, (i + 2 * step) % regions) for i in range(regions)])
 
 
-def probe_by_shards(probe, mine, near, far, here, layers, arrived):
+def probe_by_shards(probe, mine, near, far, old, here, layers, arrived):
     modes, parts, side, _ = probe.shape
     planes = modes * parts
     half = layers // 2
@@ -327,15 +401,10 @@
     near_sum = mine[:3] + other_near
     to_x = near_sum[1].at[half:].add(by_y)
     to_y = near_sum[2].at[:half].add(by_x)
-    summed = near_sum[0] + across(to_x, 1) + across(to_y, 2)
+    by_x, by_y = across(to_x, 1), across(to_y, 2)
+    summed = [near_sum[0, step] + by_x[step] + by_y[step] for step in range(layers)]
     summed, arrived = lax.optimization_barrier((summed, arrived))
-    total = summed[0]
-    for step in range(1, layers):
-        total = total + up_layers(summed[step], step)
-    core, group, layer = here[0, 0], here[0, 1], here[0, 2]
-    start = core * (side // 2) + (group * layers + layer) * SUBLANES
-    old = lax.dynamic_slice(probe.reshape(planes, side, side), (0, start, 0), (planes, SUBLANES, side))
-    fresh = (EPSILON * old + total[:-1]) / (total[-1:] + EPSILON)
+    fresh = divided(old, [summed[0]] + [up_layers(summed[step], step) for step in range(1, layers)])
     own = jnp.stack([fresh] + [up_layers(fresh, step) for step in range(1, layers)])
     x, y = across(own, 1), across(own, 2)
     arrays = [own, x, y, across(x[:half], 2), across(y[half:], 1)]
@@ -365,19 +434,19 @@
     layers = regions // 2
     sharded = groups == 4 and 2 * groups * layers * SUBLANES == side
     tile = packed(object_slab)
-    halo = shifted(tile[: side * per_row], "region", -1)
+    halo = shifted(first_rows(tile, side * per_row), "region", -1)
     place = positions - jnp.stack([region * tile_rows, jnp.zeros_like(region)])[None, :].astype(jnp.int32)
     if sharded:
         here = jnp.stack([region % 2, group, region // 2]).astype(jnp.int32).reshape(1, 3)
     else:
         here = jnp.zeros((1, 3), jnp.int32)
         groups, layers = 4, side // SUBLANES // 8
-    new_tile, spill, mine, near, far = gradient_step(
+    new_tile, spill, mine, near, far, old = gradient_step(
         place, slot_counts, here, tile, halo, probe, diffraction, groups, layers
     )
     arrived = shifted(spill, "region", 1)
     if sharded:
-        new_probe, arrived = probe_by_shards(probe, mine, near, far, here, layers, arrived)
+        new_probe, arrived = probe_by_shards(probe, mine, near, far, old, here, layers, arrived)
     else:
         new_probe = probe_from_whole(probe, mine, near, far)
     overlap = spill.shape[0]

time: 111 us -> 140 us (1.26)
  Pallas kernels: 20 us -> 50.2 us
  waiting for transfers between devices: 32.5 us -> 37.2 us
  other arithmetic: 4.67 us -> 2.12 us
  starting transfers between devices: 45.7 us -> 43.4 us
  between operations: 3.46 us -> 1.55 us
    pallas_call x0 -> x2, Pallas kernels: none -> 34.6 us  [the longest x1 32.9 us: first_rows(): pl.pallas_call(kernel, out_shape=jax.ShapeDtypeStruct((rows, LANES), jnp....]
    ppermute x8, starting transfers between devices: 23 us -> 6.81 us  [across(): lax.ppermute(block, 'group', [(i, i ^ hop) for i in range(lax.axis_size('...]
    ppermute x7, starting transfers between devices: 13.9 us -> 24.4 us  [from_partner(): lax.ppermute(block, 'region', [(i, i ^ 1) for i in range(lax.axis_size('r...]
    pallas_call x1, Pallas kernels: 17.9 us -> 13.7 us  [gradient_step(): pl.pallas_call(step_kernel, out_shape=(jax.ShapeDtypeStruct(tile.shape, f...]
    unnamed x13 -> x25, local copies, waits for them, and re-layouts: 1.07 us -> 5.19 us
    ppermute x8, waiting for transfers between devices: 18.9 us -> 23 us  [across(): lax.ppermute(block, 'group', [(i, i ^ hop) for i in range(lax.axis_size('...]
    slice x2 -> x0, local copies, waits for them, and re-layouts: 3.35 us -> none  [the longest x1 2.7 us: on_device(): halo = shifted(tile[:side * per_row], 'region', -1)]
    ppermute x6, starting transfers between devices: 5.42 us -> 8.77 us  [up_layers(): lax.ppermute(block, 'region', [(i, (i + 2 * step) % regions) for i in ran...]
  transfers between devices with their start and end apart: 23 -> 23, of which waited for: 14 -> 16; matrix products, arithmetic and copies ran while one was open for 3% -> 1% of each run, Pallas kernels for 0% -> 0%
where the time goes in v3:
time: 140 us
  Pallas kernels  50.2 us (36%)
  starting transfers between devices  43.4 us (31%)
  waiting for transfers between devices  37.2 us (27%)
  local copies, waits for them, and re-layouts  5.27 us (4%)
  other arithmetic  2.12 us (2%)
  between operations  1.55 us (1%)
    pallas_call x1, Pallas kernels, first_rows(): pl.pallas_call(kernel, out_shape=jax.ShapeDtypeStruct((rows, LANES), jnp....  32.9 us
    ppermute x7, starting transfers between devices, from_partner(): lax.ppermute(block, 'region', [(i, i ^ 1) for i in range(lax.axis_size('r...  24.4 us
    ppermute x8, waiting for transfers between devices, across(): lax.ppermute(block, 'group', [(i, i ^ hop) for i in range(lax.axis_size('...  23 us
    pallas_call x1, Pallas kernels, gradient_step(): pl.pallas_call(step_kernel, out_shape=(jax.ShapeDtypeStruct(tile.shape, f...  13.7 us
    ppermute x6, waiting for transfers between devices, up_layers(): lax.ppermute(block, 'region', [(i, (i + 2 * step) % regions) for i in ran...  9.34 us
    ppermute x6, starting transfers between devices, up_layers(): lax.ppermute(block, 'region', [(i, (i + 2 * step) % regions) for i in ran...  8.77 us
    ppermute x8, starting transfers between devices, across(): lax.ppermute(block, 'group', [(i, i ^ hop) for i in range(lax.axis_size('...  6.81 us
    unnamed x25, local copies, waits for them, and re-layouts  5.19 us
  transfers between devices with their start and end apart: 23, of which 16 were waited for; matrix products, arithmetic and copies ran while one was open for 1% of the time, Pallas kernels for 0%

profile of v3, /device:TPU:0, one launch (start us, length us, event | category | flops | bytes accessed | tf_op | source)
XLA Modules:
  0.0 139.7 jit_solution(17079830225245887922)
XLA Ops:
  0.6 0.0 copy-start.5
  0.7 32.9 %first_rows.1 = f32[2048,128]{1,0:T(8,128)} custom-call(f32[4096,128]{1,0:T(8,128)} %bitcast.95), custom_call_target="tpu_custom_call" | custom-call | tf_op jit(solution)/shard_map/first_rows/pallas_call | solution.py:332
  33.5 1.3 collective-permute-start
  35.5 0.1 copy.9
  35.6 0.1 pad_add_fusion
  35.7 0.1 add_bitcast_fusion.here_ref
  35.8 2.5 %collective-permute-done.halo_hbm = f32[2048,128]{1,0:T(8,128)S(1)} collective-permute-done((f32[2048,128]{1,0:T(8,128)}, f32[2048,128]{1,0:T(8,128)S(1)}, u32[]{:S(2)}, u32[]{:S(2)}) %collective-permute-start) | collective-permute-done | bytes 1048608 | tf_op jit(solution)/shard_map/ppermute | solution.py:21
  38.3 1.6 %copy-done = f32[512,2,512]{2,1,0:T(2,128)S(1)} copy-done((f32[512,2,512]{2,1,0:T(2,128)S(1)}, f32[512,2,512]{2,1,0:T(2,128)}, u32[]{:S(2)}) %copy-start) | copy-done | bytes 2097176
  39.9 1.6 %copy-done.2 = f32[4,2,256,256]{3,2,1,0:T(8,128)S(1)} copy-done((f32[4,2,256,256]{3,2,1,0:T(8,128)S(1)}, f32[4,2,256,256]{3,2,1,0:T(8,128)}, u32[]{:S(2)}) %copy-start.2) | copy-done | bytes 2097176
  41.5 1.2 copy-done.4
  42.7 13.7 %gradient_step.1 = (f32[4096,128]{1,0:T(8,128)}, f32[2048,128]{1,0:T(8,128)S(1)}, f32[4,4,9,8,256]{4,3,2,1,0:T(8,128)S(1)}, f32[3,4,9,8,256]{4,3,2,1,0:T(8,128)S...) custom-call(s32[4,2]{1,0:T(4,128)S(1)} %broadcast_subtract_fusion.place_ref, s32[1,1]{1,0:T(1,128)S(6)} %copy.15.count_ref, ...), custom_call_target="tpu_custom_call" | custom-call | flops 25769803776 | bytes 16777216 | tf_op jit(solution)/shard_map/gradient_step/pallas_call | solution.py:296
  56.4 23.4 %collective-permute-start.1 = (f32[4,9,8,256]{3,2,1,0:T(8,128)S(1)}, f32[4,9,8,256]{3,2,1,0:T(8,128)S(1)}, u32[]{:S(2)}, u32[]{:S(2)}) collective-permute-start(f32[4,9,8,256]{3,2,1,0:T(8,128)S(1)} %get-tuple-element.42), channel_id=1, source_target_pairs={{0,4},{4,0},{8,12},{12,8},{16,20},{20,16},{24,28},{28,24},{1,5},{5... | collective-permute-start | bytes 884744 | tf_op jit(solution)/shard_map/ppermute | solution.py:385
  79.8 1.2 collective-permute-done.1
  81.0 0.4 collective-permute-start.2
  81.4 2.1 %collective-permute-start.7 = (f32[2048,128]{1,0:T(8,128)S(1)}, f32[2048,128]{1,0:T(8,128)S(1)}, u32[]{:S(2)}, u32[]{:S(2)}) collective-permute-start(f32[2048,128]{1,0:T(8,128)S(1)} %get-tuple-element.45), channel_id=1, source_target_pairs={{0,4},{4,8},{8,12},{12,16},{16,20},{20,24},{24,28},{1,5},{5,9},{9,... | collective-permute-start | bytes 3145736 | tf_op jit(solution)/shard_map/ppermute | solution.py:21
  83.6 0.1 collective-permute-start.3
  83.6 0.1 collective-permute-start.5
  83.7 0.0 collective-permute-done.2
  83.7 0.1 slice_add_fusion
  83.8 0.0 copy-start.6
  83.9 6.0 %collective-permute-done.3 = f32[2,9,8,256]{3,2,1,0:T(8,128)S(1)} collective-permute-done((f32[2,9,8,256]{3,2,1,0:T(8,128)S(1)}, f32[2,9,8,256]{3,2,1,0:T(8,128)S(1)}, u32[]{:S(2)}, u32[]{:S(2)}) %collective-permute-start.3) | collective-permute-done | bytes 147488 | tf_op jit(solution)/shard_map/ppermute | solution.py:381
  89.9 0.1 collective-permute-done.5
  90.0 0.1 collective-permute-start.4
  90.1 2.2 %collective-permute-start.6 = (f32[4,9,8,256]{3,2,1,0:T(8,128)S(1)}, f32[4,9,8,256]{3,2,1,0:T(8,128)S(1)}, u32[]{:S(2)}, u32[]{:S(2)}) collective-permute-start(f32[4,9,8,256]{3,2,1,0:T(8,128)S(1)} %get-tuple-element.57), channel_id=1, source_target_pairs={{0,2},{1,3},{2,0},{3,1},{4,6},{5,7},{6,4},{7,5},{8,10},{9,11},{10,... | collective-permute-start | bytes 884744 | tf_op jit(solution)/shard_map/ppermute | solution.py:381
  92.3 6.9 %collective-permute-done.4 = f32[4,9,8,256]{3,2,1,0:T(8,128)S(1)} collective-permute-done((f32[4,9,8,256]{3,2,1,0:T(8,128)S(1)}, f32[4,9,8,256]{3,2,1,0:T(8,128)S(1)}, u32[]{:S(2)}, u32[]{:S(2)}) %collective-permute-start.4) | collective-permute-done | bytes 294944 | tf_op jit(solution)/shard_map/ppermute | solution.py:381
  99.3 0.3 collective-permute-done.6
  99.6 0.7 fusion.4
  100.3 0.0 collective-permute-done.7
  100.3 1.4 collective-permute-start.8
  101.7 1.1 collective-permute-start.9
  102.8 2.9 %collective-permute-start.10 = (f32[9,8,256]{2,1,0:T(8,128)S(1)}, f32[9,8,256]{2,1,0:T(8,128)S(1)}, u32[]{:S(2)}, u32[]{:S(2)}) collective-permute-start(f32[9,8,256]{2,1,0:T(8,128)S(1)} %get-tuple-element.51), channel_id=1, source_target_pairs={{0,24},{4,28},{8,0},{12,4},{16,8},{20,12},{24,16},{28,20},{1,25},{... | collective-permute-start | bytes 221192 | tf_op jit(solution)/shard_map/ppermute | solution.py:390
  105.7 1.5 %collective-permute-done.8.refs_1_ = f32[9,8,256]{2,1,0:T(8,128)S(1)} collective-permute-done((f32[9,8,256]{2,1,0:T(8,128)S(1)}, f32[9,8,256]{2,1,0:T(8,128)S(1)}, u32[]{:S(2)}, u32[]{:S(2)}) %collective-permute-start.8) | collective-permute-done | bytes 73760 | tf_op jit(solution)/shard_map/ppermute | solution.py:390
  107.3 2.1 %collective-permute-done.9.refs_2_ = f32[9,8,256]{2,1,0:T(8,128)S(1)} collective-permute-done((f32[9,8,256]{2,1,0:T(8,128)S(1)}, f32[9,8,256]{2,1,0:T(8,128)S(1)}, u32[]{:S(2)}, u32[]{:S(2)}) %collective-permute-start.9) | collective-permute-done | bytes 73760 | tf_op jit(solution)/shard_map/ppermute | solution.py:390
  109.4 0.0 collective-permute-done.10.refs_3_
  109.4 0.6 copy-done.9
  110.0 0.0 copy-done.10
  110.0 1.7 %divided.1 = f32[8,8,256]{2,1,0:T(8,128)} custom-call(f32[8,8,256]{2,1,0:T(8,128)} %copy-done.1, f32[9,8,256]{2,1,0:T(8,128)} %get-tuple-element.48.refs_0_, f32[9,8,256]{2,1,0:T(8,128)} %copy-done.8, f32[9,8,256]{2,1,0:T(8,128)} %copy-done.9, f32[9,8,256]{2,1,0:T(8,128)} %copy-done.10), custom_call_target="tpu_custom_call" | custom-call | tf_op jit(solution)/shard_map/divided/pallas_call | solution.py:352
  111.7 2.8 %collective-permute-start.13 = (f32[8,8,256]{2,1,0:T(8,128)}, f32[8,8,256]{2,1,0:T(8,128)S(1)}, u32[]{:S(2)}, u32[]{:S(2)}) collective-permute-start(f32[8,8,256]{2,1,0:T(8,128)} %divided.1), channel_id=1, source_target_pairs={{0,24},{4,28},{8,0},{12,4},{16,8},{20,12},{24,16},{28,20},{1,25},{... | collective-permute-start | bytes 196616 | tf_op jit(solution)/shard_map/ppermute | solution.py:390
  114.5 0.0 collective-permute-start.12
  114.5 0.5 collective-permute-start.11
  115.0 1.7 %collective-permute-done.13 = f32[8,8,256]{2,1,0:T(8,128)S(1)} collective-permute-done((f32[8,8,256]{2,1,0:T(8,128)}, f32[8,8,256]{2,1,0:T(8,128)S(1)}, u32[]{:S(2)}, u32[]{:S(2)}) %collective-permute-start.13) | collective-permute-done | bytes 65568 | tf_op jit(solution)/shard_map/ppermute | solution.py:390
  116.7 3.2 %collective-permute-done.12 = f32[8,8,256]{2,1,0:T(8,128)S(1)} collective-permute-done((f32[8,8,256]{2,1,0:T(8,128)}, f32[8,8,256]{2,1,0:T(8,128)S(1)}, u32[]{:S(2)}, u32[]{:S(2)}) %collective-permute-start.12) | collective-permute-done | bytes 65568 | tf_op jit(solution)/shard_map/ppermute | solution.py:390
  119.8 0.9 collective-permute-done.11
  120.8 0.9 pad_maximum_fusion.refs_0_
  121.6 1.9 %collective-permute-start.15 = (f32[4,8,8,256]{3,2,1,0:T(8,128)S(1)}, f32[4,8,8,256]{3,2,1,0:T(8,128)S(1)}, u32[]{:S(2)}, u32[]{:S(2)}) collective-permute-start(f32[4,8,8,256]{3,2,1,0:T(8,128)S(1)} %pad_maximum_fusion.refs_0_), channel_id=1, source_target_pairs={{0,2},{1,3},{2,0},{3,1},{4,6},{5,7},{6,4},{7,5},{8,10},{9,11},{10,... | collective-permute-start | bytes 786440 | tf_op jit(solution)/shard_map/ppermute | solution.py:381
  123.6 0.7 collective-permute-start.14
  124.3 3.9 %collective-permute-done.15.refs_2_ = f32[4,8,8,256]{3,2,1,0:T(8,128)S(1)} collective-permute-done((f32[4,8,8,256]{3,2,1,0:T(8,128)S(1)}, f32[4,8,8,256]{3,2,1,0:T(8,128)S(1)}, u32[]{:S(2)}, u32[]{:S(2)}) %collective-permute-start.15) | collective-permute-done | bytes 262176 | tf_op jit(solution)/shard_map/ppermute | solution.py:381
  128.2 1.6 %collective-permute-start.17 = (f32[2,8,8,256]{3,2,1,0:T(8,128)S(1)}, f32[2,8,8,256]{3,2,1,0:T(8,128)S(1)}, u32[]{:S(2)}, u32[]{:S(2)}) collective-permute-start(f32[2,8,8,256]{3,2,1,0:T(8,128)S(1)} %slice.165), channel_id=1, source_target_pairs={{0,1},{1,0},{2,3},{3,2},{4,5},{5,4},{6,7},{7,6},{8,9},{9,8},{10,11... | collective-permute-start | bytes 393224 | tf_op jit(solution)/shard_map/ppermute | solution.py:381
  129.8 1.5 %collective-permute-done.14.refs_1_ = f32[4,8,8,256]{3,2,1,0:T(8,128)S(1)} collective-permute-done((f32[4,8,8,256]{3,2,1,0:T(8,128)S(1)}, f32[4,8,8,256]{3,2,1,0:T(8,128)S(1)}, u32[]{:S(2)}, u32[]{:S(2)}) %collective-permute-start.14) | collective-permute-done | bytes 262176 | tf_op jit(solution)/shard_map/ppermute | solution.py:381
  131.3 0.1 collective-permute-start.16
  131.4 0.1 collective-permute-start.18
  131.5 0.5 collective-permute-start.20
  132.0 0.1 collective-permute-start.19
  132.0 1.2 collective-permute-done.17.refs_4_
  133.2 0.0 collective-permute-start.22
  133.2 3.1 %collective-permute-done.16.refs_3_ = f32[2,8,8,256]{3,2,1,0:T(8,128)S(1)} collective-permute-done((f32[2,8,8,256]{3,2,1,0:T(8,128)S(1)}, f32[2,8,8,256]{3,2,1,0:T(8,128)S(1)}, u32[]{:S(2)}, u32[]{:S(2)}) %collective-permute-start.16) | collective-permute-done | bytes 131104 | tf_op jit(solution)/shard_map/ppermute | solution.py:381
  136.3 0.0 collective-permute-start.21
  136.3 0.2 subtract_dynamic-update-slice_fusion
  136.6 0.0 copy-start.7
  136.6 0.0 collective-permute-done.18.refs_5_
  136.6 0.0 collective-permute-done.20.refs_7_
  136.6 0.0 collective-permute-done.19.refs_6_
  136.6 1.1 collective-permute-done.21.refs_8_
  137.7 2.0 %put_in_place.1 = f32[8,32,8,256]{3,2,1,0:T(8,128)} custom-call(s32[1,3]{1,0:T(1,128)S(1)} %add_bitcast_fusion.here_ref, f32[4,8,8,256]{3,2,1,0:T(8,128)S(1)} %pad_maximum_fusion.refs_0_, f32[4,8,8,256]{3,2,1,0:T(8,128)S(1)} %collective-permute-done.14.refs_1_, f32[4,8,8,256]{3,2,1,0:T(8,128)S(1)} %collective-permute-done.15.refs_2_, ...), custom_call_target="tpu_custom_call" | custom-call | bytes 4194304 | tf_op jit(solution)/shard_map/put_in_place/pallas_call | solution.py:369
  (24 shorter events, 0.2 us)
Async XLA Ops:
  0.6 37.7 %copy-start.5 = (bf16[2,256,256]{2,1,0:T(8,128)(2,1)S(1)}, bf16[2,256,256]{2,1,0:T(8,128)(2,1)}, u32[]{:S(2)}) copy-start(bf16[2,256,256]{2,1,0:T(8,128)(2,1)} %constant.97.clone.order_ref) | copy-start | bytes 786436
  0.6 34.9 %copy-start.11 = (s32[4,2]{0,1:T(2,128)S(1)}, s32[4,2]{0,1:T(2,128)}, u32[]{:S(2)}) copy-start(s32[4,2]{0,1:T(2,128)} %param.14) | copy-start | bytes 100
  0.7 37.7 %copy-start.3 = (f32[4,256,256]{2,1,0:T(8,128)S(1)}, f32[4,256,256]{2,1,0:T(8,128)}, u32[]{:S(2)}) copy-start(f32[4,256,256]{2,1,0:T(8,128)} %diffraction_ref.1) | copy-start | bytes 3145732
  33.5 4.8 %collective-permute-start = (f32[2048,128]{1,0:T(8,128)}, f32[2048,128]{1,0:T(8,128)S(1)}, u32[]{:S(2)}, u32[]{:S(2)}) collective-permute-start(f32[2048,128]{1,0:T(8,128)} %first_rows.1), channel_id=1, source_target_pairs={{4,0},{8,4},{12,8},{16,12},{20,16},{24,20},{28,24},{5,1},{9,5},{13... | collective-permute-start | bytes 3145736 | tf_op jit(solution)/shard_map/ppermute | solution.py:21
  38.3 1.6 %copy-start = (f32[512,2,512]{2,1,0:T(2,128)S(1)}, f32[512,2,512]{2,1,0:T(2,128)}, u32[]{:S(2)}) copy-start(f32[512,2,512]{2,1,0:T(2,128)} %param.11) | copy-start | bytes 6291460
  39.9 1.6 %copy-start.2 = (f32[4,2,256,256]{3,2,1,0:T(8,128)S(1)}, f32[4,2,256,256]{3,2,1,0:T(8,128)}, u32[]{:S(2)}) copy-start(f32[4,2,256,256]{3,2,1,0:T(8,128)} %probe_ref.1) | copy-start | bytes 6291460
  41.5 1.2 copy-start.4
  56.4 27.5 %copy-start.1 = (f32[8,8,256]{2,1,0:T(8,128)}, f32[8,8,256]{2,1,0:T(8,128)S(1)}, u32[]{:S(2)}) copy-start(f32[8,8,256]{2,1,0:T(8,128)S(1)} %get-tuple-element.47.old_ref) | copy-start | bytes 196612
  56.4 24.6 %collective-permute-start.1 = (f32[4,9,8,256]{3,2,1,0:T(8,128)S(1)}, f32[4,9,8,256]{3,2,1,0:T(8,128)S(1)}, u32[]{:S(2)}, u32[]{:S(2)}) collective-permute-start(f32[4,9,8,256]{3,2,1,0:T(8,128)S(1)} %get-tuple-element.42), channel_id=1, source_target_pairs={{0,4},{4,0},{8,12},{12,8},{16,20},{20,16},{24,28},{28,24},{1,5},{5... | collective-permute-start | bytes 884744 | tf_op jit(solution)/shard_map/ppermute | solution.py:385
  81.0 2.7 %collective-permute-start.2 = (f32[3,4,9,8,256]{4,3,2,1,0:T(8,128)S(1)}, f32[3,4,9,8,256]{4,3,2,1,0:T(8,128)S(1)}, u32[]{:S(2)}, u32[]{:S(2)}) collective-permute-start(f32[3,4,9,8,256]{4,3,2,1,0:T(8,128)S(1)} %get-tuple-element.43), channel_id=1, source_target_pairs={{0,4},{4,0},{8,12},{12,8},{16,20},{20,16},{24,28},{28,24},{1,5},{5... | collective-permute-start | bytes 2654216 | tf_op jit(solution)/shard_map/ppermute | solution.py:385
  81.4 18.9 %collective-permute-start.7 = (f32[2048,128]{1,0:T(8,128)S(1)}, f32[2048,128]{1,0:T(8,128)S(1)}, u32[]{:S(2)}, u32[]{:S(2)}) collective-permute-start(f32[2048,128]{1,0:T(8,128)S(1)} %get-tuple-element.45), channel_id=1, source_target_pairs={{0,4},{4,8},{8,12},{12,16},{16,20},{20,24},{24,28},{1,5},{5,9},{9,... | collective-permute-start | bytes 3145736 | tf_op jit(solution)/shard_map/ppermute | solution.py:21
  83.6 6.3 %collective-permute-start.3 = (f32[2,9,8,256]{3,2,1,0:T(8,128)S(1)}, f32[2,9,8,256]{3,2,1,0:T(8,128)S(1)}, u32[]{:S(2)}, u32[]{:S(2)}) collective-permute-start(f32[2,9,8,256]{3,2,1,0:T(8,128)S(1)} %get-tuple-element.60), channel_id=1, source_target_pairs={{0,2},{1,3},{2,0},{3,1},{4,6},{5,7},{6,4},{7,5},{8,10},{9,11},{10,... | collective-permute-start | bytes 442376 | tf_op jit(solution)/shard_map/ppermute | solution.py:381
  83.6 6.3 %collective-permute-start.5 = (f32[2,9,8,256]{3,2,1,0:T(8,128)S(1)}, f32[2,9,8,256]{3,2,1,0:T(8,128)S(1)}, u32[]{:S(2)}, u32[]{:S(2)}) collective-permute-start(f32[2,9,8,256]{3,2,1,0:T(8,128)S(1)} %get-tuple-element.61), channel_id=1, source_target_pairs={{0,1},{1,0},{2,3},{3,2},{4,5},{5,4},{6,7},{7,6},{8,9},{9,8},{10,11... | collective-permute-start | bytes 442376 | tf_op jit(solution)/shard_map/ppermute | solution.py:381
  83.8 52.5 %copy-start.6 = (f32[4096,128]{1,0:T(8,128)S(1)}, f32[4096,128]{1,0:T(8,128)}, u32[]{:S(2)}) copy-start(f32[4096,128]{1,0:T(8,128)} %get-tuple-element.39) | copy-start | bytes 6291460
  90.0 9.2 %collective-permute-start.4 = (f32[4,9,8,256]{3,2,1,0:T(8,128)S(1)}, f32[4,9,8,256]{3,2,1,0:T(8,128)S(1)}, u32[]{:S(2)}, u32[]{:S(2)}) collective-permute-start(f32[4,9,8,256]{3,2,1,0:T(8,128)S(1)} %get-tuple-element.56), channel_id=1, source_target_pairs={{0,1},{1,0},{2,3},{3,2},{4,5},{5,4},{6,7},{7,6},{8,9},{9,8},{10,11... | collective-permute-start | bytes 884744 | tf_op jit(solution)/shard_map/ppermute | solution.py:381
  90.1 9.5 %collective-permute-start.6 = (f32[4,9,8,256]{3,2,1,0:T(8,128)S(1)}, f32[4,9,8,256]{3,2,1,0:T(8,128)S(1)}, u32[]{:S(2)}, u32[]{:S(2)}) collective-permute-start(f32[4,9,8,256]{3,2,1,0:T(8,128)S(1)} %get-tuple-element.57), channel_id=1, source_target_pairs={{0,2},{1,3},{2,0},{3,1},{4,6},{5,7},{6,4},{7,5},{8,10},{9,11},{10,... | collective-permute-start | bytes 884744 | tf_op jit(solution)/shard_map/ppermute | solution.py:381
  100.3 7.0 %collective-permute-start.8 = (f32[9,8,256]{2,1,0:T(8,128)S(1)}, f32[9,8,256]{2,1,0:T(8,128)S(1)}, u32[]{:S(2)}, u32[]{:S(2)}) collective-permute-start(f32[9,8,256]{2,1,0:T(8,128)S(1)} %get-tuple-element.49), channel_id=1, source_target_pairs={{0,8},{4,12},{8,16},{12,20},{16,24},{20,28},{24,0},{28,4},{1,9},{5... | collective-permute-start | bytes 221192 | tf_op jit(solution)/shard_map/ppermute | solution.py:390
  101.7 7.7 %collective-permute-start.9 = (f32[9,8,256]{2,1,0:T(8,128)S(1)}, f32[9,8,256]{2,1,0:T(8,128)S(1)}, u32[]{:S(2)}, u32[]{:S(2)}) collective-permute-start(f32[9,8,256]{2,1,0:T(8,128)S(1)} %get-tuple-element.50), channel_id=1, source_target_pairs={{0,16},{4,20},{8,24},{12,28},{16,0},{20,4},{24,8},{28,12},{1,17},{... | collective-permute-start | bytes 221192 | tf_op jit(solution)/shard_map/ppermute | solution.py:390
  102.8 6.5 %collective-permute-start.10 = (f32[9,8,256]{2,1,0:T(8,128)S(1)}, f32[9,8,256]{2,1,0:T(8,128)S(1)}, u32[]{:S(2)}, u32[]{:S(2)}) collective-permute-start(f32[9,8,256]{2,1,0:T(8,128)S(1)} %get-tuple-element.51), channel_id=1, source_target_pairs={{0,24},{4,28},{8,0},{12,4},{16,8},{20,12},{24,16},{28,20},{1,25},{... | collective-permute-start | bytes 221192 | tf_op jit(solution)/shard_map/ppermute | solution.py:390
  107.3 2.1 %copy-start.8 = (f32[9,8,256]{2,1,0:T(8,128)}, f32[9,8,256]{2,1,0:T(8,128)S(1)}, u32[]{:S(2)}) copy-start(f32[9,8,256]{2,1,0:T(8,128)S(1)} %collective-permute-done.8.refs_1_) | copy-start | bytes 221188
  109.4 0.6 copy-start.9
  109.4 0.7 copy-start.10
  111.7 5.0 %collective-permute-start.13 = (f32[8,8,256]{2,1,0:T(8,128)}, f32[8,8,256]{2,1,0:T(8,128)S(1)}, u32[]{:S(2)}, u32[]{:S(2)}) collective-permute-start(f32[8,8,256]{2,1,0:T(8,128)} %divided.1), channel_id=1, source_target_pairs={{0,24},{4,28},{8,0},{12,4},{16,8},{20,12},{24,16},{28,20},{1,25},{... | collective-permute-start | bytes 196616 | tf_op jit(solution)/shard_map/ppermute | solution.py:390
  114.5 5.4 %collective-permute-start.12 = (f32[8,8,256]{2,1,0:T(8,128)}, f32[8,8,256]{2,1,0:T(8,128)S(1)}, u32[]{:S(2)}, u32[]{:S(2)}) collective-permute-start(f32[8,8,256]{2,1,0:T(8,128)} %divided.1), channel_id=1, source_target_pairs={{0,16},{4,20},{8,24},{12,28},{16,0},{20,4},{24,8},{28,12},{1,17},{... | collective-permute-start | bytes 196616 | tf_op jit(solution)/shard_map/ppermute | solution.py:390
  114.5 6.3 %collective-permute-start.11 = (f32[8,8,256]{2,1,0:T(8,128)}, f32[8,8,256]{2,1,0:T(8,128)S(1)}, u32[]{:S(2)}, u32[]{:S(2)}) collective-permute-start(f32[8,8,256]{2,1,0:T(8,128)} %divided.1), channel_id=1, source_target_pairs={{0,8},{4,12},{8,16},{12,20},{16,24},{20,28},{24,0},{28,4},{1,9},{5... | collective-permute-start | bytes 196616 | tf_op jit(solution)/shard_map/ppermute | solution.py:390
  121.6 6.5 %collective-permute-start.15 = (f32[4,8,8,256]{3,2,1,0:T(8,128)S(1)}, f32[4,8,8,256]{3,2,1,0:T(8,128)S(1)}, u32[]{:S(2)}, u32[]{:S(2)}) collective-permute-start(f32[4,8,8,256]{3,2,1,0:T(8,128)S(1)} %pad_maximum_fusion.refs_0_), channel_id=1, source_target_pairs={{0,2},{1,3},{2,0},{3,1},{4,6},{5,7},{6,4},{7,5},{8,10},{9,11},{10,... | collective-permute-start | bytes 786440 | tf_op jit(solution)/shard_map/ppermute | solution.py:381
  123.6 7.7 %collective-permute-start.14 = (f32[4,8,8,256]{3,2,1,0:T(8,128)S(1)}, f32[4,8,8,256]{3,2,1,0:T(8,128)S(1)}, u32[]{:S(2)}, u32[]{:S(2)}) collective-permute-start(f32[4,8,8,256]{3,2,1,0:T(8,128)S(1)} %pad_maximum_fusion.refs_0_), channel_id=1, source_target_pairs={{0,1},{1,0},{2,3},{3,2},{4,5},{5,4},{6,7},{7,6},{8,9},{9,8},{10,11... | collective-permute-start | bytes 786440 | tf_op jit(solution)/shard_map/ppermute | solution.py:381
  128.2 5.0 %collective-permute-start.17 = (f32[2,8,8,256]{3,2,1,0:T(8,128)S(1)}, f32[2,8,8,256]{3,2,1,0:T(8,128)S(1)}, u32[]{:S(2)}, u32[]{:S(2)}) collective-permute-start(f32[2,8,8,256]{3,2,1,0:T(8,128)S(1)} %slice.165), channel_id=1, source_target_pairs={{0,1},{1,0},{2,3},{3,2},{4,5},{5,4},{6,7},{7,6},{8,9},{9,8},{10,11... | collective-permute-start | bytes 393224 | tf_op jit(solution)/shard_map/ppermute | solution.py:381
  131.3 5.0 %collective-permute-start.16 = (f32[2,8,8,256]{3,2,1,0:T(8,128)S(1)}, f32[2,8,8,256]{3,2,1,0:T(8,128)S(1)}, u32[]{:S(2)}, u32[]{:S(2)}) collective-permute-start(f32[2,8,8,256]{3,2,1,0:T(8,128)S(1)} %slice.164), channel_id=1, source_target_pairs={{0,2},{1,3},{2,0},{3,1},{4,6},{5,7},{6,4},{7,5},{8,10},{9,11},{10,... | collective-permute-start | bytes 393224 | tf_op jit(solution)/shard_map/ppermute | solution.py:381
  131.4 5.2 %collective-permute-start.18 = (f32[4,8,8,256]{3,2,1,0:T(8,128)S(1)}, f32[4,8,8,256]{3,2,1,0:T(8,128)S(1)}, u32[]{:S(2)}, u32[]{:S(2)}) collective-permute-start(f32[4,8,8,256]{3,2,1,0:T(8,128)S(1)} %pad_maximum_fusion.refs_0_), channel_id=1, source_target_pairs={{0,4},{4,0},{8,12},{12,8},{16,20},{20,16},{24,28},{28,24},{1,5},{5... | collective-permute-start | bytes 786440 | tf_op jit(solution)/shard_map/ppermute | solution.py:385
  131.5 5.1 %collective-permute-start.20 = (f32[4,8,8,256]{3,2,1,0:T(8,128)S(1)}, f32[4,8,8,256]{3,2,1,0:T(8,128)S(1)}, u32[]{:S(2)}, u32[]{:S(2)}) collective-permute-start(f32[4,8,8,256]{3,2,1,0:T(8,128)S(1)} %collective-permute-done.15.refs_2_), channel_id=1, source_target_pairs={{0,4},{4,0},{8,12},{12,8},{16,20},{20,16},{24,28},{28,24},{1,5},{5... | collective-permute-start | bytes 786440 | tf_op jit(solution)/shard_map/ppermute | solution.py:385
  132.0 4.6 %collective-permute-start.19 = (f32[4,8,8,256]{3,2,1,0:T(8,128)S(1)}, f32[4,8,8,256]{3,2,1,0:T(8,128)S(1)}, u32[]{:S(2)}, u32[]{:S(2)}) collective-permute-start(f32[4,8,8,256]{3,2,1,0:T(8,128)S(1)} %collective-permute-done.14.refs_1_), channel_id=1, source_target_pairs={{0,4},{4,0},{8,12},{12,8},{16,20},{20,16},{24,28},{28,24},{1,5},{5... | collective-permute-start | bytes 786440 | tf_op jit(solution)/shard_map/ppermute | solution.py:385
  133.2 3.4 %collective-permute-start.22 = (f32[2,8,8,256]{3,2,1,0:T(8,128)S(1)}, f32[2,8,8,256]{3,2,1,0:T(8,128)S(1)}, u32[]{:S(2)}, u32[]{:S(2)}) collective-permute-start(f32[2,8,8,256]{3,2,1,0:T(8,128)S(1)} %collective-permute-done.17.refs_4_), channel_id=1, source_target_pairs={{0,4},{4,0},{8,12},{12,8},{16,20},{20,16},{24,28},{28,24},{1,5},{5... | collective-permute-start | bytes 393224 | tf_op jit(solution)/shard_map/ppermute | solution.py:385
  136.3 1.3 collective-permute-start.21
  136.6 3.1 %copy-start.7 = (f32[4096,128]{1,0:T(8,128)}, f32[4096,128]{1,0:T(8,128)S(1)}, u32[]{:S(2)}) copy-start(f32[4096,128]{1,0:T(8,128)S(1)} %subtract_dynamic-update-slice_fusion) | copy-start | bytes 6291460

commit v4 on v3

--- a/solution.py
+++ b/solution.py
@@ -91,54 +91,26 @@
     return product([first, *split(rest)])
 
 
-def step_kernel(
+def all_slots(
+    local,
+    tile_rows,
     place_ref,
     count_ref,
-    here_ref,
-    object_hbm,
-    halo_hbm,
     probe_ref,
-    diffraction_ref,
     table_ref,
-    order_ref,
-    object_out,
-    spill_out,
-    mine_out,
-    near_out,
-    far_out,
-    old_out,
     extended,
     gradient,
     sums,
-    window,
     power,
     measured,
+    window,
     terms,
     result,
     back,
-    semaphores,
 ):
     modes, _, side, _ = probe_ref.shape
     half = side // 2
-    tile_rows = object_hbm.shape[0]
-    halo_rows = halo_hbm.shape[0]
     per_row = SUBLANES
-    chunks = sums.shape[0]
-    copies = [
-        pltpu.make_async_copy(object_hbm, extended.at[pl.ds(0, tile_rows)], semaphores.at[0]),
-        pltpu.make_async_copy(halo_hbm, extended.at[pl.ds(tile_rows, halo_rows)], semaphores.at[1]),
-    ]
-    for copy in copies:
-        copy.start()
-    gradient[...] = jnp.zeros_like(gradient)
-    sums[...] = jnp.zeros_like(sums)
-    total = jnp.zeros((side, side), jnp.float32)
-    for mode in range(modes):
-        total = total + probe_ref[mode, 0] * probe_ref[mode, 0] + probe_ref[mode, 1] * probe_ref[mode, 1]
-    power[...] = total
-    scale = 1.0 / jnp.max(total)
-    for copy in copies:
-        copy.wait()
     lane = lax.broadcasted_iota(jnp.int32, (side, LANES), 1)
     blocks = side // LANES
     left, right = pl.ds(0, half), pl.ds(half, half)
@@ -148,7 +120,7 @@
     def rows_of(stream):
         return pl.ds(stream[0] * side, len(stream) * side)
 
-    def slot(index, carry):
+    def slot(index):
         row = place_ref[index, 0]
         column = place_ref[index, 1]
         first = column // LANES
@@ -168,15 +140,6 @@
                 window[part, :, pl.ds(block * LANES, LANES)] = jnp.where(
                     lane < LANES - shift, rolled[block], rolled[block + 1]
                 )
-        move = order_ref[0]
-        seen = moved(diffraction_ref[index], lambda bits: dot(
-            jnp.concatenate([order_ref[1]] * 3, axis=1), jnp.concatenate(bits, axis=0)
-        ))
-        seen = moved(seen, lambda bits: dot(
-            jnp.concatenate(bits, axis=1), jnp.concatenate([move] * 3, axis=0)
-        ))
-        measured[...] = seen.T
-
         for stream in streams:
             for mode in stream:
                 for rows in pieces:
@@ -207,7 +170,7 @@
                 intensity = jnp.zeros((ROWS, half), jnp.float32)
                 for real, imag in far:
                     intensity = intensity + real * real + imag * imag
-                amount = measured[rows, pl.ds(odd * half, half)]
+                amount = measured[index, rows, pl.ds(odd * half, half)]
                 ratio = amount * lax.rsqrt(amount * jnp.maximum(intensity, 1.0))
                 for mode, (real, imag) in enumerate(far):
                     keep(terms, odd, mode * side + rows.start, real * ratio, imag * ratio)
@@ -262,10 +225,108 @@
                 before = rolled[block - 1] if block else zero
                 at = strided(block, part)
                 gradient[at, :] = gradient[at, :] + jnp.where(lane >= shift, here, before)
+
+    def visit(index, carry):
+        inside = place_ref[index, 0] + side <= tile_rows
+        pl.when(inside if local else jnp.logical_not(inside))(lambda: slot(index))
         return carry
 
-    lax.fori_loop(0, count_ref[0, 0], slot, 0)
+    lax.fori_loop(0, count_ref[0, 0], visit, 0)
+
+
+def first_kernel(
+    place_ref,
+    count_ref,
+    tile_hbm,
+    probe_ref,
+    diffraction_ref,
+    table_ref,
+    order_ref,
+    tile_out,
+    gradient,
+    sums,
+    measured,
+    power,
+    probe_out,
+    table_out,
+    window,
+    terms,
+    result,
+    back,
+    semaphore,
+):
+    modes, _, side, _ = probe_ref.shape
+    copy = pltpu.make_async_copy(tile_hbm, tile_out, semaphore)
+    copy.start()
+    gradient[...] = jnp.zeros_like(gradient)
+    sums[...] = jnp.zeros_like(sums)
+    total = jnp.zeros((side, side), jnp.float32)
+    for mode in range(modes):
+        total = total + probe_ref[mode, 0] * probe_ref[mode, 0] + probe_ref[mode, 1] * probe_ref[mode, 1]
+    power[...] = total
+    probe_out[...] = probe_ref[...]
+    table_out[...] = table_ref[...]
+    move = order_ref[0]
+
+    def order(index, carry):
+        seen = moved(diffraction_ref[index], lambda bits: dot(
+            jnp.concatenate([order_ref[1]] * 3, axis=1), jnp.concatenate(bits, axis=0)
+        ))
+        seen = moved(seen, lambda bits: dot(
+            jnp.concatenate(bits, axis=1), jnp.concatenate([move] * 3, axis=0)
+        ))
+        measured[index] = seen.T
+        return carry
+
+    lax.fori_loop(0, count_ref[0, 0], order, 0)
+    copy.wait()
+    all_slots(
+        True, tile_out.shape[0] // SUBLANES, place_ref, count_ref, probe_ref, table_ref, tile_out,
+        gradient, sums, power, measured, window, terms, result, back,
+    )
+
+
+def second_kernel(
+    place_ref,
+    count_ref,
+    here_ref,
+    halo_ref,
+    tile_ref,
+    gradient_ref,
+    sums_ref,
+    measured,
+    power,
+    probe_ref,
+    table_ref,
+    object_out,
+    top_out,
+    spill_out,
+    mine_out,
+    near_out,
+    far_out,
+    old_out,
+    extended,
+    gradient,
+    sums,
+    window,
+    terms,
+    result,
+    back,
+):
+    modes = probe_ref.shape[0]
+    tile_rows, halo_rows, chunks = tile_ref.shape[0], halo_ref.shape[0], sums.shape[0]
+    extended[pl.ds(0, tile_rows), :] = tile_ref[...]
+    extended[pl.ds(tile_rows, halo_rows), :] = halo_ref[...]
+    gradient[pl.ds(0, tile_rows), :] = gradient_ref[...]
+    gradient[pl.ds(tile_rows, halo_rows), :] = jnp.zeros((halo_rows, LANES), jnp.float32)
+    sums[...] = sums_ref[...]
+    scale = 1.0 / jnp.max(power[...])
+    all_slots(
+        False, tile_rows // SUBLANES, place_ref, count_ref, probe_ref, table_ref, extended,
+        gradient, sums, power, measured, window, terms, result, back,
+    )
     object_out[...] = extended[pl.ds(0, tile_rows), :] - gradient[pl.ds(0, tile_rows), :] * scale
+    top_out[...] = object_out[pl.ds(0, halo_rows), :]
     spill_out[...] = gradient[pl.ds(tile_rows, halo_rows), :] * scale
     core, group, layer = here_ref[0, 0], here_ref[0, 1], here_ref[0, 2]
     groups, layers = mine_out.shape[0], mine_out.shape[1]
@@ -290,51 +351,71 @@
     f32 = jnp.float32
     smem = pl.BlockSpec(memory_space=pltpu.SMEM)
     vmem = pl.BlockSpec(memory_space=pltpu.VMEM)
-    anywhere = pl.BlockSpec(memory_space=pl.ANY)
     chunk = (planes, SUBLANES, side)
-    products = 3 * 16 * modes * diffraction.shape[0] * side**3
+    products = 3 * 16 * modes * diffraction.shape[0] * side**3 // 2
+    table, order = jnp.asarray(tables(side)), jnp.asarray(parity_order(side))
+    work = [
+        pltpu.VMEM((2, side, side), f32),
+        pltpu.VMEM((2, modes * side, 2 * side), jnp.bfloat16),
+        pltpu.VMEM((2, modes * side, side), f32),
+        pltpu.VMEM((2, side, side), f32),
+    ]
+    shape = jax.ShapeDtypeStruct
+    cost = pl.CostEstimate(flops=2 * products, bytes_accessed=16 << 20, transcendentals=0)
+    begun = pl.pallas_call(
+        first_kernel,
+        out_shape=(
+            shape(tile.shape, f32),
+            shape(tile.shape, f32),
+            shape((chunks, *chunk), f32),
+            shape(diffraction.shape, f32),
+            shape((side, side), f32),
+            shape(probe.shape, f32),
+            shape(table.shape, table.dtype),
+        ),
+        in_specs=[smem, smem, pl.BlockSpec(memory_space=pl.ANY), vmem, vmem, vmem, vmem],
+        out_specs=(vmem,) * 7,
+        scratch_shapes=work + [pltpu.SemaphoreType.DMA],
+        compiler_params=pltpu.CompilerParams(vmem_limit_bytes=28 * 1024 * 1024),
+        cost_estimate=cost,
+        name="slots_inside",
+    )(place, count, tile, probe, diffraction, table, order)
     return pl.pallas_call(
-        step_kernel,
+        second_kernel,
         out_shape=(
-            jax.ShapeDtypeStruct(tile.shape, f32),
-            jax.ShapeDtypeStruct(halo.shape, f32),
-            jax.ShapeDtypeStruct((groups, layers, *chunk), f32),
-            jax.ShapeDtypeStruct((groups - 1, layers, *chunk), f32),
-            jax.ShapeDtypeStruct((layers, *chunk), f32),
-            jax.ShapeDtypeStruct((planes - 1, SUBLANES, side), f32),
+            shape(tile.shape, f32),
+            shape(halo.shape, f32),
+            shape(halo.shape, f32),
+            shape((groups, layers, *chunk), f32),
+            shape((groups - 1, layers, *chunk), f32),
+            shape((layers, *chunk), f32),
+            shape((planes - 1, SUBLANES, side), f32),
         ),
-        in_specs=[smem, smem, smem, pl.BlockSpec(memory_space=pltpu.HBM), anywhere, vmem, vmem, vmem, vmem],
-        out_specs=(vmem,) * 6,
+        in_specs=[smem, smem, smem] + [vmem] * 8,
+        out_specs=(vmem,) * 7,
         scratch_shapes=[
             pltpu.VMEM((tile.shape[0] + halo.shape[0], LANES), f32),
             pltpu.VMEM((tile.shape[0] + halo.shape[0], LANES), f32),
             pltpu.VMEM((chunks, *chunk), f32),
-            pltpu.VMEM((2, side, side), f32),
-            pltpu.VMEM((side, side), f32),
-            pltpu.VMEM((side, side), f32),
-            pltpu.VMEM((2, modes * side, 2 * side), jnp.bfloat16),
-            pltpu.VMEM((2, modes * side, side), f32),
-            pltpu.VMEM((2, side, side), f32),
-            pltpu.SemaphoreType.DMA((2,)),
-        ],
+        ]
+        + work,
         compiler_params=pltpu.CompilerParams(vmem_limit_bytes=30 * 1024 * 1024),
-        cost_estimate=pl.CostEstimate(flops=2 * products, bytes_accessed=16 << 20, transcendentals=0),
-        name="gradient_step",
-    )(place, count, here, tile, halo, probe, diffraction, jnp.asarray(tables(side)), jnp.asarray(parity_order(side)))
+        cost_estimate=cost,
+        name="slots_across",
+    )(place, count, here, halo, *begun)
 
 
 def first_rows(tile, rows):
-    def kernel(tile_ref, out_ref, semaphore):
-        copy = pltpu.make_async_copy(tile_ref.at[pl.ds(0, rows)], out_ref, semaphore)
-        copy.start()
-        copy.wait()
-
+    def kernel(tile_ref, out_ref):
+        out_ref[...] = tile_ref[...]
+
+    block = pl.BlockSpec((rows // 4, LANES), lambda i: (i, 0))
     return pl.pallas_call(
         kernel,
+        grid=(4,),
         out_shape=jax.ShapeDtypeStruct((rows, LANES), jnp.float32),
-        in_specs=[pl.BlockSpec(memory_space=pltpu.HBM)],
-        out_specs=pl.BlockSpec(memory_space=pl.ANY),
-        scratch_shapes=[pltpu.SemaphoreType.DMA],
+        in_specs=[block],
+        out_specs=block,
         compiler_params=pltpu.CompilerParams(vmem_limit_bytes=62 * 1024 * 1024),
         name="first_rows",
     )(tile)
@@ -350,31 +431,64 @@
 
 def divided(old, parts):
     return pl.pallas_call(
-        divide_kernel, out_shape=jax.ShapeDtypeStruct(old.shape, jnp.float32), name="divided"
+        divide_kernel,
+        out_shape=jax.ShapeDtypeStruct(old.shape, jnp.float32),
+        compiler_params=pltpu.CompilerParams(vmem_limit_bytes=4 * 1024 * 1024),
+        name="divided",
     )(old, *parts)
 
 
 def place_kernel(layers, pieces, here_ref, *refs):
-    *sources, out = refs
+    sources, out, semaphores = refs[: len(pieces)], refs[-2], refs[-1]
     core, group, layer = here_ref[0, 0], here_ref[0, 1], here_ref[0, 2]
-    for source, (flip, hop, first) in zip(sources, pieces):
+    copies = []
+    for source, (flip, hop, start) in zip(sources, pieces):
         for j in range(source.shape[0]):
-            from_layer = lax.rem(layer + layers - (first + j), layers)
+            from_layer = lax.rem(layer + layers - (start + j), layers)
             at = (core ^ flip) * (out.shape[1] // 2) + (group ^ hop) * layers + from_layer
-            out[:, at] = source[j]
-
-
-def put_in_place(here, layers, pieces, arrays, planes, side):
-    vmem = pl.BlockSpec(memory_space=pltpu.VMEM)
+            copies.append(pltpu.make_async_copy(source.at[j], out.at[:, at], semaphores.at[len(copies)]))
+    for copy in copies:
+        copy.start()
+    for copy in copies:
+        copy.wait()
+
+
+def put_in_place(here, layers, pieces, arrays, planes, side, held=None):
+    vmem, anywhere = pl.BlockSpec(memory_space=pltpu.VMEM), pl.BlockSpec(memory_space=pl.ANY)
+    rest = [] if held is None else [held]
     return pl.pallas_call(
         functools.partial(place_kernel, layers, pieces),
         out_shape=jax.ShapeDtypeStruct((planes, side // SUBLANES, SUBLANES, side), jnp.float32),
-        in_specs=[pl.BlockSpec(memory_space=pltpu.SMEM)] + [vmem] * len(arrays),
-        out_specs=vmem,
-        compiler_params=pltpu.CompilerParams(vmem_limit_bytes=24 * 1024 * 1024),
+        in_specs=[pl.BlockSpec(memory_space=pltpu.SMEM)] + [vmem] * len(arrays) + [anywhere] * len(rest),
+        out_specs=anywhere,
+        scratch_shapes=[pltpu.SemaphoreType.DMA((sum(array.shape[0] for array in arrays),))],
+        input_output_aliases={} if held is None else {1 + len(arrays): 0},
+        compiler_params=pltpu.CompilerParams(vmem_limit_bytes=8 * 1024 * 1024),
         cost_estimate=pl.CostEstimate(flops=0, bytes_accessed=4 << 20, transcendentals=0),
         name="put_in_place",
-    )(here, *arrays)
+    )(here, *arrays, *rest)
+
+
+def top_kernel(held_ref, top_ref, arrived_ref, out_ref, rows, semaphore):
+    rows[...] = top_ref[...] - arrived_ref[...]
+    copy = pltpu.make_async_copy(rows, out_ref.at[pl.ds(0, rows.shape[0])], semaphore)
+    copy.start()
+    copy.wait()
+
+
+def with_top(tile, top, arrived):
+    vmem, anywhere = pl.BlockSpec(memory_space=pltpu.VMEM), pl.BlockSpec(memory_space=pl.ANY)
+    return pl.pallas_call(
+        top_kernel,
+        out_shape=jax.ShapeDtypeStruct(tile.shape, jnp.float32),
+        in_specs=[anywhere, vmem, vmem],
+        out_specs=anywhere,
+        scratch_shapes=[pltpu.VMEM(top.shape, jnp.float32), pltpu.SemaphoreType.DMA],
+        input_output_aliases={0: 0},
+        compiler_params=pltpu.CompilerParams(vmem_limit_bytes=8 * 1024 * 1024),
+        cost_estimate=pl.CostEstimate(flops=0, bytes_accessed=2 << 20, transcendentals=0),
+        name="with_top",
+    )(tile, top, arrived)
 
 
 def across(block, hop):
@@ -390,7 +504,7 @@
     return lax.ppermute(block, "region", [(i, (i + 2 * step) % regions) for i in range(regions)])
 
 
-def probe_by_shards(probe, mine, near, far, old, here, layers, arrived):
+def probe_by_shards(probe, mine, near, far, old, here, layers, spill):
     modes, parts, side, _ = probe.shape
     planes = modes * parts
     half = layers // 2
@@ -403,15 +517,21 @@
     to_y = near_sum[2].at[:half].add(by_x)
     by_x, by_y = across(to_x, 1), across(to_y, 2)
     summed = [near_sum[0, step] + by_x[step] + by_y[step] for step in range(layers)]
-    summed, arrived = lax.optimization_barrier((summed, arrived))
     fresh = divided(old, [summed[0]] + [up_layers(summed[step], step) for step in range(1, layers)])
     own = jnp.stack([fresh] + [up_layers(fresh, step) for step in range(1, layers)])
+    own, spill = lax.optimization_barrier((own, spill))
     x, y = across(own, 1), across(own, 2)
-    arrays = [own, x, y, across(x[:half], 2), across(y[half:], 1)]
-    pieces = [(0, 0), (1, 0), (2, 0), (3, 0), (3, half)]
-    arrays = arrays + [from_partner(array) for array in arrays]
-    pieces = tuple((flip, hop, first) for flip in range(2) for hop, first in pieces)
-    return put_in_place(here, layers, pieces, arrays, planes, side).reshape(probe.shape), arrived
+    arrived = shifted(spill, "region", 1)
+    near = [own, x, y]
+    near = near + [from_partner(array) for array in near]
+    placed = put_in_place(
+        here, layers, tuple((flip, hop, 0) for flip in range(2) for hop in range(3)), near, planes, side
+    )
+    far = [across(x[:half], 2), across(y[half:], 1)]
+    far = far + [from_partner(array) for array in far]
+    pieces = tuple((flip, 3, start) for flip in range(2) for start in (0, half))
+    placed = put_in_place(here, layers, pieces, far, planes, side, placed)
+    return placed.reshape(probe.shape), arrived
 
 
 def probe_from_whole(probe, mine, near, far):
@@ -441,16 +561,15 @@
     else:
         here = jnp.zeros((1, 3), jnp.int32)
         groups, layers = 4, side // SUBLANES // 8
-    new_tile, spill, mine, near, far, old = gradient_step(
+    new_tile, top, spill, mine, near, far, old = gradient_step(
         place, slot_counts, here, tile, halo, probe, diffraction, groups, layers
     )
-    arrived = shifted(spill, "region", 1)
     if sharded:
-        new_probe, arrived = probe_by_shards(probe, mine, near, far, old, here, layers, arrived)
+        new_probe, arrived = probe_by_shards(probe, mine, near, far, old, here, layers, spill)
     else:
+        arrived = shifted(spill, "region", 1)
         new_probe = probe_from_whole(probe, mine, near, far)
-    overlap = spill.shape[0]
-    new_tile = lax.dynamic_update_slice(new_tile, new_tile[:overlap] - arrived, (0, 0))
+    new_tile = with_top(new_tile, top, arrived)
     return (unpacked(new_tile, object_slab.shape), new_probe)
 
 

time: 140 us -> 100 us (0.71)
  starting transfers between devices: 43.4 us -> 21.9 us
  Pallas kernels: 50.2 us -> 35.5 us
  waiting for transfers between devices: 37.2 us -> 35.1 us
  other arithmetic: 2.12 us -> 0.43 us
    ppermute x7, starting transfers between devices: 24.4 us -> 1.18 us  [from_partner(): lax.ppermute(block, 'region', [(i, i ^ 1) for i in range(lax.axis_size('r...]
    pallas_call x2 -> x4, Pallas kernels: 46.6 us -> 32.2 us  [the longest x1 19.2 us: gradient_step(): pl.pallas_call(first_kernel, out_shape=(shape(tile.shape, f32), shape(til...]
    ppermute x8, starting transfers between devices: 6.81 us -> 9.48 us  [across(): lax.ppermute(block, 'group', [(i, i ^ hop) for i in range(lax.axis_size('...]
    ppermute x2, waiting for transfers between devices: 2.54 us -> 0.01 us  [shifted(): return lax.ppermute(block, axis, route)]
    pallas_call x1, Pallas kernels: 1.68 us -> 0.03 us  [divided(): pl.pallas_call(divide_kernel, out_shape=jax.ShapeDtypeStruct(old.shape, j...]
    pallas_call x1 -> x2, Pallas kernels: 2 us -> 3.28 us  [put_in_place(): pl.pallas_call(functools.partial(place_kernel, layers, pieces), out_shape...]
    unnamed x25 -> x13, local copies, waits for them, and re-layouts: 5.19 us -> 4.51 us
  transfers between devices with their start and end apart: 23 -> 23, of which waited for: 16 -> 14; matrix products, arithmetic and copies ran while one was open for 1% -> 0% of each run, Pallas kernels for 0% -> 23%
where the time goes in v4:
time: 100 us; the launch traced here: 99.1 us
  Pallas kernels  35.5 us (36%)
  waiting for transfers between devices  35.1 us (35%)
  starting transfers between devices  21.9 us (22%)
  local copies, waits for them, and re-layouts  4.6 us (5%)
  between operations  1.68 us (2%)
    ppermute x8, waiting for transfers between devices, across(): lax.ppermute(block, 'group', [(i, i ^ hop) for i in range(lax.axis_size('...  23.3 us
    pallas_call x1, Pallas kernels, gradient_step(): pl.pallas_call(first_kernel, out_shape=(shape(tile.shape, f32), shape(til...  19.2 us
    ppermute x6, waiting for transfers between devices, up_layers(): lax.ppermute(block, 'region', [(i, (i + 2 * step) % regions) for i in ran...  10.1 us
    ppermute x8, starting transfers between devices, across(): lax.ppermute(block, 'group', [(i, i ^ hop) for i in range(lax.axis_size('...  9.48 us
    ppermute x6, starting transfers between devices, up_layers(): lax.ppermute(block, 'region', [(i, (i + 2 * step) % regions) for i in ran...  8.56 us
    pallas_call x1, Pallas kernels, gradient_step(): pl.pallas_call(second_kernel, out_shape=(shape(tile.shape, f32), shape(ha...  8.45 us
    unnamed x13, local copies, waits for them, and re-layouts  4.51 us
    pallas_call x1, Pallas kernels, first_rows(): pl.pallas_call(kernel, grid=(4,), out_shape=jax.ShapeDtypeStruct((rows, L...  3.46 us
  transfers between devices with their start and end apart: 23, of which 14 were waited for; matrix products, arithmetic and copies ran while one was open for 0% of the time, Pallas kernels for 23%

profile of v4, /device:TPU:0, one launch (start us, length us, event | category | flops | bytes accessed | tf_op | source)
XLA Modules:
  0.0 99.1 jit_solution(18148060984298075509)
XLA Ops:
  0.6 0.0 copy-start.4
  0.6 0.0 copy-start.5
  0.7 0.0 copy-start.2
  0.7 3.5 %first_rows.1 = f32[2048,128]{1,0:T(8,128)} custom-call(f32[4096,128]{1,0:T(8,128)} %bitcast.95), custom_call_target="tpu_custom_call" | custom-call | tf_op jit(solution)/shard_map/first_rows/pallas_call | solution.py:413
  4.1 1.3 %collective-permute-start = (f32[2048,128]{1,0:T(8,128)}, f32[2048,128]{1,0:T(8,128)S(1)}, u32[]{:S(2)}, u32[]{:S(2)}) collective-permute-start(f32[2048,128]{1,0:T(8,128)} %first_rows.1), channel_id=1, source_target_pairs={{4,0},{8,4},{12,8},{16,12},{20,16},{24,20},{28,24},{5,1},{9,5},{13... | collective-permute-start | bytes 3145736 | tf_op jit(solution)/shard_map/ppermute | solution.py:21
  6.1 0.1 copy.11
  6.2 0.1 pad_add_fusion
  6.3 0.1 add_bitcast_fusion.here_ref
  6.3 0.0 copy-done.2
  6.3 1.6 %copy-done = f32[512,2,512]{2,1,0:T(2,128)S(1)} copy-done((f32[512,2,512]{2,1,0:T(2,128)S(1)}, f32[512,2,512]{2,1,0:T(2,128)}, u32[]{:S(2)}) %copy-start) | copy-done | bytes 2097176
  7.9 1.6 %copy-done.1 = f32[4,2,256,256]{3,2,1,0:T(8,128)S(1)} copy-done((f32[4,2,256,256]{3,2,1,0:T(8,128)S(1)}, f32[4,2,256,256]{3,2,1,0:T(8,128)}, u32[]{:S(2)}) %copy-start.1) | copy-done | bytes 2097176
  9.5 1.2 %copy-done.3 = bf16[2,4,256,256]{3,2,1,0:T(8,128)(2,1)S(1)} copy-done((bf16[2,4,256,256]{3,2,1,0:T(8,128)(2,1)S(1)}, bf16[2,4,256,256]{3,2,1,0:T(8,128)(2,1)}, u32[]{:S(2)}) %copy-start.3) | copy-done | bytes 1048600
  10.8 19.2 %slots_inside.1 = (f32[4096,128]{1,0:T(8,128)S(1)}, f32[4096,128]{1,0:T(8,128)S(1)}, f32[32,9,8,256]{3,2,1,0:T(8,128)S(1)}, f32[4,256,256]{2,1,0:T(8,128)S(1)}, ...) custom-call(s32[4,2]{1,0:T(4,128)S(1)} %broadcast_subtract_fusion.place_ref, ...), custom_call_target="tpu_custom_call" | custom-call | flops 12884901888 | bytes 16777216 | tf_op jit(solution)/shard_map/slots_inside/pallas_call | solution.py:365
  29.9 0.0 collective-permute-done.halo_ref
  29.9 8.5 %slots_across.1 = (f32[4096,128]{1,0:T(8,128)}, f32[2048,128]{1,0:T(8,128)S(1)}, f32[2048,128]{1,0:T(8,128)S(1)}, f32[4,4,9,8,256]{4,3,2,1,0:T(8,128)S(1)}, f32[...) custom-call(s32[4,2]{1,0:T(4,128)S(1)} %broadcast_subtract_fusion.place_ref, ...), custom_call_target="tpu_custom_call" | custom-call | flops 12884901888 | bytes 16777216 | tf_op jit(solution)/shard_map/slots_across/pallas_call | solution.py:383
  38.4 0.0 collective-permute-start.1
  38.4 1.6 %collective-permute-done.1 = f32[4,9,8,256]{3,2,1,0:T(8,128)S(1)} collective-permute-done((f32[4,9,8,256]{3,2,1,0:T(8,128)S(1)}, f32[4,9,8,256]{3,2,1,0:T(8,128)S(1)}, u32[]{:S(2)}, u32[]{:S(2)}) %collective-permute-start.1) | collective-permute-done | bytes 294944 | tf_op jit(solution)/shard_map/ppermute | solution.py:499
  40.0 0.1 collective-permute-start.2
  40.2 0.1 collective-permute-start.3
  40.3 5.4 %collective-permute-start.5 = (f32[2,9,8,256]{3,2,1,0:T(8,128)S(1)}, f32[2,9,8,256]{3,2,1,0:T(8,128)S(1)}, u32[]{:S(2)}, u32[]{:S(2)}) collective-permute-start(f32[2,9,8,256]{3,2,1,0:T(8,128)S(1)} %get-tuple-element.71), channel_id=1, source_target_pairs={{0,1},{1,0},{2,3},{3,2},{4,5},{5,4},{6,7},{7,6},{8,9},{9,8},{10,11... | collective-permute-start | bytes 442376 | tf_op jit(solution)/shard_map/ppermute | solution.py:495
  45.7 0.0 collective-permute-done.2
  45.7 0.1 slice_add_fusion
  45.8 0.5 collective-permute-done.3
  46.4 3.2 %collective-permute-done.5 = f32[2,9,8,256]{3,2,1,0:T(8,128)S(1)} collective-permute-done((f32[2,9,8,256]{3,2,1,0:T(8,128)S(1)}, f32[2,9,8,256]{3,2,1,0:T(8,128)S(1)}, u32[]{:S(2)}, u32[]{:S(2)}) %collective-permute-start.5) | collective-permute-done | bytes 147488 | tf_op jit(solution)/shard_map/ppermute | solution.py:495
  49.6 1.8 %collective-permute-start.4 = (f32[4,9,8,256]{3,2,1,0:T(8,128)S(1)}, f32[4,9,8,256]{3,2,1,0:T(8,128)S(1)}, u32[]{:S(2)}, u32[]{:S(2)}) collective-permute-start(f32[4,9,8,256]{3,2,1,0:T(8,128)S(1)} %get-tuple-element.66), channel_id=1, source_target_pairs={{0,1},{1,0},{2,3},{3,2},{4,5},{5,4},{6,7},{7,6},{8,9},{9,8},{10,11... | collective-permute-start | bytes 884744 | tf_op jit(solution)/shard_map/ppermute | solution.py:495
  51.4 0.4 collective-permute-start.6
  51.7 6.1 %collective-permute-done.4 = f32[4,9,8,256]{3,2,1,0:T(8,128)S(1)} collective-permute-done((f32[4,9,8,256]{3,2,1,0:T(8,128)S(1)}, f32[4,9,8,256]{3,2,1,0:T(8,128)S(1)}, u32[]{:S(2)}, u32[]{:S(2)}) %collective-permute-start.4) | collective-permute-done | bytes 294944 | tf_op jit(solution)/shard_map/ppermute | solution.py:495
  57.8 1.1 %collective-permute-done.6 = f32[4,9,8,256]{3,2,1,0:T(8,128)S(1)} collective-permute-done((f32[4,9,8,256]{3,2,1,0:T(8,128)S(1)}, f32[4,9,8,256]{3,2,1,0:T(8,128)S(1)}, u32[]{:S(2)}, u32[]{:S(2)}) %collective-permute-start.6) | collective-permute-done | bytes 294944 | tf_op jit(solution)/shard_map/ppermute | solution.py:495
  59.0 0.1 fusion.4
  59.1 3.8 %collective-permute-start.9 = (f32[9,8,256]{2,1,0:T(8,128)S(1)}, f32[9,8,256]{2,1,0:T(8,128)S(1)}, u32[]{:S(2)}, u32[]{:S(2)}) collective-permute-start(f32[9,8,256]{2,1,0:T(8,128)S(1)} %get-tuple-element.62), channel_id=1, source_target_pairs={{0,24},{4,28},{8,0},{12,4},{16,8},{20,12},{24,16},{28,20},{1,25},{... | collective-permute-start | bytes 221192 | tf_op jit(solution)/shard_map/ppermute | solution.py:504
  62.8 0.0 collective-permute-start.8
  62.8 0.6 collective-permute-start.7
  63.5 1.3 %collective-permute-done.9.refs_3_ = f32[9,8,256]{2,1,0:T(8,128)S(1)} collective-permute-done((f32[9,8,256]{2,1,0:T(8,128)S(1)}, f32[9,8,256]{2,1,0:T(8,128)S(1)}, u32[]{:S(2)}, u32[]{:S(2)}) %collective-permute-start.9) | collective-permute-done | bytes 73760 | tf_op jit(solution)/shard_map/ppermute | solution.py:504
  64.8 4.6 %collective-permute-done.8.refs_2_ = f32[9,8,256]{2,1,0:T(8,128)S(1)} collective-permute-done((f32[9,8,256]{2,1,0:T(8,128)S(1)}, f32[9,8,256]{2,1,0:T(8,128)S(1)}, u32[]{:S(2)}, u32[]{:S(2)}) %collective-permute-start.8) | collective-permute-done | bytes 73760 | tf_op jit(solution)/shard_map/ppermute | solution.py:504
  69.4 0.1 collective-permute-done.7.refs_1_
  69.5 0.3 collective-permute-start.12
  69.9 1.9 %collective-permute-start.11 = (f32[8,8,256]{2,1,0:T(8,128)S(1)}, f32[8,8,256]{2,1,0:T(8,128)S(1)}, u32[]{:S(2)}, u32[]{:S(2)}) collective-permute-start(f32[8,8,256]{2,1,0:T(8,128)S(1)} %divided.1), channel_id=1, source_target_pairs={{0,16},{4,20},{8,24},{12,28},{16,0},{20,4},{24,8},{28,12},{1,17},{... | collective-permute-start | bytes 196616 | tf_op jit(solution)/shard_map/ppermute | solution.py:504
  71.7 1.9 %collective-permute-start.10 = (f32[8,8,256]{2,1,0:T(8,128)S(1)}, f32[8,8,256]{2,1,0:T(8,128)S(1)}, u32[]{:S(2)}, u32[]{:S(2)}) collective-permute-start(f32[8,8,256]{2,1,0:T(8,128)S(1)} %divided.1), channel_id=1, source_target_pairs={{0,8},{4,12},{8,16},{12,20},{16,24},{20,28},{24,0},{28,4},{1,9},{5... | collective-permute-start | bytes 196616 | tf_op jit(solution)/shard_map/ppermute | solution.py:504
  73.7 0.2 collective-permute-done.12
  73.9 1.2 %collective-permute-done.11 = f32[8,8,256]{2,1,0:T(8,128)S(1)} collective-permute-done((f32[8,8,256]{2,1,0:T(8,128)S(1)}, f32[8,8,256]{2,1,0:T(8,128)S(1)}, u32[]{:S(2)}, u32[]{:S(2)}) %collective-permute-start.11) | collective-permute-done | bytes 65568 | tf_op jit(solution)/shard_map/ppermute | solution.py:504
  75.0 2.8 %collective-permute-done.10 = f32[8,8,256]{2,1,0:T(8,128)S(1)} collective-permute-done((f32[8,8,256]{2,1,0:T(8,128)S(1)}, f32[8,8,256]{2,1,0:T(8,128)S(1)}, u32[]{:S(2)}, u32[]{:S(2)}) %collective-permute-start.10) | collective-permute-done | bytes 65568 | tf_op jit(solution)/shard_map/ppermute | solution.py:504
  77.8 1.4 %collective-permute-start.13 = (f32[2048,128]{1,0:T(8,128)S(1)}, f32[2048,128]{1,0:T(8,128)S(1)}, u32[]{:S(2)}, u32[]{:S(2)}) collective-permute-start(f32[2048,128]{1,0:T(8,128)S(1)} %get-tuple-element.60), channel_id=1, source_target_pairs={{0,4},{4,8},{8,12},{12,16},{16,20},{20,24},{24,28},{1,5},{5,9},{9,... | collective-permute-start | bytes 3145736 | tf_op jit(solution)/shard_map/ppermute | solution.py:21
  79.2 0.1 collective-permute-start.16
  79.3 0.5 collective-permute-start.14
  79.8 0.4 collective-permute-start.20
  80.2 8.1 %collective-permute-done.16.refs_2_ = f32[4,8,8,256]{3,2,1,0:T(8,128)S(1)} collective-permute-done((f32[4,8,8,256]{3,2,1,0:T(8,128)S(1)}, f32[4,8,8,256]{3,2,1,0:T(8,128)S(1)}, u32[]{:S(2)}, u32[]{:S(2)}) %collective-permute-start.16) | collective-permute-done | bytes 262176 | tf_op jit(solution)/shard_map/ppermute | solution.py:495
  88.3 0.1 collective-permute-start.17
  88.4 0.1 collective-permute-start.22
  88.4 0.0 collective-permute-done.14.refs_1_
  88.5 0.6 collective-permute-start.21
  89.0 0.0 collective-permute-done.20.refs_3_
  89.0 1.2 %collective-permute-start.15 = (f32[2,8,8,256]{3,2,1,0:T(8,128)S(1)}, f32[2,8,8,256]{3,2,1,0:T(8,128)S(1)}, u32[]{:S(2)}, u32[]{:S(2)}) collective-permute-start(f32[2,8,8,256]{3,2,1,0:T(8,128)S(1)} %slice.160), channel_id=1, source_target_pairs={{0,2},{1,3},{2,0},{3,1},{4,6},{5,7},{6,4},{7,5},{8,10},{9,11},{10,... | collective-permute-start | bytes 393224 | tf_op jit(solution)/shard_map/ppermute | solution.py:495
  90.2 3.5 %collective-permute-done.17.refs_1_ = f32[2,8,8,256]{3,2,1,0:T(8,128)S(1)} collective-permute-done((f32[2,8,8,256]{3,2,1,0:T(8,128)S(1)}, f32[2,8,8,256]{3,2,1,0:T(8,128)S(1)}, u32[]{:S(2)}, u32[]{:S(2)}) %collective-permute-start.17) | collective-permute-done | bytes 131104 | tf_op jit(solution)/shard_map/ppermute | solution.py:495
  93.7 0.0 collective-permute-start.19
  93.7 0.8 collective-permute-done.15.refs_0_
  94.5 0.0 collective-permute-start.18
  94.5 0.0 collective-permute-done.22.refs_5_
  94.5 0.0 collective-permute-done.21.refs_4_
  94.5 1.9 %put_in_place.2.refs_4_ = f32[8,32,8,256]{3,2,1,0:T(8,128)} custom-call(s32[1,3]{1,0:T(1,128)S(1)} %add_bitcast_fusion.here_ref, f32[4,8,8,256]{3,2,1,0:T(8,128)S(1)} %pad_maximum_fusion.refs_0_, f32[4,8,8,256]{3,2,1,0:T(8,128)S(1)} %collective-permute-done.14.refs_1_, f32[4,8,8,256]{3,2,1,0:T(8,128)S(1)} %collective-permute-done.16.refs_2_, ...), custom_call_target="tpu_custom_call" | custom-call | bytes 4194304 | tf_op jit(solution)/shard_map/put_in_place/pallas_call | solution.py:459
  96.4 0.0 collective-permute-done.19.refs_3_
  96.4 0.0 collective-permute-done.18.refs_2_
  96.4 1.4 %put_in_place.3 = f32[8,32,8,256]{3,2,1,0:T(8,128)} custom-call(s32[1,3]{1,0:T(1,128)S(1)} %add_bitcast_fusion.here_ref, f32[2,8,8,256]{3,2,1,0:T(8,128)S(1)} %collective-permute-done.15.refs_0_, f32[2,8,8,256]{3,2,1,0:T(8,128)S(1)} %collective-permute-done.17.refs_1_, ...), custom_call_target="tpu_custom_call", output_to_operand_aliasing={{}: (5, {})} | custom-call | bytes 4194304 | tf_op jit(solution)/shard_map/put_in_place/pallas_call | solution.py:459
  97.8 0.0 collective-permute-done.13.arrived_ref
  97.9 1.1 %with_top.1 = f32[4096,128]{1,0:T(8,128)} custom-call(f32[4096,128]{1,0:T(8,128)} %get-tuple-element.51.held_ref, f32[2048,128]{1,0:T(8,128)S(1)} %get-tuple-element.52.top_ref, f32[2048,128]{1,0:T(8,128)S(1)} %collective-permute-done.13.arrived_ref), custom_call_target="tpu_custom_call", output_to_operand_aliasing={{}: (0, {})} | custom-call | bytes 2097152 | tf_op jit(solution)/shard_map/with_top/pallas_call | solution.py:481
  (14 shorter events, 0.2 us)
Async XLA Ops:
  0.6 5.7 %copy-start.4 = (bf16[2,256,256]{2,1,0:T(8,128)(2,1)S(1)}, bf16[2,256,256]{2,1,0:T(8,128)(2,1)}, u32[]{:S(2)}) copy-start(bf16[2,256,256]{2,1,0:T(8,128)(2,1)} %constant.96.clone.order_ref) | copy-start | bytes 786436
  0.6 5.4 %copy-start.5 = (s32[4,2]{0,1:T(2,128)S(1)}, s32[4,2]{0,1:T(2,128)}, u32[]{:S(2)}) copy-start(s32[4,2]{0,1:T(2,128)} %param.14) | copy-start | bytes 100
  0.7 5.7 %copy-start.2 = (f32[4,256,256]{2,1,0:T(8,128)S(1)}, f32[4,256,256]{2,1,0:T(8,128)}, u32[]{:S(2)}) copy-start(f32[4,256,256]{2,1,0:T(8,128)} %diffraction_ref.1) | copy-start | bytes 3145732
  4.1 25.8 %collective-permute-start = (f32[2048,128]{1,0:T(8,128)}, f32[2048,128]{1,0:T(8,128)S(1)}, u32[]{:S(2)}, u32[]{:S(2)}) collective-permute-start(f32[2048,128]{1,0:T(8,128)} %first_rows.1), channel_id=1, source_target_pairs={{4,0},{8,4},{12,8},{16,12},{20,16},{24,20},{28,24},{5,1},{9,5},{13... | collective-permute-start | bytes 3145736 | tf_op jit(solution)/shard_map/ppermute | solution.py:21
  6.3 1.6 %copy-start = (f32[512,2,512]{2,1,0:T(2,128)S(1)}, f32[512,2,512]{2,1,0:T(2,128)}, u32[]{:S(2)}) copy-start(f32[512,2,512]{2,1,0:T(2,128)} %param.11) | copy-start | bytes 6291460
  7.9 1.6 %copy-start.1 = (f32[4,2,256,256]{3,2,1,0:T(8,128)S(1)}, f32[4,2,256,256]{3,2,1,0:T(8,128)}, u32[]{:S(2)}) copy-start(f32[4,2,256,256]{3,2,1,0:T(8,128)} %probe_ref.1) | copy-start | bytes 6291460
  9.5 1.2 %copy-start.3 = (bf16[2,4,256,256]{3,2,1,0:T(8,128)(2,1)S(1)}, bf16[2,4,256,256]{3,2,1,0:T(8,128)(2,1)}, u32[]{:S(2)}) copy-start(bf16[2,4,256,256]{3,2,1,0:T(8,128)(2,1)} %constant.95.clone.table_ref) | copy-start | bytes 3145732
  38.4 1.6 %collective-permute-start.1 = (f32[4,9,8,256]{3,2,1,0:T(8,128)S(1)}, f32[4,9,8,256]{3,2,1,0:T(8,128)S(1)}, u32[]{:S(2)}, u32[]{:S(2)}) collective-permute-start(f32[4,9,8,256]{3,2,1,0:T(8,128)S(1)} %get-tuple-element.56), channel_id=1, source_target_pairs={{0,4},{4,0},{8,12},{12,8},{16,20},{20,16},{24,28},{28,24},{1,5},{5... | collective-permute-start | bytes 884744 | tf_op jit(solution)/shard_map/ppermute | solution.py:499
  40.0 5.7 %collective-permute-start.2 = (f32[3,4,9,8,256]{4,3,2,1,0:T(8,128)S(1)}, f32[3,4,9,8,256]{4,3,2,1,0:T(8,128)S(1)}, u32[]{:S(2)}, u32[]{:S(2)}) collective-permute-start(f32[3,4,9,8,256]{4,3,2,1,0:T(8,128)S(1)} %get-tuple-element.57), channel_id=1, source_target_pairs={{0,4},{4,0},{8,12},{12,8},{16,20},{20,16},{24,28},{28,24},{1,5},{5... | collective-permute-start | bytes 2654216 | tf_op jit(solution)/shard_map/ppermute | solution.py:499
  40.2 6.2 %collective-permute-start.3 = (f32[2,9,8,256]{3,2,1,0:T(8,128)S(1)}, f32[2,9,8,256]{3,2,1,0:T(8,128)S(1)}, u32[]{:S(2)}, u32[]{:S(2)}) collective-permute-start(f32[2,9,8,256]{3,2,1,0:T(8,128)S(1)} %get-tuple-element.70), channel_id=1, source_target_pairs={{0,2},{1,3},{2,0},{3,1},{4,6},{5,7},{6,4},{7,5},{8,10},{9,11},{10,... | collective-permute-start | bytes 442376 | tf_op jit(solution)/shard_map/ppermute | solution.py:495
  40.3 9.3 %collective-permute-start.5 = (f32[2,9,8,256]{3,2,1,0:T(8,128)S(1)}, f32[2,9,8,256]{3,2,1,0:T(8,128)S(1)}, u32[]{:S(2)}, u32[]{:S(2)}) collective-permute-start(f32[2,9,8,256]{3,2,1,0:T(8,128)S(1)} %get-tuple-element.71), channel_id=1, source_target_pairs={{0,1},{1,0},{2,3},{3,2},{4,5},{5,4},{6,7},{7,6},{8,9},{9,8},{10,11... | collective-permute-start | bytes 442376 | tf_op jit(solution)/shard_map/ppermute | solution.py:495
  49.6 8.3 %collective-permute-start.4 = (f32[4,9,8,256]{3,2,1,0:T(8,128)S(1)}, f32[4,9,8,256]{3,2,1,0:T(8,128)S(1)}, u32[]{:S(2)}, u32[]{:S(2)}) collective-permute-start(f32[4,9,8,256]{3,2,1,0:T(8,128)S(1)} %get-tuple-element.66), channel_id=1, source_target_pairs={{0,1},{1,0},{2,3},{3,2},{4,5},{5,4},{6,7},{7,6},{8,9},{9,8},{10,11... | collective-permute-start | bytes 884744 | tf_op jit(solution)/shard_map/ppermute | solution.py:495
  51.4 7.6 %collective-permute-start.6 = (f32[4,9,8,256]{3,2,1,0:T(8,128)S(1)}, f32[4,9,8,256]{3,2,1,0:T(8,128)S(1)}, u32[]{:S(2)}, u32[]{:S(2)}) collective-permute-start(f32[4,9,8,256]{3,2,1,0:T(8,128)S(1)} %get-tuple-element.67), channel_id=1, source_target_pairs={{0,2},{1,3},{2,0},{3,1},{4,6},{5,7},{6,4},{7,5},{8,10},{9,11},{10,... | collective-permute-start | bytes 884744 | tf_op jit(solution)/shard_map/ppermute | solution.py:495
  59.1 5.8 %collective-permute-start.9 = (f32[9,8,256]{2,1,0:T(8,128)S(1)}, f32[9,8,256]{2,1,0:T(8,128)S(1)}, u32[]{:S(2)}, u32[]{:S(2)}) collective-permute-start(f32[9,8,256]{2,1,0:T(8,128)S(1)} %get-tuple-element.62), channel_id=1, source_target_pairs={{0,24},{4,28},{8,0},{12,4},{16,8},{20,12},{24,16},{28,20},{1,25},{... | collective-permute-start | bytes 221192 | tf_op jit(solution)/shard_map/ppermute | solution.py:504
  62.8 6.5 %collective-permute-start.8 = (f32[9,8,256]{2,1,0:T(8,128)S(1)}, f32[9,8,256]{2,1,0:T(8,128)S(1)}, u32[]{:S(2)}, u32[]{:S(2)}) collective-permute-start(f32[9,8,256]{2,1,0:T(8,128)S(1)} %get-tuple-element.63), channel_id=1, source_target_pairs={{0,16},{4,20},{8,24},{12,28},{16,0},{20,4},{24,8},{28,12},{1,17},{... | collective-permute-start | bytes 221192 | tf_op jit(solution)/shard_map/ppermute | solution.py:504
  62.8 6.7 %collective-permute-start.7 = (f32[9,8,256]{2,1,0:T(8,128)S(1)}, f32[9,8,256]{2,1,0:T(8,128)S(1)}, u32[]{:S(2)}, u32[]{:S(2)}) collective-permute-start(f32[9,8,256]{2,1,0:T(8,128)S(1)} %get-tuple-element.64), channel_id=1, source_target_pairs={{0,8},{4,12},{8,16},{12,20},{16,24},{20,28},{24,0},{28,4},{1,9},{5... | collective-permute-start | bytes 221192 | tf_op jit(solution)/shard_map/ppermute | solution.py:504
  69.5 4.3 %collective-permute-start.12 = (f32[8,8,256]{2,1,0:T(8,128)S(1)}, f32[8,8,256]{2,1,0:T(8,128)S(1)}, u32[]{:S(2)}, u32[]{:S(2)}) collective-permute-start(f32[8,8,256]{2,1,0:T(8,128)S(1)} %divided.1), channel_id=1, source_target_pairs={{0,24},{4,28},{8,0},{12,4},{16,8},{20,12},{24,16},{28,20},{1,25},{... | collective-permute-start | bytes 196616 | tf_op jit(solution)/shard_map/ppermute | solution.py:504
  69.9 5.2 %collective-permute-start.11 = (f32[8,8,256]{2,1,0:T(8,128)S(1)}, f32[8,8,256]{2,1,0:T(8,128)S(1)}, u32[]{:S(2)}, u32[]{:S(2)}) collective-permute-start(f32[8,8,256]{2,1,0:T(8,128)S(1)} %divided.1), channel_id=1, source_target_pairs={{0,16},{4,20},{8,24},{12,28},{16,0},{20,4},{24,8},{28,12},{1,17},{... | collective-permute-start | bytes 196616 | tf_op jit(solution)/shard_map/ppermute | solution.py:504
  71.7 6.1 %collective-permute-start.10 = (f32[8,8,256]{2,1,0:T(8,128)S(1)}, f32[8,8,256]{2,1,0:T(8,128)S(1)}, u32[]{:S(2)}, u32[]{:S(2)}) collective-permute-start(f32[8,8,256]{2,1,0:T(8,128)S(1)} %divided.1), channel_id=1, source_target_pairs={{0,8},{4,12},{8,16},{12,20},{16,24},{20,28},{24,0},{28,4},{1,9},{5... | collective-permute-start | bytes 196616 | tf_op jit(solution)/shard_map/ppermute | solution.py:504
  77.8 20.0 %collective-permute-start.13 = (f32[2048,128]{1,0:T(8,128)S(1)}, f32[2048,128]{1,0:T(8,128)S(1)}, u32[]{:S(2)}, u32[]{:S(2)}) collective-permute-start(f32[2048,128]{1,0:T(8,128)S(1)} %get-tuple-element.60), channel_id=1, source_target_pairs={{0,4},{4,8},{8,12},{12,16},{16,20},{20,24},{24,28},{1,5},{5,9},{9,... | collective-permute-start | bytes 3145736 | tf_op jit(solution)/shard_map/ppermute | solution.py:21
  79.2 9.1 %collective-permute-start.16 = (f32[4,8,8,256]{3,2,1,0:T(8,128)S(1)}, f32[4,8,8,256]{3,2,1,0:T(8,128)S(1)}, u32[]{:S(2)}, u32[]{:S(2)}) collective-permute-start(f32[4,8,8,256]{3,2,1,0:T(8,128)S(1)} %pad_maximum_fusion.refs_0_), channel_id=1, source_target_pairs={{0,2},{1,3},{2,0},{3,1},{4,6},{5,7},{6,4},{7,5},{8,10},{9,11},{10,... | collective-permute-start | bytes 786440 | tf_op jit(solution)/shard_map/ppermute | solution.py:495
  79.3 9.2 %collective-permute-start.14 = (f32[4,8,8,256]{3,2,1,0:T(8,128)S(1)}, f32[4,8,8,256]{3,2,1,0:T(8,128)S(1)}, u32[]{:S(2)}, u32[]{:S(2)}) collective-permute-start(f32[4,8,8,256]{3,2,1,0:T(8,128)S(1)} %pad_maximum_fusion.refs_0_), channel_id=1, source_target_pairs={{0,1},{1,0},{2,3},{3,2},{4,5},{5,4},{6,7},{7,6},{8,9},{9,8},{10,11... | collective-permute-start | bytes 786440 | tf_op jit(solution)/shard_map/ppermute | solution.py:495
  79.8 9.2 %collective-permute-start.20 = (f32[4,8,8,256]{3,2,1,0:T(8,128)S(1)}, f32[4,8,8,256]{3,2,1,0:T(8,128)S(1)}, u32[]{:S(2)}, u32[]{:S(2)}) collective-permute-start(f32[4,8,8,256]{3,2,1,0:T(8,128)S(1)} %pad_maximum_fusion.refs_0_), channel_id=1, source_target_pairs={{0,4},{4,0},{8,12},{12,8},{16,20},{20,16},{24,28},{28,24},{1,5},{5... | collective-permute-start | bytes 786440 | tf_op jit(solution)/shard_map/ppermute | solution.py:499
  88.3 5.4 %collective-permute-start.17 = (f32[2,8,8,256]{3,2,1,0:T(8,128)S(1)}, f32[2,8,8,256]{3,2,1,0:T(8,128)S(1)}, u32[]{:S(2)}, u32[]{:S(2)}) collective-permute-start(f32[2,8,8,256]{3,2,1,0:T(8,128)S(1)} %slice.161), channel_id=1, source_target_pairs={{0,1},{1,0},{2,3},{3,2},{4,5},{5,4},{6,7},{7,6},{8,9},{9,8},{10,11... | collective-permute-start | bytes 393224 | tf_op jit(solution)/shard_map/ppermute | solution.py:495
  88.4 6.2 %collective-permute-start.22 = (f32[4,8,8,256]{3,2,1,0:T(8,128)S(1)}, f32[4,8,8,256]{3,2,1,0:T(8,128)S(1)}, u32[]{:S(2)}, u32[]{:S(2)}) collective-permute-start(f32[4,8,8,256]{3,2,1,0:T(8,128)S(1)} %collective-permute-done.16.refs_2_), channel_id=1, source_target_pairs={{0,4},{4,0},{8,12},{12,8},{16,20},{20,16},{24,28},{28,24},{1,5},{5... | collective-permute-start | bytes 786440 | tf_op jit(solution)/shard_map/ppermute | solution.py:499
  88.5 6.1 %collective-permute-start.21 = (f32[4,8,8,256]{3,2,1,0:T(8,128)S(1)}, f32[4,8,8,256]{3,2,1,0:T(8,128)S(1)}, u32[]{:S(2)}, u32[]{:S(2)}) collective-permute-start(f32[4,8,8,256]{3,2,1,0:T(8,128)S(1)} %collective-permute-done.14.refs_1_), channel_id=1, source_target_pairs={{0,4},{4,0},{8,12},{12,8},{16,20},{20,16},{24,28},{28,24},{1,5},{5... | collective-permute-start | bytes 786440 | tf_op jit(solution)/shard_map/ppermute | solution.py:499
  89.0 5.5 %collective-permute-start.15 = (f32[2,8,8,256]{3,2,1,0:T(8,128)S(1)}, f32[2,8,8,256]{3,2,1,0:T(8,128)S(1)}, u32[]{:S(2)}, u32[]{:S(2)}) collective-permute-start(f32[2,8,8,256]{3,2,1,0:T(8,128)S(1)} %slice.160), channel_id=1, source_target_pairs={{0,2},{1,3},{2,0},{3,1},{4,6},{5,7},{6,4},{7,5},{8,10},{9,11},{10,... | collective-permute-start | bytes 393224 | tf_op jit(solution)/shard_map/ppermute | solution.py:495
  93.7 2.7 %collective-permute-start.19 = (f32[2,8,8,256]{3,2,1,0:T(8,128)S(1)}, f32[2,8,8,256]{3,2,1,0:T(8,128)S(1)}, u32[]{:S(2)}, u32[]{:S(2)}) collective-permute-start(f32[2,8,8,256]{3,2,1,0:T(8,128)S(1)} %collective-permute-done.17.refs_1_), channel_id=1, source_target_pairs={{0,4},{4,0},{8,12},{12,8},{16,20},{20,16},{24,28},{28,24},{1,5},{5... | collective-permute-start | bytes 393224 | tf_op jit(solution)/shard_map/ppermute | solution.py:499
  94.5 1.9 %collective-permute-start.18 = (f32[2,8,8,256]{3,2,1,0:T(8,128)S(1)}, f32[2,8,8,256]{3,2,1,0:T(8,128)S(1)}, u32[]{:S(2)}, u32[]{:S(2)}) collective-permute-start(f32[2,8,8,256]{3,2,1,0:T(8,128)S(1)} %collective-permute-done.15.refs_0_), channel_id=1, source_target_pairs={{0,4},{4,0},{8,12},{12,8},{16,20},{20,16},{24,28},{28,24},{1,5},{5... | collective-permute-start | bytes 393224 | tf_op jit(solution)/shard_map/ppermute | solution.py:499

commit v5 on v4

--- a/solution.py
+++ b/solution.py
@@ -249,6 +249,7 @@
     power,
     probe_out,
     table_out,
+    scale_out,
     window,
     terms,
     result,
@@ -264,6 +265,7 @@
     for mode in range(modes):
         total = total + probe_ref[mode, 0] * probe_ref[mode, 0] + probe_ref[mode, 1] * probe_ref[mode, 1]
     power[...] = total
+    scale_out[...] = jnp.full(scale_out.shape, 1.0 / jnp.max(total))
     probe_out[...] = probe_ref[...]
     table_out[...] = table_ref[...]
     move = order_ref[0]
@@ -298,15 +300,13 @@
     power,
     probe_ref,
     table_ref,
-    object_out,
-    top_out,
+    gradient,
     spill_out,
     mine_out,
     near_out,
     far_out,
     old_out,
     extended,
-    gradient,
     sums,
     window,
     terms,
@@ -320,14 +320,11 @@
     gradient[pl.ds(0, tile_rows), :] = gradient_ref[...]
     gradient[pl.ds(tile_rows, halo_rows), :] = jnp.zeros((halo_rows, LANES), jnp.float32)
     sums[...] = sums_ref[...]
-    scale = 1.0 / jnp.max(power[...])
     all_slots(
         False, tile_rows // SUBLANES, place_ref, count_ref, probe_ref, table_ref, extended,
         gradient, sums, power, measured, window, terms, result, back,
     )
-    object_out[...] = extended[pl.ds(0, tile_rows), :] - gradient[pl.ds(0, tile_rows), :] * scale
-    top_out[...] = object_out[pl.ds(0, halo_rows), :]
-    spill_out[...] = gradient[pl.ds(tile_rows, halo_rows), :] * scale
+    spill_out[...] = gradient[pl.ds(tile_rows, halo_rows), :]
     core, group, layer = here_ref[0, 0], here_ref[0, 1], here_ref[0, 2]
     groups, layers = mine_out.shape[0], mine_out.shape[1]
     for hop in range(groups):
@@ -362,7 +359,7 @@
     ]
     shape = jax.ShapeDtypeStruct
     cost = pl.CostEstimate(flops=2 * products, bytes_accessed=16 << 20, transcendentals=0)
-    begun = pl.pallas_call(
+    *begun, scale = pl.pallas_call(
         first_kernel,
         out_shape=(
             shape(tile.shape, f32),
@@ -372,19 +369,19 @@
             shape((side, side), f32),
             shape(probe.shape, f32),
             shape(table.shape, table.dtype),
+            shape((1, LANES), f32),
         ),
         in_specs=[smem, smem, pl.BlockSpec(memory_space=pl.ANY), vmem, vmem, vmem, vmem],
-        out_specs=(vmem,) * 7,
+        out_specs=(vmem,) * 8,
         scratch_shapes=work + [pltpu.SemaphoreType.DMA],
         compiler_params=pltpu.CompilerParams(vmem_limit_bytes=28 * 1024 * 1024),
         cost_estimate=cost,
         name="slots_inside",
     )(place, count, tile, probe, diffraction, table, order)
-    return pl.pallas_call(
+    gradient, *rest = pl.pallas_call(
         second_kernel,
         out_shape=(
-            shape(tile.shape, f32),
-            shape(halo.shape, f32),
+            shape((tile.shape[0] + halo.shape[0], LANES), f32),
             shape(halo.shape, f32),
             shape((groups, layers, *chunk), f32),
             shape((groups - 1, layers, *chunk), f32),
@@ -392,9 +389,8 @@
             shape((planes - 1, SUBLANES, side), f32),
         ),
         in_specs=[smem, smem, smem] + [vmem] * 8,
-        out_specs=(vmem,) * 7,
+        out_specs=(vmem,) * 6,
         scratch_shapes=[
-            pltpu.VMEM((tile.shape[0] + halo.shape[0], LANES), f32),
             pltpu.VMEM((tile.shape[0] + halo.shape[0], LANES), f32),
             pltpu.VMEM((chunks, *chunk), f32),
         ]
@@ -403,20 +399,54 @@
         cost_estimate=cost,
         name="slots_across",
     )(place, count, here, halo, *begun)
+    new_tile, top = written(begun[0], gradient, scale, halo.shape[0])
+    return new_tile, top, scale, *rest
+
+
+def write_kernel(tile_ref, gradient_ref, scale_ref, out_ref, top_ref, rows, semaphores):
+    scale = scale_ref[...]
+    step = out_ref.shape[0] // 4
+    copies = []
+    for part in range(4):
+        at = pl.ds(part * step, step)
+        rows[at, :] = tile_ref[at, :] - gradient_ref[at, :] * scale
+        copies.append(pltpu.make_async_copy(rows.at[at], out_ref.at[at], semaphores.at[part]))
+        copies[-1].start()
+    top_ref[...] = rows[pl.ds(0, top_ref.shape[0]), :]
+    for copy in copies:
+        copy.wait()
+
+
+def written(tile, gradient, scale, top_rows):
+    vmem, anywhere = pl.BlockSpec(memory_space=pltpu.VMEM), pl.BlockSpec(memory_space=pl.ANY)
+    return pl.pallas_call(
+        write_kernel,
+        out_shape=(
+            jax.ShapeDtypeStruct(tile.shape, jnp.float32),
+            jax.ShapeDtypeStruct((top_rows, LANES), jnp.float32),
+        ),
+        in_specs=[vmem, vmem, vmem],
+        out_specs=(anywhere, vmem),
+        scratch_shapes=[pltpu.VMEM(tile.shape, jnp.float32), pltpu.SemaphoreType.DMA((4,))],
+        compiler_params=pltpu.CompilerParams(vmem_limit_bytes=10 * 1024 * 1024),
+        cost_estimate=pl.CostEstimate(flops=0, bytes_accessed=4 << 20, transcendentals=0),
+        name="written",
+    )(tile, gradient, scale)
 
 
 def first_rows(tile, rows):
-    def kernel(tile_ref, out_ref):
-        out_ref[...] = tile_ref[...]
-
-    block = pl.BlockSpec((rows // 4, LANES), lambda i: (i, 0))
+    def kernel(tile_ref, out_ref, semaphore):
+        copy = pltpu.make_async_copy(tile_ref.at[pl.ds(0, rows)], out_ref, semaphore)
+        copy.start()
+        copy.wait()
+
     return pl.pallas_call(
         kernel,
-        grid=(4,),
         out_shape=jax.ShapeDtypeStruct((rows, LANES), jnp.float32),
-        in_specs=[block],
-        out_specs=block,
-        compiler_params=pltpu.CompilerParams(vmem_limit_bytes=62 * 1024 * 1024),
+        in_specs=[pl.BlockSpec(memory_space=pl.ANY)],
+        out_specs=pl.BlockSpec(memory_space=pltpu.VMEM),
+        scratch_shapes=[pltpu.SemaphoreType.DMA],
+        compiler_params=pltpu.CompilerParams(vmem_limit_bytes=4 * 1024 * 1024),
         name="first_rows",
     )(tile)
 
@@ -469,26 +499,26 @@
     )(here, *arrays, *rest)
 
 
-def top_kernel(held_ref, top_ref, arrived_ref, out_ref, rows, semaphore):
-    rows[...] = top_ref[...] - arrived_ref[...]
+def top_kernel(held_ref, top_ref, arrived_ref, scale_ref, out_ref, rows, semaphore):
+    rows[...] = top_ref[...] - arrived_ref[...] * scale_ref[...]
     copy = pltpu.make_async_copy(rows, out_ref.at[pl.ds(0, rows.shape[0])], semaphore)
     copy.start()
     copy.wait()
 
 
-def with_top(tile, top, arrived):
+def with_top(tile, top, arrived, scale):
     vmem, anywhere = pl.BlockSpec(memory_space=pltpu.VMEM), pl.BlockSpec(memory_space=pl.ANY)
     return pl.pallas_call(
         top_kernel,
         out_shape=jax.ShapeDtypeStruct(tile.shape, jnp.float32),
-        in_specs=[anywhere, vmem, vmem],
+        in_specs=[anywhere, vmem, vmem, vmem],
         out_specs=anywhere,
         scratch_shapes=[pltpu.VMEM(top.shape, jnp.float32), pltpu.SemaphoreType.DMA],
         input_output_aliases={0: 0},
         compiler_params=pltpu.CompilerParams(vmem_limit_bytes=8 * 1024 * 1024),
         cost_estimate=pl.CostEstimate(flops=0, bytes_accessed=2 << 20, transcendentals=0),
         name="with_top",
-    )(tile, top, arrived)
+    )(tile, top, arrived, scale)
 
 
 def across(block, hop):
@@ -504,34 +534,39 @@
     return lax.ppermute(block, "region", [(i, (i + 2 * step) % regions) for i in range(regions)])
 
 
-def probe_by_shards(probe, mine, near, far, old, here, layers, spill):
+def probe_by_shards(probe, mine, near, far, old, here, layers, spill, new_tile, top, scale):
     modes, parts, side, _ = probe.shape
     planes = modes * parts
     half = layers // 2
     near, other_far = lax.optimization_barrier((near, from_partner(far)))
-    other_near = from_partner(near)
+    other_near, spill = lax.optimization_barrier((from_partner(near), spill))
+    arrived = shifted(spill, "region", 1)
     far_sum = mine[3] + other_far
     by_x, by_y = across(far_sum[:half], 1), across(far_sum[half:], 2)
     near_sum = mine[:3] + other_near
     to_x = near_sum[1].at[half:].add(by_y)
     to_y = near_sum[2].at[:half].add(by_x)
-    by_x, by_y = across(to_x, 1), across(to_y, 2)
+    by_x, by_y, arrived, new_tile, top = lax.optimization_barrier(
+        (across(to_x, 1), across(to_y, 2), arrived, new_tile, top)
+    )
+    new_tile = with_top(new_tile, top, arrived, scale)
     summed = [near_sum[0, step] + by_x[step] + by_y[step] for step in range(layers)]
     fresh = divided(old, [summed[0]] + [up_layers(summed[step], step) for step in range(1, layers)])
-    own = jnp.stack([fresh] + [up_layers(fresh, step) for step in range(1, layers)])
-    own, spill = lax.optimization_barrier((own, spill))
+    *others, new_tile = lax.optimization_barrier(
+        (*[up_layers(fresh, step) for step in range(1, layers)], new_tile)
+    )
+    own = jnp.stack([fresh] + others)
     x, y = across(own, 1), across(own, 2)
-    arrived = shifted(spill, "region", 1)
     near = [own, x, y]
-    near = near + [from_partner(array) for array in near]
-    placed = put_in_place(
-        here, layers, tuple((flip, hop, 0) for flip in range(2) for hop in range(3)), near, planes, side
-    )
+    placed = put_in_place(here, layers, tuple((0, hop, 0) for hop in range(3)), near, planes, side)
     far = [across(x[:half], 2), across(y[half:], 1)]
+    *far, placed = lax.optimization_barrier((*far, placed))
+    near = [from_partner(array) for array in near]
+    placed = put_in_place(here, layers, tuple((1, hop, 0) for hop in range(3)), near, planes, side, placed)
     far = far + [from_partner(array) for array in far]
     pieces = tuple((flip, 3, start) for flip in range(2) for start in (0, half))
     placed = put_in_place(here, layers, pieces, far, planes, side, placed)
-    return placed.reshape(probe.shape), arrived
+    return placed.reshape(probe.shape), new_tile
 
 
 def probe_from_whole(probe, mine, near, far):
@@ -561,15 +596,16 @@
     else:
         here = jnp.zeros((1, 3), jnp.int32)
         groups, layers = 4, side // SUBLANES // 8
-    new_tile, top, spill, mine, near, far, old = gradient_step(
+    new_tile, top, scale, spill, mine, near, far, old = gradient_step(
         place, slot_counts, here, tile, halo, probe, diffraction, groups, layers
     )
     if sharded:
-        new_probe, arrived = probe_by_shards(probe, mine, near, far, old, here, layers, spill)
+        new_probe, new_tile = probe_by_shards(
+            probe, mine, near, far, old, here, layers, spill, new_tile, top, scale
+        )
     else:
-        arrived = shifted(spill, "region", 1)
+        new_tile = with_top(new_tile, top, shifted(spill, "region", 1), scale)
         new_probe = probe_from_whole(probe, mine, near, far)
-    new_tile = with_top(new_tile, top, arrived)
     return (unpacked(new_tile, object_slab.shape), new_probe)
 
 

time: 100 us -> 96.1 us (0.961); the launches traced: 99.1 us -> 94.2 us
  waiting for transfers between devices: 35.1 us -> 25 us
  starting transfers between devices: 21.9 us -> 27.8 us
  Pallas kernels: 35.5 us -> 33.5 us
  local copies, waits for them, and re-layouts: 4.6 us -> 5.81 us
    pallas_call x1, Pallas kernels: 19.2 us -> 9.09 us  [gradient_step(): pl.pallas_call(first_kernel, out_shape=(shape(tile.shape, f32), shape(til...]
    ppermute x8, waiting for transfers between devices: 23.3 us -> 14.7 us  [across(): lax.ppermute(block, 'group', [(i, i ^ hop) for i in range(lax.axis_size('...]
    pallas_call x2 -> x3, Pallas kernels: 11.9 us -> 18.8 us  [the longest x1 17.3 us: gradient_step(): pl.pallas_call(second_kernel, out_shape=(shape((tile.shape[0] + halo.shap...]
    ppermute x6, starting transfers between devices: 8.56 us -> 11.8 us  [up_layers(): lax.ppermute(block, 'region', [(i, (i + 2 * step) % regions) for i in ran...]
    unnamed x13 -> x15, local copies, waits for them, and re-layouts: 4.51 us -> 5.73 us
    pallas_call x2 -> x3, Pallas kernels: 3.28 us -> 4.43 us  [put_in_place(): pl.pallas_call(functools.partial(place_kernel, layers, pieces), out_shape...]
    ppermute x8, starting transfers between devices: 9.48 us -> 10.6 us  [across(): lax.ppermute(block, 'group', [(i, i ^ hop) for i in range(lax.axis_size('...]
    ppermute x6, waiting for transfers between devices: 10.1 us -> 9.08 us  [up_layers(): lax.ppermute(block, 'region', [(i, (i + 2 * step) % regions) for i in ran...]
  transfers between devices with their start and end apart: 23 -> 23, of which waited for: 14 -> 11; matrix products, arithmetic and copies ran while one was open for 0% -> 1% of each run, Pallas kernels for 23% -> 16%
where the time goes in v5:
time: 96.1 us; the launch traced here: 94.2 us
  Pallas kernels  33.5 us (35%)
  starting transfers between devices  27.8 us (29%)
  waiting for transfers between devices  25 us (26%)
  local copies, waits for them, and re-layouts  5.81 us (6%)
  between operations  1.68 us (2%)
    pallas_call x1, Pallas kernels, gradient_step(): pl.pallas_call(second_kernel, out_shape=(shape((tile.shape[0] + halo.shap...  17.3 us
    ppermute x8, waiting for transfers between devices, across(): lax.ppermute(block, 'group', [(i, i ^ hop) for i in range(lax.axis_size('...  14.7 us
    ppermute x6, starting transfers between devices, up_layers(): lax.ppermute(block, 'region', [(i, (i + 2 * step) % regions) for i in ran...  11.8 us
    ppermute x8, starting transfers between devices, across(): lax.ppermute(block, 'group', [(i, i ^ hop) for i in range(lax.axis_size('...  10.6 us
    pallas_call x1, Pallas kernels, gradient_step(): pl.pallas_call(first_kernel, out_shape=(shape(tile.shape, f32), shape(til...  9.09 us
    ppermute x6, waiting for transfers between devices, up_layers(): lax.ppermute(block, 'region', [(i, (i + 2 * step) % regions) for i in ran...  9.08 us
    unnamed x15, local copies, waits for them, and re-layouts  5.73 us
    pallas_call x3, Pallas kernels, put_in_place(): pl.pallas_call(functools.partial(place_kernel, layers, pieces), out_shape...  4.43 us
  transfers between devices with their start and end apart: 23, of which 11 were waited for; matrix products, arithmetic and copies ran while one was open for 1% of the time, Pallas kernels for 16%

profile of v5, /device:TPU:0, one launch (start us, length us, event | category | flops | bytes accessed | tf_op | source)
XLA Modules:
  0.0 94.2 jit_solution(11812026527921533764)
XLA Ops:
  0.6 1.6 %copy-done = f32[512,2,512]{2,1,0:T(2,128)S(1)} copy-done((f32[512,2,512]{2,1,0:T(2,128)S(1)}, f32[512,2,512]{2,1,0:T(2,128)}, u32[]{:S(2)}) %copy-start) | copy-done | bytes 2097176
  2.2 0.1 first_rows.1
  2.3 1.4 %collective-permute-start = (f32[2048,128]{1,0:T(8,128)S(1)}, f32[2048,128]{1,0:T(8,128)}, u32[]{:S(2)}, u32[]{:S(2)}) collective-permute-start(f32[2048,128]{1,0:T(8,128)S(1)} %first_rows.1), channel_id=1, source_target_pairs={{4,0},{8,4},{12,8},{16,12},{20,16},{24,20},{28,24},{5,1},{9,5},{13... | collective-permute-start | bytes 3145736 | tf_op jit(solution)/shard_map/ppermute | solution.py:21
  4.4 0.1 copy.12
  4.5 0.1 pad_add_fusion
  4.6 0.1 add_bitcast_fusion.here_ref
  4.7 0.0 copy-done.1
  4.7 1.6 %copy-done.2 = f32[4,2,256,256]{3,2,1,0:T(8,128)S(1)} copy-done((f32[4,2,256,256]{3,2,1,0:T(8,128)S(1)}, f32[4,2,256,256]{3,2,1,0:T(8,128)}, u32[]{:S(2)}) %copy-start.2) | copy-done | bytes 2097176
  6.3 1.2 %copy-done.3 = f32[4,256,256]{2,1,0:T(8,128)S(1)} copy-done((f32[4,256,256]{2,1,0:T(8,128)S(1)}, f32[4,256,256]{2,1,0:T(8,128)}, u32[]{:S(2)}) %copy-start.3) | copy-done | bytes 1048600
  7.5 1.2 %copy-done.4 = bf16[2,4,256,256]{3,2,1,0:T(8,128)(2,1)S(1)} copy-done((bf16[2,4,256,256]{3,2,1,0:T(8,128)(2,1)S(1)}, bf16[2,4,256,256]{3,2,1,0:T(8,128)(2,1)}, u32[]{:S(2)}) %copy-start.4) | copy-done | bytes 1048600
  8.7 9.1 %slots_inside.1 = (f32[4096,128]{1,0:T(8,128)S(1)}, f32[4096,128]{1,0:T(8,128)S(1)}, f32[32,9,8,256]{3,2,1,0:T(8,128)S(1)}, f32[4,256,256]{2,1,0:T(8,128)S(1)}, ...) custom-call(s32[4,2]{1,0:T(4,128)S(1)} %broadcast_subtract_fusion.pl, ...), custom_call_target="tpu_custom_call" | custom-call | flops 12884901888 | bytes 16777216 | tf_op jit(solution)/shard_map/slots_inside/pallas_call | solution.py:362
  17.8 0.0 collective-permute-done.halo_ref
  17.8 17.3 %slots_across.1 = (f32[6144,128]{1,0:T(8,128)S(1)}, f32[2048,128]{1,0:T(8,128)S(1)}, f32[4,4,9,8,256]{4,3,2,1,0:T(8,128)S(1)}, f32[3,4,9,8,256]{4,3,2,1,0:T(8,12...) custom-call(s32[4,2]{1,0:T(4,128)S(1)} %broadcast_subtract_fusion.place_ref, s32[1,1]{1,0:T(1,128)S(6)} %copy.20.count_ref, ...), custom_call_target="tpu_custom_call" | custom-call | flops 12884901888 | bytes 16777216 | tf_op jit(solution)/shard_map/slots_across/pallas_call | solution.py:381
  35.2 0.6 collective-permute-start.1
  35.8 1.2 %collective-permute-done.1 = f32[4,9,8,256]{3,2,1,0:T(8,128)S(1)} collective-permute-done((f32[4,9,8,256]{3,2,1,0:T(8,128)S(1)}, f32[4,9,8,256]{3,2,1,0:T(8,128)S(1)}, u32[]{:S(2)}, u32[]{:S(2)}) %collective-permute-start.1) | collective-permute-done | bytes 294944 | tf_op jit(solution)/shard_map/ppermute | solution.py:529
  37.0 0.4 collective-permute-start.2
  37.5 0.1 collective-permute-start.5
  37.5 3.9 %collective-permute-start.3 = (f32[2,9,8,256]{3,2,1,0:T(8,128)S(1)}, f32[2,9,8,256]{3,2,1,0:T(8,128)S(1)}, u32[]{:S(2)}, u32[]{:S(2)}) collective-permute-start(f32[2,9,8,256]{3,2,1,0:T(8,128)S(1)} %get-tuple-element.99), channel_id=1, source_target_pairs={{0,2},{1,3},{2,0},{3,1},{4,6},{5,7},{6,4},{7,5},{8,10},{9,11},{10,... | collective-permute-start | bytes 442376 | tf_op jit(solution)/shard_map/ppermute | solution.py:525
  41.4 0.0 collective-permute-done.2
  41.4 1.9 %collective-permute-start.7 = (f32[2048,128]{1,0:T(8,128)S(1)}, f32[2048,128]{1,0:T(8,128)S(1)}, u32[]{:S(2)}, u32[]{:S(2)}) collective-permute-start(f32[2048,128]{1,0:T(8,128)S(1)} %get-tuple-element.73), channel_id=1, source_target_pairs={{0,4},{4,8},{8,12},{12,16},{16,20},{20,24},{24,28},{1,5},{5,9},{9,... | collective-permute-start | bytes 3145736 | tf_op jit(solution)/shard_map/ppermute | solution.py:21
  43.3 0.1 slice_add_fusion
  43.5 0.0 collective-permute-done.5
  43.5 2.0 %collective-permute-done.3 = f32[2,9,8,256]{3,2,1,0:T(8,128)S(1)} collective-permute-done((f32[2,9,8,256]{3,2,1,0:T(8,128)S(1)}, f32[2,9,8,256]{3,2,1,0:T(8,128)S(1)}, u32[]{:S(2)}, u32[]{:S(2)}) %collective-permute-start.3) | collective-permute-done | bytes 147488 | tf_op jit(solution)/shard_map/ppermute | solution.py:525
  45.5 1.8 %collective-permute-start.6 = (f32[4,9,8,256]{3,2,1,0:T(8,128)S(1)}, f32[4,9,8,256]{3,2,1,0:T(8,128)S(1)}, u32[]{:S(2)}, u32[]{:S(2)}) collective-permute-start(f32[4,9,8,256]{3,2,1,0:T(8,128)S(1)} %get-tuple-element.94), channel_id=1, source_target_pairs={{0,2},{1,3},{2,0},{3,1},{4,6},{5,7},{6,4},{7,5},{8,10},{9,11},{10,... | collective-permute-start | bytes 884744 | tf_op jit(solution)/shard_map/ppermute | solution.py:525
  47.3 0.4 collective-permute-start.4
  47.7 1.4 %written.1 = (f32[4096,128]{1,0:T(8,128)}, f32[2048,128]{1,0:T(8,128)S(1)}) custom-call(f32[4096,128]{1,0:T(8,128)S(1)} %get-tuple-element.58.tile_ref, f32[6144,128]{1,0:T(8,128)S(1)} %get-tuple-element.74.gradient_ref, f32[1,128]{1,0:T(1,128)S(1)} %get-tuple-element.75.scale_ref), custom_call_target="tpu_custom_call" | custom-call | bytes 4194304 | tf_op jit(solution)/shard_map/written/pallas_call | solution.py:422
  49.1 5.0 %collective-permute-done.6 = f32[4,9,8,256]{3,2,1,0:T(8,128)S(1)} collective-permute-done((f32[4,9,8,256]{3,2,1,0:T(8,128)S(1)}, f32[4,9,8,256]{3,2,1,0:T(8,128)S(1)}, u32[]{:S(2)}, u32[]{:S(2)}) %collective-permute-start.6) | collective-permute-done | bytes 294944 | tf_op jit(solution)/shard_map/ppermute | solution.py:525
  54.1 1.5 %collective-permute-done.4 = f32[4,9,8,256]{3,2,1,0:T(8,128)S(1)} collective-permute-done((f32[4,9,8,256]{3,2,1,0:T(8,128)S(1)}, f32[4,9,8,256]{3,2,1,0:T(8,128)S(1)}, u32[]{:S(2)}, u32[]{:S(2)}) %collective-permute-start.4) | collective-permute-done | bytes 294944 | tf_op jit(solution)/shard_map/ppermute | solution.py:525
  55.6 0.0 collective-permute-done.7.arrived_ref
  55.6 0.1 fusion.5
  55.6 7.9 %collective-permute-start.10 = (f32[9,8,256]{2,1,0:T(8,128)S(1)}, f32[9,8,256]{2,1,0:T(8,128)S(1)}, u32[]{:S(2)}, u32[]{:S(2)}) collective-permute-start(f32[9,8,256]{2,1,0:T(8,128)S(1)} %get-tuple-element.90), channel_id=1, source_target_pairs={{0,24},{4,28},{8,0},{12,4},{16,8},{20,12},{24,16},{28,20},{1,25},{... | collective-permute-start | bytes 221192 | tf_op jit(solution)/shard_map/ppermute | solution.py:534
  63.6 0.0 collective-permute-start.9
  63.6 0.6 collective-permute-start.8
  64.2 1.3 %collective-permute-done.10.refs_3_ = f32[9,8,256]{2,1,0:T(8,128)S(1)} collective-permute-done((f32[9,8,256]{2,1,0:T(8,128)S(1)}, f32[9,8,256]{2,1,0:T(8,128)S(1)}, u32[]{:S(2)}, u32[]{:S(2)}) %collective-permute-start.10) | collective-permute-done | bytes 73760 | tf_op jit(solution)/shard_map/ppermute | solution.py:534
  65.5 3.3 %collective-permute-done.9.refs_2_ = f32[9,8,256]{2,1,0:T(8,128)S(1)} collective-permute-done((f32[9,8,256]{2,1,0:T(8,128)S(1)}, f32[9,8,256]{2,1,0:T(8,128)S(1)}, u32[]{:S(2)}, u32[]{:S(2)}) %collective-permute-start.9) | collective-permute-done | bytes 73760 | tf_op jit(solution)/shard_map/ppermute | solution.py:534
  68.8 0.9 collective-permute-done.8.refs_1_
  69.7 1.3 %collective-permute-start.13 = (f32[8,8,256]{2,1,0:T(8,128)S(1)}, f32[8,8,256]{2,1,0:T(8,128)S(1)}, u32[]{:S(2)}, u32[]{:S(2)}) collective-permute-start(f32[8,8,256]{2,1,0:T(8,128)S(1)} %divided.1), channel_id=1, source_target_pairs={{0,24},{4,28},{8,0},{12,4},{16,8},{20,12},{24,16},{28,20},{1,25},{... | collective-permute-start | bytes 196616 | tf_op jit(solution)/shard_map/ppermute | solution.py:534
  71.1 0.0 collective-permute-start.12
  71.1 1.9 %collective-permute-start.11 = (f32[8,8,256]{2,1,0:T(8,128)S(1)}, f32[8,8,256]{2,1,0:T(8,128)S(1)}, u32[]{:S(2)}, u32[]{:S(2)}) collective-permute-start(f32[8,8,256]{2,1,0:T(8,128)S(1)} %divided.1), channel_id=1, source_target_pairs={{0,8},{4,12},{8,16},{12,20},{16,24},{20,28},{24,0},{28,4},{1,9},{5... | collective-permute-start | bytes 196616 | tf_op jit(solution)/shard_map/ppermute | solution.py:534
  73.0 1.1 %with_top.1 = f32[4096,128]{1,0:T(8,128)} custom-call(f32[4096,128]{1,0:T(8,128)} %get-tuple-element.80.held_ref, f32[2048,128]{1,0:T(8,128)S(1)} %get-tuple-element.81.top_ref, f32[2048,128]{1,0:T(8,128)S(1)} %collective-permute-done.7.arrived_ref, f32[1,128]{1,0:T(1,128)S(1)} %get-tuple-element.75.scale_ref), custom_call_target="tpu_custom_call", output_to_operand_aliasing={{}: (0, {})} | custom-call | bytes 2097152 | tf_op jit(solution)/shard_map/with_top/pallas_call | solution.py:511
  74.1 0.0 collective-permute-done.13
  74.1 3.5 %collective-permute-done.12 = f32[8,8,256]{2,1,0:T(8,128)S(1)} collective-permute-done((f32[8,8,256]{2,1,0:T(8,128)S(1)}, f32[8,8,256]{2,1,0:T(8,128)S(1)}, u32[]{:S(2)}, u32[]{:S(2)}) %collective-permute-start.12) | collective-permute-done | bytes 65568 | tf_op jit(solution)/shard_map/ppermute | solution.py:534
  77.6 0.0 collective-permute-done.11
  77.6 0.1 collective-permute-start.16
  77.7 1.9 %collective-permute-start.14 = (f32[4,8,8,256]{3,2,1,0:T(8,128)S(1)}, f32[4,8,8,256]{3,2,1,0:T(8,128)S(1)}, u32[]{:S(2)}, u32[]{:S(2)}) collective-permute-start(f32[4,8,8,256]{3,2,1,0:T(8,128)S(1)} %pad_maximum_fusion.refs_0_), channel_id=1, source_target_pairs={{0,1},{1,0},{2,3},{3,2},{4,5},{5,4},{6,7},{7,6},{8,9},{9,8},{10,11... | collective-permute-start | bytes 786440 | tf_op jit(solution)/shard_map/ppermute | solution.py:525
  79.6 0.0 collective-permute-start.20
  79.6 5.0 %collective-permute-done.16.refs_2_ = f32[4,8,8,256]{3,2,1,0:T(8,128)S(1)} collective-permute-done((f32[4,8,8,256]{3,2,1,0:T(8,128)S(1)}, f32[4,8,8,256]{3,2,1,0:T(8,128)S(1)}, u32[]{:S(2)}, u32[]{:S(2)}) %collective-permute-start.16) | collective-permute-done | bytes 262176 | tf_op jit(solution)/shard_map/ppermute | solution.py:525
  84.6 0.1 collective-permute-start.17
  84.7 0.4 collective-permute-done.14.refs_1_
  85.1 2.5 %collective-permute-start.15 = (f32[2,8,8,256]{3,2,1,0:T(8,128)S(1)}, f32[2,8,8,256]{3,2,1,0:T(8,128)S(1)}, u32[]{:S(2)}, u32[]{:S(2)}) collective-permute-start(f32[2,8,8,256]{3,2,1,0:T(8,128)S(1)} %slice.152), channel_id=1, source_target_pairs={{0,2},{1,3},{2,0},{3,1},{4,6},{5,7},{6,4},{7,5},{8,10},{9,11},{10,... | collective-permute-start | bytes 393224 | tf_op jit(solution)/shard_map/ppermute | solution.py:525
  87.6 0.0 collective-permute-start.22
  87.6 0.5 collective-permute-start.21
  88.1 1.5 %put_in_place.3.refs_3_ = f32[8,32,8,256]{3,2,1,0:T(8,128)} custom-call(s32[1,3]{1,0:T(1,128)S(1)} %add_bitcast_fusion.here_ref, f32[4,8,8,256]{3,2,1,0:T(8,128)S(1)} %pad_maximum_fusion.refs_0_, f32[4,8,8,256]{3,2,1,0:T(8,128)S(1)} %collective-permute-done.14.refs_1_, f32[4,8,8,256]{3,2,1,0:T(8,128)S(1)} %collective-permute-done.16.refs_2_), custom_call_target="tpu_custom_call" | custom-call | bytes 4194304 | tf_op jit(solution)/shard_map/put_in_place/pallas_call | solution.py:489
  89.6 0.0 collective-permute-done.17.refs_1_
  89.7 0.9 collective-permute-done.15.refs_0_
  90.5 0.0 collective-permute-start.18
  90.5 0.5 collective-permute-start.19
  91.1 0.0 collective-permute-done.20.refs_0_
  91.1 0.0 collective-permute-done.22.refs_2_
  91.1 0.0 collective-permute-done.21.refs_1_
  91.1 1.5 %put_in_place.4.refs_4_ = f32[8,32,8,256]{3,2,1,0:T(8,128)} custom-call(s32[1,3]{1,0:T(1,128)S(1)} %add_bitcast_fusion.here_ref, f32[4,8,8,256]{3,2,1,0:T(8,128)S(1)} %collective-permute-done.20.refs_0_, f32[4,8,8,256]{3,2,1,0:T(8,128)S(1)} %collective-permute-done.21.refs_1_, ...), custom_call_target="tpu_custom_call", output_to_operand_aliasing={{}: (4, {})} | custom-call | bytes 4194304 | tf_op jit(solution)/shard_map/put_in_place/pallas_call | solution.py:489
  92.6 0.0 collective-permute-done.18.refs_2_
  92.6 0.0 collective-permute-done.19.refs_3_
  92.6 1.4 %put_in_place.5 = f32[8,32,8,256]{3,2,1,0:T(8,128)} custom-call(s32[1,3]{1,0:T(1,128)S(1)} %add_bitcast_fusion.here_ref, f32[2,8,8,256]{3,2,1,0:T(8,128)S(1)} %collective-permute-done.15.refs_0_, f32[2,8,8,256]{3,2,1,0:T(8,128)S(1)} %collective-permute-done.17.refs_1_, ...), custom_call_target="tpu_custom_call", output_to_operand_aliasing={{}: (5, {})} | custom-call | bytes 4194304 | tf_op jit(solution)/shard_map/put_in_place/pallas_call | solution.py:489
  (18 shorter events, 0.2 us)
Async XLA Ops:
  0.6 3.8 %copy-start.6 = (s32[4,2]{0,1:T(2,128)S(1)}, s32[4,2]{0,1:T(2,128)}, u32[]{:S(2)}) copy-start(s32[4,2]{0,1:T(2,128)} %param.14) | copy-start | bytes 100
  0.6 1.6 %copy-start = (f32[512,2,512]{2,1,0:T(2,128)S(1)}, f32[512,2,512]{2,1,0:T(2,128)}, u32[]{:S(2)}) copy-start(f32[512,2,512]{2,1,0:T(2,128)} %param.11) | copy-start | bytes 6291460
  2.2 2.5 %copy-start.1 = (f32[512,2,512]{2,1,0:T(2,128)S(1)}, f32[512,2,512]{2,1,0:T(2,128)}, u32[]{:S(2)}) copy-start(f32[512,2,512]{2,1,0:T(2,128)} %param.11) | copy-start | bytes 6291460
  2.2 2.5 %copy-start.5 = (bf16[2,256,256]{2,1,0:T(8,128)(2,1)S(1)}, bf16[2,256,256]{2,1,0:T(8,128)(2,1)}, u32[]{:S(2)}) copy-start(bf16[2,256,256]{2,1,0:T(8,128)(2,1)} %constant.96.clone.order_ref) | copy-start | bytes 786436
  2.3 15.5 %collective-permute-start = (f32[2048,128]{1,0:T(8,128)S(1)}, f32[2048,128]{1,0:T(8,128)}, u32[]{:S(2)}, u32[]{:S(2)}) collective-permute-start(f32[2048,128]{1,0:T(8,128)S(1)} %first_rows.1), channel_id=1, source_target_pairs={{4,0},{8,4},{12,8},{16,12},{20,16},{24,20},{28,24},{5,1},{9,5},{13... | collective-permute-start | bytes 3145736 | tf_op jit(solution)/shard_map/ppermute | solution.py:21
  4.7 1.6 %copy-start.2 = (f32[4,2,256,256]{3,2,1,0:T(8,128)S(1)}, f32[4,2,256,256]{3,2,1,0:T(8,128)}, u32[]{:S(2)}) copy-start(f32[4,2,256,256]{3,2,1,0:T(8,128)} %probe_ref.1) | copy-start | bytes 6291460
  6.3 1.2 %copy-start.3 = (f32[4,256,256]{2,1,0:T(8,128)S(1)}, f32[4,256,256]{2,1,0:T(8,128)}, u32[]{:S(2)}) copy-start(f32[4,256,256]{2,1,0:T(8,128)} %diffraction_ref.1) | copy-start | bytes 3145732
  7.5 1.2 %copy-start.4 = (bf16[2,4,256,256]{3,2,1,0:T(8,128)(2,1)S(1)}, bf16[2,4,256,256]{3,2,1,0:T(8,128)(2,1)}, u32[]{:S(2)}) copy-start(bf16[2,4,256,256]{3,2,1,0:T(8,128)(2,1)} %constant.95.clone.table_ref) | copy-start | bytes 3145732
  35.2 1.8 %collective-permute-start.1 = (f32[4,9,8,256]{3,2,1,0:T(8,128)S(1)}, f32[4,9,8,256]{3,2,1,0:T(8,128)S(1)}, u32[]{:S(2)}, u32[]{:S(2)}) collective-permute-start(f32[4,9,8,256]{3,2,1,0:T(8,128)S(1)} %get-tuple-element.68), channel_id=1, source_target_pairs={{0,4},{4,0},{8,12},{12,8},{16,20},{20,16},{24,28},{28,24},{1,5},{5... | collective-permute-start | bytes 884744 | tf_op jit(solution)/shard_map/ppermute | solution.py:529
  37.0 4.4 %collective-permute-start.2 = (f32[3,4,9,8,256]{4,3,2,1,0:T(8,128)S(1)}, f32[3,4,9,8,256]{4,3,2,1,0:T(8,128)S(1)}, u32[]{:S(2)}, u32[]{:S(2)}) collective-permute-start(f32[3,4,9,8,256]{4,3,2,1,0:T(8,128)S(1)} %get-tuple-element.69), channel_id=1, source_target_pairs={{0,4},{4,0},{8,12},{12,8},{16,20},{20,16},{24,28},{28,24},{1,5},{5... | collective-permute-start | bytes 2654216 | tf_op jit(solution)/shard_map/ppermute | solution.py:529
  37.5 6.1 %collective-permute-start.5 = (f32[2,9,8,256]{3,2,1,0:T(8,128)S(1)}, f32[2,9,8,256]{3,2,1,0:T(8,128)S(1)}, u32[]{:S(2)}, u32[]{:S(2)}) collective-permute-start(f32[2,9,8,256]{3,2,1,0:T(8,128)S(1)} %get-tuple-element.98), channel_id=1, source_target_pairs={{0,1},{1,0},{2,3},{3,2},{4,5},{5,4},{6,7},{7,6},{8,9},{9,8},{10,11... | collective-permute-start | bytes 442376 | tf_op jit(solution)/shard_map/ppermute | solution.py:525
  37.5 7.9 %collective-permute-start.3 = (f32[2,9,8,256]{3,2,1,0:T(8,128)S(1)}, f32[2,9,8,256]{3,2,1,0:T(8,128)S(1)}, u32[]{:S(2)}, u32[]{:S(2)}) collective-permute-start(f32[2,9,8,256]{3,2,1,0:T(8,128)S(1)} %get-tuple-element.99), channel_id=1, source_target_pairs={{0,2},{1,3},{2,0},{3,1},{4,6},{5,7},{6,4},{7,5},{8,10},{9,11},{10,... | collective-permute-start | bytes 442376 | tf_op jit(solution)/shard_map/ppermute | solution.py:525
  41.4 14.2 %collective-permute-start.7 = (f32[2048,128]{1,0:T(8,128)S(1)}, f32[2048,128]{1,0:T(8,128)S(1)}, u32[]{:S(2)}, u32[]{:S(2)}) collective-permute-start(f32[2048,128]{1,0:T(8,128)S(1)} %get-tuple-element.73), channel_id=1, source_target_pairs={{0,4},{4,8},{8,12},{12,16},{16,20},{20,24},{24,28},{1,5},{5,9},{9,... | collective-permute-start | bytes 3145736 | tf_op jit(solution)/shard_map/ppermute | solution.py:21
  45.5 8.6 %collective-permute-start.6 = (f32[4,9,8,256]{3,2,1,0:T(8,128)S(1)}, f32[4,9,8,256]{3,2,1,0:T(8,128)S(1)}, u32[]{:S(2)}, u32[]{:S(2)}) collective-permute-start(f32[4,9,8,256]{3,2,1,0:T(8,128)S(1)} %get-tuple-element.94), channel_id=1, source_target_pairs={{0,2},{1,3},{2,0},{3,1},{4,6},{5,7},{6,4},{7,5},{8,10},{9,11},{10,... | collective-permute-start | bytes 884744 | tf_op jit(solution)/shard_map/ppermute | solution.py:525
  47.3 8.2 %collective-permute-start.4 = (f32[4,9,8,256]{3,2,1,0:T(8,128)S(1)}, f32[4,9,8,256]{3,2,1,0:T(8,128)S(1)}, u32[]{:S(2)}, u32[]{:S(2)}) collective-permute-start(f32[4,9,8,256]{3,2,1,0:T(8,128)S(1)} %get-tuple-element.95), channel_id=1, source_target_pairs={{0,1},{1,0},{2,3},{3,2},{4,5},{5,4},{6,7},{7,6},{8,9},{9,8},{10,11... | collective-permute-start | bytes 884744 | tf_op jit(solution)/shard_map/ppermute | solution.py:525
  55.6 9.9 %collective-permute-start.10 = (f32[9,8,256]{2,1,0:T(8,128)S(1)}, f32[9,8,256]{2,1,0:T(8,128)S(1)}, u32[]{:S(2)}, u32[]{:S(2)}) collective-permute-start(f32[9,8,256]{2,1,0:T(8,128)S(1)} %get-tuple-element.90), channel_id=1, source_target_pairs={{0,24},{4,28},{8,0},{12,4},{16,8},{20,12},{24,16},{28,20},{1,25},{... | collective-permute-start | bytes 221192 | tf_op jit(solution)/shard_map/ppermute | solution.py:534
  63.6 5.3 %collective-permute-start.9 = (f32[9,8,256]{2,1,0:T(8,128)S(1)}, f32[9,8,256]{2,1,0:T(8,128)S(1)}, u32[]{:S(2)}, u32[]{:S(2)}) collective-permute-start(f32[9,8,256]{2,1,0:T(8,128)S(1)} %get-tuple-element.91), channel_id=1, source_target_pairs={{0,16},{4,20},{8,24},{12,28},{16,0},{20,4},{24,8},{28,12},{1,17},{... | collective-permute-start | bytes 221192 | tf_op jit(solution)/shard_map/ppermute | solution.py:534
  63.6 6.2 %collective-permute-start.8 = (f32[9,8,256]{2,1,0:T(8,128)S(1)}, f32[9,8,256]{2,1,0:T(8,128)S(1)}, u32[]{:S(2)}, u32[]{:S(2)}) collective-permute-start(f32[9,8,256]{2,1,0:T(8,128)S(1)} %get-tuple-element.92), channel_id=1, source_target_pairs={{0,8},{4,12},{8,16},{12,20},{16,24},{20,28},{24,0},{28,4},{1,9},{5... | collective-permute-start | bytes 221192 | tf_op jit(solution)/shard_map/ppermute | solution.py:534
  69.7 4.3 %collective-permute-start.13 = (f32[8,8,256]{2,1,0:T(8,128)S(1)}, f32[8,8,256]{2,1,0:T(8,128)S(1)}, u32[]{:S(2)}, u32[]{:S(2)}) collective-permute-start(f32[8,8,256]{2,1,0:T(8,128)S(1)} %divided.1), channel_id=1, source_target_pairs={{0,24},{4,28},{8,0},{12,4},{16,8},{20,12},{24,16},{28,20},{1,25},{... | collective-permute-start | bytes 196616 | tf_op jit(solution)/shard_map/ppermute | solution.py:534
  71.1 6.6 %collective-permute-start.12 = (f32[8,8,256]{2,1,0:T(8,128)S(1)}, f32[8,8,256]{2,1,0:T(8,128)S(1)}, u32[]{:S(2)}, u32[]{:S(2)}) collective-permute-start(f32[8,8,256]{2,1,0:T(8,128)S(1)} %divided.1), channel_id=1, source_target_pairs={{0,16},{4,20},{8,24},{12,28},{16,0},{20,4},{24,8},{28,12},{1,17},{... | collective-permute-start | bytes 196616 | tf_op jit(solution)/shard_map/ppermute | solution.py:534
  71.1 6.5 %collective-permute-start.11 = (f32[8,8,256]{2,1,0:T(8,128)S(1)}, f32[8,8,256]{2,1,0:T(8,128)S(1)}, u32[]{:S(2)}, u32[]{:S(2)}) collective-permute-start(f32[8,8,256]{2,1,0:T(8,128)S(1)} %divided.1), channel_id=1, source_target_pairs={{0,8},{4,12},{8,16},{12,20},{16,24},{20,28},{24,0},{28,4},{1,9},{5... | collective-permute-start | bytes 196616 | tf_op jit(solution)/shard_map/ppermute | solution.py:534
  77.6 7.0 %collective-permute-start.16 = (f32[4,8,8,256]{3,2,1,0:T(8,128)S(1)}, f32[4,8,8,256]{3,2,1,0:T(8,128)S(1)}, u32[]{:S(2)}, u32[]{:S(2)}) collective-permute-start(f32[4,8,8,256]{3,2,1,0:T(8,128)S(1)} %pad_maximum_fusion.refs_0_), channel_id=1, source_target_pairs={{0,2},{1,3},{2,0},{3,1},{4,6},{5,7},{6,4},{7,5},{8,10},{9,11},{10,... | collective-permute-start | bytes 786440 | tf_op jit(solution)/shard_map/ppermute | solution.py:525
  77.7 7.4 %collective-permute-start.14 = (f32[4,8,8,256]{3,2,1,0:T(8,128)S(1)}, f32[4,8,8,256]{3,2,1,0:T(8,128)S(1)}, u32[]{:S(2)}, u32[]{:S(2)}) collective-permute-start(f32[4,8,8,256]{3,2,1,0:T(8,128)S(1)} %pad_maximum_fusion.refs_0_), channel_id=1, source_target_pairs={{0,1},{1,0},{2,3},{3,2},{4,5},{5,4},{6,7},{7,6},{8,9},{9,8},{10,11... | collective-permute-start | bytes 786440 | tf_op jit(solution)/shard_map/ppermute | solution.py:525
  79.6 11.4 %collective-permute-start.20 = (f32[4,8,8,256]{3,2,1,0:T(8,128)S(1)}, f32[4,8,8,256]{3,2,1,0:T(8,128)S(1)}, u32[]{:S(2)}, u32[]{:S(2)}) collective-permute-start(f32[4,8,8,256]{3,2,1,0:T(8,128)S(1)} %pad_maximum_fusion.refs_0_), channel_id=1, source_target_pairs={{0,4},{4,0},{8,12},{12,8},{16,20},{20,16},{24,28},{28,24},{1,5},{5... | collective-permute-start | bytes 786440 | tf_op jit(solution)/shard_map/ppermute | solution.py:529
  84.6 5.0 %collective-permute-start.17 = (f32[2,8,8,256]{3,2,1,0:T(8,128)S(1)}, f32[2,8,8,256]{3,2,1,0:T(8,128)S(1)}, u32[]{:S(2)}, u32[]{:S(2)}) collective-permute-start(f32[2,8,8,256]{3,2,1,0:T(8,128)S(1)} %slice.153), channel_id=1, source_target_pairs={{0,1},{1,0},{2,3},{3,2},{4,5},{5,4},{6,7},{7,6},{8,9},{9,8},{10,11... | collective-permute-start | bytes 393224 | tf_op jit(solution)/shard_map/ppermute | solution.py:525
  85.1 5.4 %collective-permute-start.15 = (f32[2,8,8,256]{3,2,1,0:T(8,128)S(1)}, f32[2,8,8,256]{3,2,1,0:T(8,128)S(1)}, u32[]{:S(2)}, u32[]{:S(2)}) collective-permute-start(f32[2,8,8,256]{3,2,1,0:T(8,128)S(1)} %slice.152), channel_id=1, source_target_pairs={{0,2},{1,3},{2,0},{3,1},{4,6},{5,7},{6,4},{7,5},{8,10},{9,11},{10,... | collective-permute-start | bytes 393224 | tf_op jit(solution)/shard_map/ppermute | solution.py:525
  87.6 3.5 %collective-permute-start.22 = (f32[4,8,8,256]{3,2,1,0:T(8,128)S(1)}, f32[4,8,8,256]{3,2,1,0:T(8,128)S(1)}, u32[]{:S(2)}, u32[]{:S(2)}) collective-permute-start(f32[4,8,8,256]{3,2,1,0:T(8,128)S(1)} %collective-permute-done.16.refs_2_), channel_id=1, source_target_pairs={{0,4},{4,0},{8,12},{12,8},{16,20},{20,16},{24,28},{28,24},{1,5},{5... | collective-permute-start | bytes 786440 | tf_op jit(solution)/shard_map/ppermute | solution.py:529
  87.6 3.5 %collective-permute-start.21 = (f32[4,8,8,256]{3,2,1,0:T(8,128)S(1)}, f32[4,8,8,256]{3,2,1,0:T(8,128)S(1)}, u32[]{:S(2)}, u32[]{:S(2)}) collective-permute-start(f32[4,8,8,256]{3,2,1,0:T(8,128)S(1)} %collective-permute-done.14.refs_1_), channel_id=1, source_target_pairs={{0,4},{4,0},{8,12},{12,8},{16,20},{20,16},{24,28},{28,24},{1,5},{5... | collective-permute-start | bytes 786440 | tf_op jit(solution)/shard_map/ppermute | solution.py:529
  90.5 2.1 %collective-permute-start.18 = (f32[2,8,8,256]{3,2,1,0:T(8,128)S(1)}, f32[2,8,8,256]{3,2,1,0:T(8,128)S(1)}, u32[]{:S(2)}, u32[]{:S(2)}) collective-permute-start(f32[2,8,8,256]{3,2,1,0:T(8,128)S(1)} %collective-permute-done.15.refs_0_), channel_id=1, source_target_pairs={{0,4},{4,0},{8,12},{12,8},{16,20},{20,16},{24,28},{28,24},{1,5},{5... | collective-permute-start | bytes 393224 | tf_op jit(solution)/shard_map/ppermute | solution.py:529
  90.5 2.1 %collective-permute-start.19 = (f32[2,8,8,256]{3,2,1,0:T(8,128)S(1)}, f32[2,8,8,256]{3,2,1,0:T(8,128)S(1)}, u32[]{:S(2)}, u32[]{:S(2)}) collective-permute-start(f32[2,8,8,256]{3,2,1,0:T(8,128)S(1)} %collective-permute-done.17.refs_1_), channel_id=1, source_target_pairs={{0,4},{4,0},{8,12},{12,8},{16,20},{20,16},{24,28},{28,24},{1,5},{5... | collective-permute-start | bytes 393224 | tf_op jit(solution)/shard_map/ppermute | solution.py:529
